TPU v7x, 32 devices: a whole 2x2x4 slice. The times are simulated.
32 devices in a mesh: dom: 8 (over z, x), feat: 4 (over y, core).
Axes of the slice: x: 2, y: 2, z: 4, core: 2. Of those that a mesh axis runs over, the one named last changes fastest.
Arguments:
- inputs_t: bfloat16 [128, 32768], P('feat', 'dom'), may hold values from -6 to 6
- tiles_first: bfloat16 [512, 128, 128], P('dom'), may hold values from 9e-05 to 1, as said below
- first_dst: int32 [512], P('dom'), may hold values from 0 to 15, as said below
- first_src: int32 [512], P('dom'), may hold values from 0 to 31
- w1_self: bfloat16 [128, 256], P('feat'), may hold values from -0.5 to 0.5
- w1_neigh: bfloat16 [128, 256], P('feat'), may hold values from -6 to 6
- bias_first: float32 [256], replicated, may hold values from -3 to 3
- fetch_ids: int32 [32, 32, 2], P(None, ('dom', 'feat')), may hold values from 0 to 3, as said below
- tiles_out: bfloat16 [12288, 128, 128], P(('dom', 'feat')), may hold values from 9e-05 to 1, as said below
- out_dst: int32 [12288], P(('dom', 'feat')), may hold values from 0 to 3, as said below
- out_src: int32 [12288], P(('dom', 'feat')), may hold values from 0 to 63, as said below
- output_self_weight: bfloat16 [256, 172], replicated, may hold values from -1 to 1
- output_neighbour_weight: bfloat16 [256, 172], replicated, may hold values from -2 to 2
- bias_out: float32 [172], replicated, may hold values from -4 to 4
- labels: int32 [16384], P(('dom', 'feat')), may hold values from 0 to 171
Outputs:
- grad_w1_self: float32 [128, 256], P('feat')
- grad_w1_neigh: float32 [128, 256], P('feat')
- grad_b1: float32 [256], replicated
- grad_w3_self: float32 [256, 172], replicated
- grad_w3_neigh: float32 [256, 172], replicated
- grad_b3: float32 [172], replicated
Inputs may be any that keep to these rules, and one draw needn't show every extreme that they name: `first_dst`: each partition's first-layer tiles name every destination block at least once. `fetch_ids`: the 2 blocks one device requests from one owner are different. `out_dst`: each device's tiles name every local target block at least once. `out_src`: each device's tiles read every one of its slots at least once. `tiles_first`: every entry is positive. `tiles_out`: every entry is positive.
All inputs are finite; a program needn't handle non-finite values.
Results may differ from a plain program's by a relative error of at most 0.0034.
The roundings to bfloat16 on the way count: a program that leaves them out, or rounds other values in their place, can miss the bound.
Values may be sent and summed in bfloat16 or wider, within the bound.
No kernel may reach another device: no remote copies, remote signals or barrier semaphores. Data moves between devices by JAX's collectives and lax.ppermute only.
A program may use at most 192 MiB of HBM per device.

v0:
```python
import math

import jax
import jax.numpy as jnp
from jax import lax
from jax.sharding import PartitionSpec as P


def first_mean(features_t, tiles, dst_ids, src_ids, blocks):
    width = features_t.shape[0]
    side = tiles.shape[1]
    pool = features_t.reshape(width, features_t.shape[1] // side, side)
    picked = jnp.take(pool, src_ids, axis=1)
    product = jnp.einsum("fts,tds->tfd", picked, tiles, preferred_element_type=jnp.float32)
    summed = jnp.zeros((blocks + 1, width, side), jnp.float32).at[dst_ids].add(product)[:blocks]
    weight_sum = (
        jnp.zeros((blocks + 1, side), jnp.float32)
        .at[dst_ids]
        .add(jnp.sum(tiles, axis=2, dtype=jnp.float32))[:blocks]
    )
    neighbour_aggregate = summed / weight_sum[:, None, :]
    return neighbour_aggregate.transpose(1, 0, 2).reshape(width, blocks * side).astype(jnp.bfloat16)


def tile_mean(tiles, dst_ids, src_ids, source_pool, blocks):
    tile_total = tiles.shape[0]
    group_size = math.gcd(tile_total, 128)
    side = tiles.shape[1]
    width = source_pool.shape[-1]

    def add_group(summed, index):
        offset = index * group_size
        tile_part = lax.dynamic_slice_in_dim(tiles, offset, group_size, 0)
        dst_part = lax.dynamic_slice_in_dim(dst_ids, offset, group_size, 0)
        src_part = lax.dynamic_slice_in_dim(src_ids, offset, group_size, 0)
        product = jnp.einsum(
            "tij,tjw->tiw", tile_part, source_pool[src_part], preferred_element_type=jnp.float32
        )
        return (summed.at[dst_part].add(product), None)

    summed, unused = lax.scan(
        add_group,
        jnp.zeros((blocks, side, width), jnp.float32),
        jnp.arange(tile_total // group_size),
    )
    weight_sum = (
        jnp.zeros((blocks, side), jnp.float32)
        .at[dst_ids]
        .add(jnp.sum(tiles, axis=2, dtype=jnp.float32))
    )
    return (summed, weight_sum)


def tile_back(tiles, dst_ids, src_ids, grad_blocks, slots):
    tile_total = tiles.shape[0]
    group_size = math.gcd(tile_total, 128)
    side = tiles.shape[1]
    width = grad_blocks.shape[-1]

    def add_group(summed, index):
        offset = index * group_size
        tile_part = lax.dynamic_slice_in_dim(tiles, offset, group_size, 0)
        dst_part = lax.dynamic_slice_in_dim(dst_ids, offset, group_size, 0)
        src_part = lax.dynamic_slice_in_dim(src_ids, offset, group_size, 0)
        product = jnp.einsum(
            "tji,tjw->tiw", tile_part, grad_blocks[dst_part], preferred_element_type=jnp.float32
        )
        return (summed.at[src_part].add(product), None)

    summed, unused = lax.scan(
        add_group,
        jnp.zeros((slots, side, width), jnp.float32),
        jnp.arange(tile_total // group_size),
    )
    return summed


def on_device(
    inputs_t,
    tiles_first,
    first_dst,
    first_src,
    w1_self,
    w1_neigh,
    bias_first,
    fetch_ids,
    tiles_out,
    out_dst,
    out_src,
    output_self_weight,
    output_neighbour_weight,
    bias_out,
    labels,
):
    n_dom = lax.axis_size("dom")
    n_feat = lax.axis_size("feat")
    devices = n_dom * n_feat
    side = tiles_out.shape[1]
    rows_dev = labels.shape[0]
    blocks = rows_dev // side
    slots_peer = fetch_ids.shape[2]
    width = w1_self.shape[1]
    classes = output_self_weight.shape[1]
    scale = 1.0 / math.sqrt(devices * rows_dev)
    rows_dom = n_feat * rows_dev
    agg_t = first_mean(inputs_t, tiles_first, first_dst, first_src, n_feat * blocks)
    self_t = inputs_t[:, :rows_dom]
    contract = (((0,), (0,)), ((), ()))
    pre = (
        lax.psum_scatter(
            lax.dot_general(agg_t, w1_neigh, contract, preferred_element_type=jnp.float32)
            + lax.dot_general(self_t, w1_self, contract, preferred_element_type=jnp.float32),
            "feat",
            scatter_dimension=0,
            tiled=True,
        )
        + bias_first
    )
    hidden_units = jnp.maximum(pre, 0.0).astype(jnp.bfloat16)
    hidden_blocks = hidden_units.reshape(blocks, side, width)
    wanted = fetch_ids[:, 0, :]
    outgoing = hidden_blocks[wanted]
    incoming = lax.all_to_all(outgoing, ("dom", "feat"), split_axis=0, concat_axis=0, tiled=True)
    source_pool = incoming.reshape(devices * slots_peer, side, width)
    summed, weight_sum = tile_mean(tiles_out, out_dst, out_src, source_pool, blocks)
    neighbour_aggregate = (
        (summed / weight_sum[:, :, None]).reshape(rows_dev, width).astype(jnp.bfloat16)
    )
    logits = (
        jnp.dot(hidden_units, output_self_weight, preferred_element_type=jnp.float32)
        + jnp.dot(neighbour_aggregate, output_neighbour_weight, preferred_element_type=jnp.float32)
        + bias_out
    )
    expo = jnp.exp(logits - jnp.max(logits, axis=1, keepdims=True))
    prob = expo / jnp.sum(expo, axis=1, keepdims=True)
    onehot = (labels[:, None] == jnp.arange(classes, dtype=jnp.int32)[None, :]).astype(jnp.float32)
    logits_gradient = (prob - onehot) * scale
    logit_gradient = logits_gradient.astype(jnp.bfloat16)
    partial_output_self_weight = jnp.dot(
        hidden_units.T, logit_gradient, preferred_element_type=jnp.float32
    )
    partial_output_neighbour_weight = jnp.dot(
        neighbour_aggregate.T, logit_gradient, preferred_element_type=jnp.float32
    )
    part_b3 = jnp.sum(logits_gradient, axis=0)
    aggregate_gradient = jnp.dot(
        logit_gradient, output_neighbour_weight.T, preferred_element_type=jnp.float32
    )
    gnum = (aggregate_gradient.reshape(blocks, side, width) / weight_sum[:, :, None]).astype(
        jnp.bfloat16
    )
    slot_grad = tile_back(tiles_out, out_dst, out_src, gnum, devices * slots_peer).astype(
        jnp.bfloat16
    )
    slot_grad = slot_grad.reshape(devices, slots_peer, side, width)
    returned = lax.all_to_all(slot_grad, ("dom", "feat"), split_axis=0, concat_axis=0, tiled=True)
    picker = (wanted.reshape(-1)[:, None] == jnp.arange(blocks, dtype=jnp.int32)[None, :]).astype(
        jnp.bfloat16
    )
    back = jnp.einsum(
        "sb,siw->biw",
        picker,
        returned.reshape(devices * slots_peer, side, width),
        preferred_element_type=jnp.float32,
    )
    grad_hidden = back.reshape(rows_dev, width) + jnp.dot(
        logit_gradient, output_self_weight.T, preferred_element_type=jnp.float32
    )
    grad_pre = jnp.where(pre > 0.0, grad_hidden, 0.0).astype(jnp.bfloat16)
    part_b1 = jnp.sum(grad_pre.astype(jnp.float32), axis=0)
    grad_all = lax.all_gather(grad_pre, "feat", axis=0, tiled=True)
    part_w1s = jnp.dot(self_t, grad_all, preferred_element_type=jnp.float32)
    part_w1n = jnp.dot(agg_t, grad_all, preferred_element_type=jnp.float32)
    grad_w1_self, grad_w1_neigh = lax.psum((part_w1s, part_w1n), "dom")
    grad_w3_self, grad_w3_neigh, grad_b3, grad_b1 = lax.psum(
        (partial_output_self_weight, partial_output_neighbour_weight, part_b3, part_b1),
        ("dom", "feat"),
    )
    return (grad_w1_self, grad_w1_neigh, grad_b1, grad_w3_self, grad_w3_neigh, grad_b3)


def solution(mesh):
    in_specs = (
        P("feat", "dom"),
        P("dom", None, None),
        P("dom"),
        P("dom"),
        P("feat", None),
        P("feat", None),
        P(),
        P(None, ("dom", "feat"), None),
        P(("dom", "feat"), None, None),
        P(("dom", "feat")),
        P(("dom", "feat")),
        P(),
        P(),
        P(),
        P(("dom", "feat")),
    )
    out_specs = (P("feat", None), P("feat", None), P(), P(), P(), P())
    return jax.shard_map(
        on_device, mesh=mesh, in_specs=in_specs, out_specs=out_specs, check_vma=False
    )
```

profile of v0, /device:TPU:0, one launch (start us, length us, event | category | flops | bytes accessed | tf_op | source)
XLA Modules:
  0.0 851.3 jit_solution(13606272173968878322)
XLA Ops:
  10.3 2.2 convert_reduce_fusion.1
  14.0 2.8 fusion.9
  16.9 3.2 scatter_fusion.2
  20.6 1.8 convolution_add_fusion
  22.7 34.0 %reduce-scatter.2.cloned.1.call-done = f32[512,256]{1,0:T(8,128)} async-done(((f32[2048,256]{1,0:T(8,128)}), f32[512,256]{1,0:T(8,128)}) %reduce-scatter.2.cloned.1.call-update) | async-done | bytes 524304 | tf_op jit(solution)/shard_map/reduce_scatter | solution.py:110
  57.9 2.8 gather_fusion.3
  60.6 4.7 all-to-all-start
  65.4 7.6 convert_reduce_fusion
  73.0 3.1 scatter_custom_fusion.4
  77.2 82.6 %all-to-all-done = bf16[32,2,128,256]{3,2,1,0:T(8,128)(2,1)} async-done(((bf16[32,2,128,256]{3,2,1,0:T(8,128)(2,1)}), bf16[32,2,128,256]{3,2,1,0:T(8,128)(2,1)}, u32[]{:S(2)}, u32[]{:S(2)}) %all-to-all-start) | async-done | bytes 4194336 | tf_op jit(solution)/shard_map/all_to_all | solution.py:123
  159.8 140.8 %while.20 = (s32[]{:T(128)}, f32[4,128,256]{2,1,0:T(8,128)S(1)}, s32[3]{0:T(128)S(1)}, s32[384]{0:T(512)S(1)}, bf16[384,128,128]{2,1,0:T(8,128)(2,1)}, /*index=5...) while((s32[]{:T(128)}, f32[4,128,256]{2,1,0:T(8,128)S(1)}, ...), condition=%wide.region_6.7_spmd, body=%wide.region_4.6_spmd.sunk | while | flops 1077937920 | bytes 96476848 | solution.py:41
  161.2 8.7 %gather_fusion = bf16[128,128,256]{2,1,0:T(8,128)(2,1)} fusion(bf16[64,128,256]{2,1,0:T(8,128)(2,1)} %get-tuple-element.283, s32[1024]{0:T(1024)S(1)} %pad_clamp_fusion.6), kind=kCustom, calls=%fused_computation.clone.1 | custom fusion | bytes 16777728 | tf_op jit(solution)/shard_map/while/body/eval_jaxpr/gather | solution.py:37
  169.9 12.7 %fusion.74 = f32[128,128,256]{2,1,0:T(8,128)} fusion(bf16[128,128,256]{2,1,0:T(8,128)(2,1)} %gather_fusion, bf16[384,128,128]{2,1,0:T(8,128)(2,1)} %get-tuple-element.281, s32[]{:T(128)S(6)} %select_n.81), kind=kOutput, calls=%fused_computation.9.clone.1 | convolution fusion | flops 1073741824 | bytes 29360132 | tf_op jit(solution)/shard_map/while/body/eval_jaxpr/tij,tjw->tiw/dot_general | solution.py:36
  182.6 24.1 %scatter_fusion = f32[4,128,256]{2,1,0:T(8,128)S(1)} fusion(f32[4,128,256]{2,1,0:T(8,128)S(1)} %get-tuple-element.267, s32[128]{0:T(128)S(1)} %get-tuple-element.244, f32[128,128,256]{2,1,0:T(8,128)} %fusion.74), kind=kCustom, calls=%fused_computation.4.clone.1 | custom fusion | flops 4194304 | bytes 50332160 | tf_op jit(solution)/shard_map/while/body/eval_jaxpr/scatter-add | solution.py:39
  208.1 8.8 %gather_fusion = bf16[128,128,256]{2,1,0:T(8,128)(2,1)} fusion(bf16[64,128,256]{2,1,0:T(8,128)(2,1)} %get-tuple-element.283, s32[1024]{0:T(1024)S(1)} %pad_clamp_fusion.6), kind=kCustom, calls=%fused_computation.clone.1 | custom fusion | bytes 16777728 | tf_op jit(solution)/shard_map/while/body/eval_jaxpr/gather | solution.py:37
  216.8 12.7 %fusion.74 = f32[128,128,256]{2,1,0:T(8,128)} fusion(bf16[128,128,256]{2,1,0:T(8,128)(2,1)} %gather_fusion, bf16[384,128,128]{2,1,0:T(8,128)(2,1)} %get-tuple-element.281, s32[]{:T(128)S(6)} %select_n.81), kind=kOutput, calls=%fused_computation.9.clone.1 | convolution fusion | flops 1073741824 | bytes 29360132 | tf_op jit(solution)/shard_map/while/body/eval_jaxpr/tij,tjw->tiw/dot_general | solution.py:36
  229.6 24.1 %scatter_fusion = f32[4,128,256]{2,1,0:T(8,128)S(1)} fusion(f32[4,128,256]{2,1,0:T(8,128)S(1)} %get-tuple-element.267, s32[128]{0:T(128)S(1)} %get-tuple-element.244, f32[128,128,256]{2,1,0:T(8,128)} %fusion.74), kind=kCustom, calls=%fused_computation.4.clone.1 | custom fusion | flops 4194304 | bytes 50332160 | tf_op jit(solution)/shard_map/while/body/eval_jaxpr/scatter-add | solution.py:39
  255.0 8.8 %gather_fusion = bf16[128,128,256]{2,1,0:T(8,128)(2,1)} fusion(bf16[64,128,256]{2,1,0:T(8,128)(2,1)} %get-tuple-element.283, s32[1024]{0:T(1024)S(1)} %pad_clamp_fusion.6), kind=kCustom, calls=%fused_computation.clone.1 | custom fusion | bytes 16777728 | tf_op jit(solution)/shard_map/while/body/eval_jaxpr/gather | solution.py:37
  263.8 12.7 %fusion.74 = f32[128,128,256]{2,1,0:T(8,128)} fusion(bf16[128,128,256]{2,1,0:T(8,128)(2,1)} %gather_fusion, bf16[384,128,128]{2,1,0:T(8,128)(2,1)} %get-tuple-element.281, s32[]{:T(128)S(6)} %select_n.81), kind=kOutput, calls=%fused_computation.9.clone.1 | convolution fusion | flops 1073741824 | bytes 29360132 | tf_op jit(solution)/shard_map/while/body/eval_jaxpr/tij,tjw->tiw/dot_general | solution.py:36
  276.5 24.1 %scatter_fusion = f32[4,128,256]{2,1,0:T(8,128)S(1)} fusion(f32[4,128,256]{2,1,0:T(8,128)S(1)} %get-tuple-element.267, s32[128]{0:T(128)S(1)} %get-tuple-element.244, f32[128,128,256]{2,1,0:T(8,128)} %fusion.74), kind=kCustom, calls=%fused_computation.4.clone.1 | custom fusion | flops 4194304 | bytes 50332160 | tf_op jit(solution)/shard_map/while/body/eval_jaxpr/scatter-add | solution.py:39
  302.7 4.3 broadcast_in_dim.65
  307.0 176.9 %while.21 = (s32[]{:T(128)}, f32[64,128,256]{2,1,0:T(8,128)}, s32[3]{0:T(128)S(1)}, s32[384]{0:T(512)S(1)}, bf16[384,128,128]{2,1,0:T(8,128)(2,1)}, /*index=5*/s...) while((s32[]{:T(128)}, f32[64,128,256]{2,1,0:T(8,128)}, ...), condition=%wide.region_13.14_spmd, body=%wide.region_11.13_spmd.sunk | while | flops 1077937920 | bytes 96476848 | solution.py:70
  308.3 6.5 gather_fusion.1
  314.8 12.8 %fusion.77 = f32[128,128,256]{2,1,0:T(8,128)} fusion(bf16[128,128,256]{2,1,0:T(8,128)(2,1)} %gather_fusion.1, bf16[384,128,128]{2,1,0:T(8,128)(2,1)} %get-tuple-element.314, s32[]{:T(128)S(6)} %select_n.83), kind=kOutput, calls=%fused_computation.15.clone.1 | convolution fusion | flops 1073741824 | bytes 29360132 | tf_op jit(solution)/shard_map/while/body/eval_jaxpr/tji,tjw->tiw/dot_general | solution.py:65
  327.6 38.3 %scatter_fusion.1 = f32[64,128,256]{2,1,0:T(8,128)} fusion(f32[64,128,256]{2,1,0:T(8,128)} %get-tuple-element.300, s32[128]{0:T(128)S(1)} %get-tuple-element.253, f32[128,128,256]{2,1,0:T(8,128)} %fusion.77), kind=kCustom, calls=%fused_computation.5.clone.1 | custom fusion | flops 4194304 | bytes 50332160 | tf_op jit(solution)/shard_map/while/body/eval_jaxpr/scatter-add | solution.py:68
  367.2 6.5 gather_fusion.1
  373.7 12.8 %fusion.77 = f32[128,128,256]{2,1,0:T(8,128)} fusion(bf16[128,128,256]{2,1,0:T(8,128)(2,1)} %gather_fusion.1, bf16[384,128,128]{2,1,0:T(8,128)(2,1)} %get-tuple-element.314, s32[]{:T(128)S(6)} %select_n.83), kind=kOutput, calls=%fused_computation.15.clone.1 | convolution fusion | flops 1073741824 | bytes 29360132 | tf_op jit(solution)/shard_map/while/body/eval_jaxpr/tji,tjw->tiw/dot_general | solution.py:65
  386.5 38.4 %scatter_fusion.1 = f32[64,128,256]{2,1,0:T(8,128)} fusion(f32[64,128,256]{2,1,0:T(8,128)} %get-tuple-element.300, s32[128]{0:T(128)S(1)} %get-tuple-element.253, f32[128,128,256]{2,1,0:T(8,128)} %fusion.77), kind=kCustom, calls=%fused_computation.5.clone.1 | custom fusion | flops 4194304 | bytes 50332160 | tf_op jit(solution)/shard_map/while/body/eval_jaxpr/scatter-add | solution.py:68
  426.2 6.5 gather_fusion.1
  432.7 12.8 %fusion.77 = f32[128,128,256]{2,1,0:T(8,128)} fusion(bf16[128,128,256]{2,1,0:T(8,128)(2,1)} %gather_fusion.1, bf16[384,128,128]{2,1,0:T(8,128)(2,1)} %get-tuple-element.314, s32[]{:T(128)S(6)} %select_n.83), kind=kOutput, calls=%fused_computation.15.clone.1 | convolution fusion | flops 1073741824 | bytes 29360132 | tf_op jit(solution)/shard_map/while/body/eval_jaxpr/tji,tjw->tiw/dot_general | solution.py:65
  445.5 38.4 %scatter_fusion.1 = f32[64,128,256]{2,1,0:T(8,128)} fusion(f32[64,128,256]{2,1,0:T(8,128)} %get-tuple-element.300, s32[128]{0:T(128)S(1)} %get-tuple-element.253, f32[128,128,256]{2,1,0:T(8,128)} %fusion.77), kind=kCustom, calls=%fused_computation.5.clone.1 | custom fusion | flops 4194304 | bytes 50332160 | tf_op jit(solution)/shard_map/while/body/eval_jaxpr/scatter-add | solution.py:68
  483.9 4.0 convert_element_type.54
  487.9 6.4 copy.50
  494.3 5.6 all-to-all-start.1
  500.1 94.1 %all-to-all-done.1 = bf16[32,2,128,256]{3,1,2,0:T(2,128)(2,1)} async-done(((bf16[32,2,128,256]{3,1,2,0:T(2,128)(2,1)}), bf16[32,2,128,256]{3,1,2,0:T(2,128)(2,1)}, u32[]{:S(2)}, u32[]{:S(2)}) %all-to-all-start.1) | async-done | bytes 4194336 | tf_op jit(solution)/shard_map/all_to_all | solution.py:156
  594.2 8.9 %copy.51 = bf16[32,2,128,256]{3,1,0,2:T(2,128)(2,1)} copy(bf16[32,2,128,256]{3,1,2,0:T(2,128)(2,1)} %all-to-all-done.1) | data formatting | bytes 8388608 | tf_op jit(solution)/shard_map/all_to_all | solution.py:156
  603.2 7.3 reshape.87
  610.5 2.8 fusion.30
  616.5 15.6 %all-gather.2.cloned.1.call-done = bf16[2048,256]{1,0:T(8,128)(2,1)} async-done(((bf16[512,256]{1,0:T(8,128)(2,1)}), bf16[2048,256]{1,0:T(8,128)(2,1)}) %all-gather.2.cloned.1.call-update) | async-done | bytes 1048592 | tf_op jit(solution)/shard_map/all_gather | solution.py:171
  632.1 2.1 fusion.16
  634.2 2.1 convolution_bitcast_fusion
  636.4 39.4 %all-reduce = (f32[256]{0:T(256)}, f32[172]{0:T(256)}) all-reduce(f32[256]{0:T(256)S(1)} %get-tuple-element.159, f32[172]{0:T(256)S(1)} %copy-done.25), channel_id=1, replica_groups=mesh['dom'=8,'feat'=4] {'dom','feat'}, use_global_device_ids=true, to_apply=%region_17.18 | all-reduce | flops 428 | bytes 3424 | tf_op jit(solution)/shard_map/psum | solution.py:175
  675.8 90.1 %all-reduce.6.cloned.1.call-done = (f32[256,172]{0,1:T(8,128)}, f32[256,172]{0,1:T(8,128)}) async-done(((f32[256,172]{0,1:T(8,128)}, f32[256,172]{0,1:T(8,128)}), (f32[256,172]{0,1:T(8,128)}, f32[256,172]{0,1:T(8,128)})) %all-reduce.6.cloned.1.call-update) | async-done | bytes 352272 | tf_op jit(solution)/shard_map/psum | solution.py:175
  765.9 72.9 %all-reduce.8.cloned.1.call-done = (f32[32,256]{1,0:T(8,128)}, f32[32,256]{1,0:T(8,128)}) async-done(((f32[32,256]{1,0:T(8,128)}, f32[32,256]{1,0:T(8,128)}), (f32[32,256]{1,0:T(8,128)}, f32[32,256]{1,0:T(8,128)})) %all-reduce.8.cloned.1.call-update) | async-done | bytes 65552 | tf_op jit(solution)/shard_map/psum | solution.py:174
  838.8 1.4 copy.84
  840.2 1.4 copy.85
  841.5 1.6 copy.86
  843.1 1.6 copy.87
  (118 shorter events, 16.9 us)
Async XLA Ops:
  7.2 293.6 %copy-start = (bf16[256,172]{0,1:T(8,128)(2,1)S(1)}, bf16[256,172]{0,1:T(8,128)(2,1)}, u32[]{:S(2)}) copy-start(bf16[256,172]{0,1:T(8,128)(2,1)} %param.31) | copy-start | bytes 264196
  7.2 13.4 %copy-start.12 = (bf16[32,4096]{1,0:T(8,128)(2,1)S(1)}, bf16[32,4096]{1,0:T(8,128)(2,1)}, u32[]{:S(2)}) copy-start(bf16[32,4096]{1,0:T(8,128)(2,1)} %param.19) | copy-start | bytes 786436
  7.2 12.9 %copy-start.20 = (bf16[32,256]{1,0:T(8,128)(2,1)S(1)}, bf16[32,256]{1,0:T(8,128)(2,1)}, u32[]{:S(2)}) copy-start(bf16[32,256]{1,0:T(8,128)(2,1)} %param.24) | copy-start | bytes 49156
  7.2 13.4 %copy-start.21 = (bf16[32,256]{1,0:T(8,128)(2,1)S(1)}, bf16[32,256]{1,0:T(8,128)(2,1)}, u32[]{:S(2)}) copy-start(bf16[32,256]{1,0:T(8,128)(2,1)} %param.23) | copy-start | bytes 49156
  7.2 49.5 %reduce-scatter.2.cloned.1.call-start = ((), (), s32[]{:S(2)}) async-start(), calls=%async_computation.3 | async-start | bytes 2621440 | tf_op jit(solution)/shard_map/reduce_scatter | solution.py:110
  13.3 9.1 %copy-start.16 = (f32[16,128]{1,0:T(8,128)}, f32[16,128]{1,0:T(8,128)S(1)}, u32[]{:S(2)}) copy-start(f32[16,128]{1,0:T(8,128)S(1)} %slice.21) | copy-start | bytes 24580
  13.4 9.1 %copy-start.26 = (s32[32,1,2]{0,2,1:T(2,128)S(1)}, s32[32,1,2]{0,2,1:T(2,128)}, u32[]{:S(2)}) copy-start(s32[32,1,2]{0,2,1:T(2,128)} %param.26) | copy-start | bytes 772
  13.4 43.4 %copy-start.23 = (f32[256]{0:T(256)S(1)}, f32[256]{0:T(256)}, u32[]{:S(2)}) copy-start(f32[256]{0:T(256)} %param.25) | copy-start | bytes 3076
  20.1 2.6 copy-start.4
  57.8 18.3 %copy-start.2 = (bf16[512,256]{1,0:T(8,128)(2,1)}, bf16[512,256]{1,0:T(8,128)(2,1)S(1)}, u32[]{:S(2)}) copy-start(bf16[512,256]{1,0:T(8,128)(2,1)S(1)} %maximum_convert_fusion) | copy-start | bytes 786436
  57.9 7.5 copy-start.18
  60.6 99.1 %all-to-all-start = ((bf16[32,2,128,256]{3,2,1,0:T(8,128)(2,1)}), bf16[32,2,128,256]{3,2,1,0:T(8,128)(2,1)}, u32[]{:S(2)}, u32[]{:S(2)}) async-start(bf16[32,2,128,256]{3,2,1,0:T(8,128)(2,1)} %bitcast.72), calls=%async_computation.1 | async-start | bytes 8388608 | tf_op jit(solution)/shard_map/all_to_all | solution.py:123
  65.4 10.8 %copy-start.14 = (bf16[256,172]{0,1:T(8,128)(2,1)S(1)}, bf16[256,172]{0,1:T(8,128)(2,1)}, u32[]{:S(2)}) copy-start(bf16[256,172]{0,1:T(8,128)(2,1)} %param.30) | copy-start | bytes 264196
  65.4 94.4 %copy-start.22 = (s32[384]{0:T(512)S(1)}, s32[384]{0:T(512)}, u32[]{:S(2)}) copy-start(s32[384]{0:T(512)} %param.29) | copy-start | bytes 4612
  159.8 140.8 %copy-start.19 = (f32[4,128]{1,0:T(4,128)S(1)}, f32[4,128]{1,0:T(4,128)}, u32[]{:S(2)}) copy-start(f32[4,128]{1,0:T(4,128)} %scatter_custom_fusion.4) | copy-start | bytes 6148
  159.8 141.0 %copy-start.11 = (f32[512,172]{0,1:T(8,128)S(1)}, f32[512,172]{0,1:T(8,128)}, u32[]{:S(2)}) copy-start(f32[512,172]{0,1:T(8,128)} %fusion.37) | copy-start | bytes 1056772
  159.8 141.0 %copy-start.29 = (f32[172]{0:T(256)S(1)}, f32[172]{0:T(256)}, u32[]{:S(2)}) copy-start(f32[172]{0:T(256)} %param.32) | copy-start | bytes 2068
  159.8 141.3 %copy-start.28 = (s32[512]{0:T(512)S(1)}, s32[512]{0:T(512)}, u32[]{:S(2)}) copy-start(s32[512]{0:T(512)} %param.33) | copy-start | bytes 6148
  300.7 1.8 copy-start.8
  301.9 0.7 copy-start.6
  487.9 12.0 %copy-start.27 = (s32[32,1,2]{0,2,1:T(2,128)S(1)}, s32[32,1,2]{0,2,1:T(2,128)}, u32[]{:S(2)}) copy-start(s32[32,1,2]{0,2,1:T(2,128)} %param.26) | copy-start | bytes 772
  494.3 99.9 %all-to-all-start.1 = ((bf16[32,2,128,256]{3,1,2,0:T(2,128)(2,1)}), bf16[32,2,128,256]{3,1,2,0:T(2,128)(2,1)}, u32[]{:S(2)}, u32[]{:S(2)}) async-start(bf16[32,2,128,256]{3,1,2,0:T(2,128)(2,1)} %copy.50), calls=%async_computation.2 | async-start | bytes 8388608 | tf_op jit(solution)/shard_map/all_to_all | solution.py:156
  499.8 132.3 %all-gather.2.cloned.1.call-start = ((), (), s32[]{:S(2)}) async-start(), calls=%async_computation.4 | async-start | bytes 1310720 | tf_op jit(solution)/shard_map/all_gather | solution.py:171
  603.1 10.4 %copy-start.7 = (bf16[512,172]{0,1:T(8,128)(2,1)S(1)}, bf16[512,172]{0,1:T(8,128)(2,1)}, u32[]{:S(2)}) copy-start(bf16[512,172]{0,1:T(8,128)(2,1)} %copy-done.6) | copy-start | bytes 528388
  603.1 10.4 %copy-start.10 = (f32[512,256]{1,0:T(8,128)S(1)}, f32[512,256]{1,0:T(8,128)}, u32[]{:S(2)}) copy-start(f32[512,256]{1,0:T(8,128)} %reduce-scatter.2.cloned.1.call-done) | copy-start | bytes 1572868
  603.1 10.4 %copy-start.15 = (bf16[256,172]{0,1:T(8,128)(2,1)S(1)}, bf16[256,172]{0,1:T(8,128)(2,1)}, u32[]{:S(2)}) copy-start(bf16[256,172]{0,1:T(8,128)(2,1)} %param.30) | copy-start | bytes 264196
  603.1 10.4 %copy-start.24 = (f32[256]{0:T(256)S(1)}, f32[256]{0:T(256)}, u32[]{:S(2)}) copy-start(f32[256]{0:T(256)} %param.25) | copy-start | bytes 3076
  603.1 11.5 %copy-start.9 = (bf16[4,128,256]{2,1,0:T(8,128)(2,1)S(1)}, bf16[4,128,256]{2,1,0:T(8,128)(2,1)}, u32[]{:S(2)}) copy-start(bf16[4,128,256]{2,1,0:T(8,128)(2,1)} %copy-done.8) | copy-start | bytes 786436
  603.1 12.4 %copy-start.3 = (bf16[512,256]{1,0:T(8,128)(2,1)S(1)}, bf16[512,256]{1,0:T(8,128)(2,1)}, u32[]{:S(2)}) copy-start(bf16[512,256]{1,0:T(8,128)(2,1)} %copy-done.2) | copy-start | bytes 786436
  603.1 29.0 %copy-start.5 = (f32[17,32,128]{2,1,0:T(8,128)S(1)}, f32[17,32,128]{2,1,0:T(8,128)}, u32[]{:S(2)}) copy-start(f32[17,32,128]{2,1,0:T(8,128)} %copy-done.4) | copy-start | bytes 835588
  603.1 29.0 %copy-start.17 = (f32[16,128]{1,0:T(8,128)S(1)}, f32[16,128]{1,0:T(8,128)}, u32[]{:S(2)}) copy-start(f32[16,128]{1,0:T(8,128)} %copy-done.16) | copy-start | bytes 24580
  603.2 31.1 %copy-start.13 = (bf16[32,4096]{1,0:T(8,128)(2,1)S(1)}, bf16[32,4096]{1,0:T(8,128)(2,1)}, u32[]{:S(2)}) copy-start(bf16[32,4096]{1,0:T(8,128)(2,1)} %param.19) | copy-start | bytes 786436
  603.2 33.2 %copy-start.25 = (f32[172]{0:T(256)S(1)}, f32[172]{0:T(256)}, u32[]{:S(2)}) copy-start(f32[172]{0:T(256)} %get-tuple-element.155) | copy-start | bytes 2068
  603.2 241.6 %copy-start.1 = (bf16[256,172]{0,1:T(8,128)(2,1)S(1)}, bf16[256,172]{0,1:T(8,128)(2,1)}, u32[]{:S(2)}) copy-start(bf16[256,172]{0,1:T(8,128)(2,1)} %param.31) | copy-start | bytes 264196
  614.5 151.4 %all-reduce.6.cloned.1.call-start = ((), (), s32[]{:S(2)}) async-start(), calls=%async_computation.5 | async-start | bytes 720896 | tf_op jit(solution)/shard_map/psum | solution.py:175
  616.4 222.4 %all-reduce.8.cloned.1.call-start = ((), (), s32[]{:S(2)}) async-start(), calls=%async_computation.6 | async-start | bytes 131072 | tf_op jit(solution)/shard_map/psum | solution.py:174
Sparse Core Ops, SparseCore 0:
  22.6 34.1 reduce-scatter.1
  614.7 17.3 all-gather.1
  639.0 126.8 all-reduce.5
  769.9 68.8 all-reduce.7
where the time goes:
time: 853 us; the launch traced here: 851 us
  waiting for transfers between devices  389 us (46%)
  other arithmetic  213 us (25%)
  matrix products  93 us (11%)
  local copies, waits for them, and re-layouts  87.6 us (10%)
  blocking collectives  39.4 us (5%)
  between operations  14.3 us (2%)
  starting transfers between devices  10.5 us (1%)
    scatter-add x3, other arithmetic, add_group(): return (summed.at[src_part].add(product), None)  115 us
    all_to_all x1, waiting for transfers between devices, on_device(): lax.all_to_all(slot_grad, ('dom', 'feat'), split_axis=0, concat_axis=0, t...  94.1 us
    psum x1, waiting for transfers between devices, on_device(): lax.psum((partial_output_self_weight, partial_output_neighbour_weight, pa...  90.1 us
    all_to_all x1, waiting for transfers between devices, on_device(): lax.all_to_all(outgoing, ('dom', 'feat'), split_axis=0, concat_axis=0, ti...  82.6 us
    psum x1, waiting for transfers between devices, on_device(): grad_w1_self, grad_w1_neigh = lax.psum((part_w1s, part_w1n), 'dom')  72.9 us
    scatter-add x3, other arithmetic, add_group(): return (summed.at[dst_part].add(product), None)  72.2 us
    psum x1, blocking collectives, on_device(): lax.psum((partial_output_self_weight, partial_output_neighbour_weight, pa...  39.4 us
    dot_general x3, matrix products, add_group(): jnp.einsum('tji,tjw->tiw', tile_part, grad_blocks[dst_part], preferred_el...  38.3 us
  transfers between devices with their start and end apart: 6, of which 6 were waited for; matrix products, arithmetic and copies ran while one was open for 2% of the time, Pallas kernels for 0%

commit v1 on v0

v1 whole, which is shorter than its diff:
```python
import math

import jax
import jax.numpy as jnp
from jax import lax
from jax.experimental import pallas as pl
from jax.experimental.pallas import tpu as pltpu
from jax.sharding import PartitionSpec as P

F32 = jnp.float32
BF16 = jnp.bfloat16
BIG = pltpu.CompilerParams(vmem_limit_bytes=58 << 20)
VMEM = pl.BlockSpec(memory_space=pltpu.VMEM)


def group_of(count, most):
    return math.gcd(count, most)


def first_layer(features_t, tiles, dst_ids, src_ids, blocks, owners):
    width, nodes = features_t.shape
    total, side, _ = tiles.shape
    step = group_of(total, 32)
    unroll = group_of(step, 16)
    steps = total // step
    per_owner = blocks // owners

    def kernel(dst_s, src_s, tile_ref, feat_ref, out_ref, acc):
        i = pl.program_id(0)

        @pl.when(i == 0)
        def _():
            acc[...] = jnp.zeros_like(acc)

        ones = jnp.ones((16, side), BF16)

        def body(g, carry):
            products = []
            for u in range(unroll):
                t = g * unroll + u
                start = pl.multiple_of(src_s[i * step + t] * side, side)
                left = jnp.concatenate([feat_ref[:, pl.ds(start, side)], ones], axis=0)
                products.append(
                    lax.dot_general(
                        left, tile_ref[t], (((1,), (1,)), ((), ())), preferred_element_type=F32
                    )
                )
            for u in range(unroll):
                acc[dst_s[i * step + g * unroll + u]] += products[u]
            return carry

        lax.fori_loop(0, step // unroll, body, 0)

        @pl.when(i == steps - 1)
        def _():
            for q in range(owners):
                for b in range(per_owner):
                    block = acc[q * per_owner + b]
                    mean = block[:width] / block[width : width + 1]
                    out_ref[q, :width, b * side : (b + 1) * side] = mean.astype(BF16)
                rows = per_owner * side
                out_ref[q, width:, :] = feat_ref[:, q * rows : (q + 1) * rows]

    shape = (owners, 2 * width, per_owner * side)
    return pl.pallas_call(
        kernel,
        grid_spec=pltpu.PrefetchScalarGridSpec(
            num_scalar_prefetch=2,
            grid=(steps,),
            in_specs=[
                pl.BlockSpec((step, side, side), lambda i, *_: (i, 0, 0)),
                pl.BlockSpec((width, nodes), lambda i, *_: (0, 0)),
            ],
            out_specs=pl.BlockSpec(shape, lambda i, *_: (0, 0, 0)),
            scratch_shapes=[pltpu.VMEM((blocks, width + 16, side), F32)],
        ),
        out_shape=jax.ShapeDtypeStruct(shape, BF16),
        compiler_params=BIG,
        name="first_layer",
    )(dst_ids, src_ids, tiles, features_t)


def hidden_layer(parts_t, weights, bias):
    rows = parts_t.shape[1]
    width = weights.shape[1]

    def kernel(parts_ref, w_ref, b_ref, pre_ref, hidden_ref):
        pre = (
            lax.dot_general(
                parts_ref[...], w_ref[...], (((0,), (0,)), ((), ())), preferred_element_type=F32
            )
            + b_ref[...]
        )
        pre_ref[...] = pre
        hidden_ref[...] = jnp.maximum(pre, 0.0).astype(BF16)

    return pl.pallas_call(
        kernel,
        in_specs=[VMEM] * 3,
        out_specs=[VMEM] * 2,
        out_shape=[
            jax.ShapeDtypeStruct((rows, width), F32),
            jax.ShapeDtypeStruct((rows, width), BF16),
        ],
        compiler_params=BIG,
        name="hidden_layer",
    )(parts_t, weights, bias)


def row_weights(tiles, dst_ids, blocks):
    total, side, _ = tiles.shape
    step = group_of(total, 32)
    unroll = group_of(step, 8)
    steps = total // step

    def kernel(dst_s, tile_ref, out_ref, acc):
        i = pl.program_id(0)

        @pl.when(i == 0)
        def _():
            acc[...] = jnp.zeros_like(acc)

        def body(g, carry):
            for u in range(unroll):
                t = g * unroll + u
                acc[dst_s[i * step + t]] += tile_ref[t].astype(F32)
            return carry

        lax.fori_loop(0, step // unroll, body, 0)

        @pl.when(i == steps - 1)
        def _():
            for b in range(blocks):
                out_ref[b] = jnp.broadcast_to(
                    jnp.sum(acc[b], axis=1, keepdims=True), (side, side)
                )

    return pl.pallas_call(
        kernel,
        grid_spec=pltpu.PrefetchScalarGridSpec(
            num_scalar_prefetch=1,
            grid=(steps,),
            in_specs=[pl.BlockSpec((step, side, side), lambda i, *_: (i, 0, 0))],
            out_specs=pl.BlockSpec((blocks, side, side), lambda i, *_: (0, 0, 0)),
            scratch_shapes=[pltpu.VMEM((blocks, side, side), F32)],
        ),
        out_shape=jax.ShapeDtypeStruct((blocks, side, side), F32),
        compiler_params=BIG,
        cost_estimate=pl.CostEstimate(
            flops=2 * total * side * side, bytes_accessed=2 * total * side * side, transcendentals=0
        ),
        name="row_weights",
    )(dst_ids, tiles)


def output_layer(
    tiles, dst_ids, src_ids, pool, weight, hidden, w_self, w_neigh, bias, labels, scale
):
    total, side, _ = tiles.shape
    blocks = weight.shape[0]
    width = pool.shape[2]
    classes = w_self.shape[1]
    step = group_of(total, 32)
    unroll = group_of(step, 32)
    steps = total // step
    lead = (((0,), (0,)), ((), ()))
    last = (((1,), (1,)), ((), ()))

    def kernel(
        dst_s, src_s, tile_ref, pool_ref, weight_ref, hidden_ref, ws_ref, wn_ref, bias_ref,
        labels_ref, gws_ref, gwn_ref, gb_ref, gnum_ref, own_ref, acc,
    ):
        i = pl.program_id(0)

        @pl.when(i == 0)
        def _():
            acc[...] = jnp.zeros_like(acc)

        def body(g, carry):
            products = []
            for u in range(unroll):
                t = g * unroll + u
                products.append(
                    jnp.dot(tile_ref[t], pool_ref[src_s[i * step + t]], preferred_element_type=F32)
                )
            for u in range(unroll):
                acc[dst_s[i * step + g * unroll + u]] += products[u]
            return carry

        lax.fori_loop(0, step // unroll, body, 0)

        @pl.when(i == steps - 1)
        def _():
            gws = jnp.zeros((width, classes), F32)
            gwn = jnp.zeros((width, classes), F32)
            gb = jnp.zeros((1, classes), F32)
            for b in range(blocks):
                rows = slice(b * side, (b + 1) * side)
                under = weight_ref[b][:, :1]
                mean = (acc[b] / under).astype(BF16)
                own = hidden_ref[rows, :]
                logits = (
                    jnp.dot(own, ws_ref[...], preferred_element_type=F32)
                    + jnp.dot(mean, wn_ref[...], preferred_element_type=F32)
                    + bias_ref[...]
                )
                expo = jnp.exp(logits - jnp.max(logits, axis=1, keepdims=True))
                prob = expo / jnp.sum(expo, axis=1, keepdims=True)
                lane = lax.broadcasted_iota(jnp.int32, (side, classes), 1)
                onehot = jnp.where(labels_ref[rows, :] == lane, 1.0, 0.0)
                grad = (prob - onehot) * scale
                glog = grad.astype(BF16)
                gb = gb + jnp.sum(grad, axis=0, keepdims=True)
                gws = gws + lax.dot_general(own, glog, lead, preferred_element_type=F32)
                gwn = gwn + lax.dot_general(mean, glog, lead, preferred_element_type=F32)
                back = lax.dot_general(glog, wn_ref[...], last, preferred_element_type=F32)
                gnum_ref[b] = (back / under).astype(BF16)
                own_ref[rows, :] = lax.dot_general(
                    glog, ws_ref[...], last, preferred_element_type=F32
                )
            gws_ref[...] = gws
            gwn_ref[...] = gwn
            gb_ref[...] = gb

    def whole(*shape):
        return pl.BlockSpec(shape, lambda i, *_: (0,) * len(shape))

    rows = blocks * side
    out = [
        ((width, classes), F32),
        ((width, classes), F32),
        ((1, classes), F32),
        ((blocks, side, width), BF16),
        ((rows, width), F32),
    ]
    return pl.pallas_call(
        kernel,
        grid_spec=pltpu.PrefetchScalarGridSpec(
            num_scalar_prefetch=2,
            grid=(steps,),
            in_specs=[
                pl.BlockSpec((step, side, side), lambda i, *_: (i, 0, 0)),
                pl.BlockSpec(memory_space=pltpu.VMEM),
                whole(blocks, side, side),
                whole(rows, width),
                whole(width, classes),
                whole(width, classes),
                whole(1, classes),
                whole(rows, 1),
            ],
            out_specs=[whole(*s) for s, _ in out],
            scratch_shapes=[pltpu.VMEM((blocks, side, width), F32)],
        ),
        out_shape=[jax.ShapeDtypeStruct(s, d) for s, d in out],
        compiler_params=BIG,
        name="output_layer",
    )(
        dst_ids, src_ids, tiles, pool, weight, hidden, w_self, w_neigh,
        bias.reshape(1, classes), labels.reshape(rows, 1),
    )


def slot_gradients(tiles, dst_ids, src_ids, gnum, slots):
    total, side, _ = tiles.shape
    width = gnum.shape[2]
    step = group_of(total, 32)
    unroll = group_of(step, 32)
    steps = total // step
    piece = group_of(slots, 8)

    def kernel(dst_s, src_s, tile_ref, gnum_ref, out_ref, acc):
        i = pl.program_id(0)

        @pl.when(i == 0)
        def _():
            acc[...] = jnp.zeros_like(acc)

        @pl.when(i < steps)
        def _():
            def body(g, carry):
                products = []
                for u in range(unroll):
                    t = g * unroll + u
                    products.append(
                        lax.dot_general(
                            tile_ref[t], gnum_ref[dst_s[i * step + t]],
                            (((0,), (0,)), ((), ())), preferred_element_type=F32,
                        )
                    )
                for u in range(unroll):
                    acc[src_s[i * step + g * unroll + u]] += products[u]
                return carry

            lax.fori_loop(0, step // unroll, body, 0)

        @pl.when(i >= steps)
        def _():
            out_ref[...] = acc[pl.ds((i - steps) * piece, piece)].astype(BF16)

    return pl.pallas_call(
        kernel,
        grid_spec=pltpu.PrefetchScalarGridSpec(
            num_scalar_prefetch=2,
            grid=(steps + slots // piece,),
            in_specs=[
                pl.BlockSpec(
                    (step, side, side), lambda i, *_: (jnp.minimum(i, steps - 1), 0, 0)
                ),
                pl.BlockSpec(gnum.shape, lambda i, *_: (0, 0, 0)),
            ],
            out_specs=pl.BlockSpec(
                (piece, side, width), lambda i, *_: (jnp.maximum(i - steps, 0), 0, 0)
            ),
            scratch_shapes=[pltpu.VMEM((slots, side, width), F32)],
        ),
        out_shape=jax.ShapeDtypeStruct((slots, side, width), BF16),
        compiler_params=BIG,
        name="slot_gradients",
    )(dst_ids, src_ids, tiles, gnum)


def first_gradients(returned, wanted, own, pre, parts_t):
    slots, side, width = returned.shape
    rows = own.shape[0]
    blocks = rows // side
    features = parts_t.shape[0]
    step = group_of(slots, 16)
    steps = slots // step

    def kernel(want_s, ret_ref, own_ref, pre_ref, parts_ref, gw_ref, gb_ref, acc):
        i = pl.program_id(0)

        @pl.when(i == 0)
        def _():
            acc[...] = jnp.zeros_like(acc)

        for s in range(step):
            acc[want_s[i * step + s]] += ret_ref[s].astype(F32)

        @pl.when(i == steps - 1)
        def _():
            grad = acc[...].reshape(rows, width) + own_ref[...]
            grad_pre = jnp.where(pre_ref[...] > 0.0, grad, 0.0).astype(BF16)
            gb = jnp.sum(grad_pre.astype(F32), axis=0, keepdims=True)
            gb_ref[...] = jnp.broadcast_to(gb, gb_ref.shape)
            gw_ref[...] = jnp.dot(parts_ref[...], grad_pre, preferred_element_type=F32)

    def whole(*shape):
        return pl.BlockSpec(shape, lambda i, *_: (0,) * len(shape))

    return pl.pallas_call(
        kernel,
        grid_spec=pltpu.PrefetchScalarGridSpec(
            num_scalar_prefetch=1,
            grid=(steps,),
            in_specs=[
                pl.BlockSpec((step, side, width), lambda i, *_: (i, 0, 0)),
                whole(rows, width),
                whole(rows, width),
                whole(*parts_t.shape),
            ],
            out_specs=[whole(features, width), whole(8, width)],
            scratch_shapes=[pltpu.VMEM((blocks, side, width), F32)],
        ),
        out_shape=[
            jax.ShapeDtypeStruct((features, width), F32),
            jax.ShapeDtypeStruct((8, width), F32),
        ],
        compiler_params=BIG,
        name="first_gradients",
    )(wanted, returned, own, pre, parts_t)


def doubling_sum(value, axis):
    size = lax.axis_size(axis)
    reach = 1
    while reach < size:
        value = value + lax.ppermute(value, axis, [(k, k ^ reach) for k in range(size)])
        reach *= 2
    return value


def on_device(
    inputs_t, tiles_first, first_dst, first_src, w1_self, w1_neigh, bias_first, fetch_ids,
    tiles_out, out_dst, out_src, output_self_weight, output_neighbour_weight, bias_out, labels,
):
    every = ("dom", "feat")
    n_feat = lax.axis_size("feat")
    devices = lax.axis_size("dom") * n_feat
    side = tiles_out.shape[1]
    rows_dev = labels.shape[0]
    blocks = rows_dev // side
    slots_peer = fetch_ids.shape[2]
    features, width = w1_self.shape
    classes = output_self_weight.shape[1]
    scale = 1.0 / math.sqrt(devices * rows_dev)

    weights = lax.all_gather(jnp.concatenate([w1_neigh, w1_self]), "feat", axis=0, tiled=True)
    parts = first_layer(inputs_t, tiles_first, first_dst, first_src, n_feat * blocks, n_feat)
    parts = lax.all_to_all(parts, "feat", split_axis=0, concat_axis=0, tiled=True)
    parts_t = parts.reshape(n_feat * 2 * features, rows_dev)
    pre, hidden = hidden_layer(parts_t, weights, bias_first.reshape(1, width))
    wanted = fetch_ids[:, 0, :]
    outgoing = hidden.reshape(blocks, side, width)[wanted]
    pool = lax.all_to_all(outgoing, every, split_axis=0, concat_axis=0, tiled=True)
    pool = pool.reshape(devices * slots_peer, side, width)
    weight = row_weights(tiles_out, out_dst, blocks)
    gws, gwn, gb3, gnum, own = output_layer(
        tiles_out, out_dst, out_src, pool, weight, hidden, output_self_weight,
        output_neighbour_weight, bias_out, labels, scale,
    )
    part = jnp.concatenate([gws, gwn], axis=0)
    part = part.reshape(devices, 2 * width // devices, classes)
    part = lax.all_to_all(part, every, split_axis=0, concat_axis=0, tiled=True)
    both = lax.all_gather(jnp.sum(part, axis=0), every, axis=0, tiled=True)
    slot_grad = slot_gradients(tiles_out, out_dst, out_src, gnum, devices * slots_peer)
    slot_grad = slot_grad.reshape(devices, slots_peer, side, width)
    returned = lax.all_to_all(slot_grad, every, split_axis=0, concat_axis=0, tiled=True)
    gw1, gb1 = first_gradients(
        returned.reshape(devices * slots_peer, side, width), wanted.reshape(-1), own, pre, parts_t
    )
    row = jnp.zeros((1, width), F32).at[:, :classes].set(gb3)
    small = jnp.concatenate([gb1[:1], row, jnp.zeros((6, width), F32)])
    small = jnp.broadcast_to(small, (n_feat, 8, width))
    last = jnp.concatenate([gw1.reshape(n_feat, 2 * features, width), small], axis=1)
    last = lax.all_to_all(last, "feat", split_axis=0, concat_axis=0, tiled=True)
    last = doubling_sum(jnp.sum(last, axis=0), "dom")
    edge = 2 * features
    return (
        last[features:edge],
        last[:features],
        last[edge],
        both[:width],
        both[width:],
        last[edge + 1, :classes],
    )


def solution(mesh):
    in_specs = (
        P("feat", "dom"),
        P("dom", None, None),
        P("dom"),
        P("dom"),
        P("feat", None),
        P("feat", None),
        P(),
        P(None, ("dom", "feat"), None),
        P(("dom", "feat"), None, None),
        P(("dom", "feat")),
        P(("dom", "feat")),
        P(),
        P(),
        P(),
        P(("dom", "feat")),
    )
    out_specs = (P("feat", None), P("feat", None), P(), P(), P(), P())
    return jax.shard_map(
        on_device, mesh=mesh, in_specs=in_specs, out_specs=out_specs, check_vma=False
    )
```

time: 853 us -> 348 us (0.41)
  other arithmetic: 213 us -> 5.39 us
  waiting for transfers between devices: 389 us -> 196 us
  matrix products: 93 us -> 0 us
  local copies, waits for them, and re-layouts: 87.6 us -> 11.9 us
  Pallas kernels: 0 us -> 59.9 us
  starting transfers between devices: 10.5 us -> 26.6 us
  between operations: 14.3 us -> 0.8 us
    scatter-add x9 -> x0, other arithmetic: 194 us -> none  [the longest x3 115 us: add_group(): return (summed.at[src_part].add(product), None)]
    psum x2 -> x0, waiting for transfers between devices: 163 us -> none  [the longest x1 90.1 us: on_device(): lax.psum((partial_output_self_weight, partial_output_neighbour_weight, pa...]
    dot_general x18 -> x0, matrix products: 93 us -> none  [the longest x3 38.3 us: add_group(): jnp.einsum('tji,tjw->tiw', tile_part, grad_blocks[dst_part], preferred_el...]
    pallas_call x0 -> x6, Pallas kernels: none -> 59.9 us  [the longest x1 18.4 us: output_layer(): pl.pallas_call(kernel, grid_spec=pltpu.PrefetchScalarGridSpec(num_scalar_...]
    all_gather x0 -> x2, blocking collectives: none -> 45.6 us  [the longest x1 39.2 us: on_device(): both = lax.all_gather(jnp.sum(part, axis=0), every, axis=0, tiled=True)]
    gather x8 -> x1, local copies, waits for them, and re-layouts: 49.2 us -> 3.74 us  [on_device(): outgoing = hidden.reshape(blocks, side, width)[wanted]]
    psum x1 -> x0, blocking collectives: 39.4 us -> none  [on_device(): lax.psum((partial_output_self_weight, partial_output_neighbour_weight, pa...]
    reduce_scatter x1 -> x0, waiting for transfers between devices: 34 us -> none  [on_device(): lax.psum_scatter(lax.dot_general(agg_t, w1_neigh, contract, preferred_ele...]
  transfers between devices with their start and end apart: 6 -> 8, of which waited for: 6 -> 5; matrix products, arithmetic and copies ran while one was open for 2% -> 2% of each run, Pallas kernels for 0% -> 3%
where the time goes in v1:
time: 348 us; the launch traced here: 346 us
  waiting for transfers between devices  196 us (56%)
  Pallas kernels  59.9 us (17%)
  blocking collectives  45.6 us (13%)
  starting transfers between devices  26.6 us (8%)
  local copies, waits for them, and re-layouts  11.9 us (3%)
  other arithmetic  5.39 us (2%)
    all_to_all x1, waiting for transfers between devices, on_device(): lax.all_to_all(slot_grad, every, split_axis=0, concat_axis=0, tiled=True)  92.2 us
    all_to_all x1, waiting for transfers between devices, on_device(): lax.all_to_all(outgoing, every, split_axis=0, concat_axis=0, tiled=True)  80.8 us
    all_gather x1, blocking collectives, on_device(): both = lax.all_gather(jnp.sum(part, axis=0), every, axis=0, tiled=True)  39.2 us
    pallas_call x1, Pallas kernels, output_layer(): pl.pallas_call(kernel, grid_spec=pltpu.PrefetchScalarGridSpec(num_scalar_...  18.4 us
    pallas_call x1, Pallas kernels, slot_gradients(): pl.pallas_call(kernel, grid_spec=pltpu.PrefetchScalarGridSpec(num_scalar_...  18.2 us
    all_to_all x1, waiting for transfers between devices, on_device(): part = lax.all_to_all(part, every, split_axis=0, concat_axis=0, tiled=True)  13.7 us
    pallas_call x1, Pallas kernels, row_weights(): pl.pallas_call(kernel, grid_spec=pltpu.PrefetchScalarGridSpec(num_scalar_...  11.1 us
  transfers between devices with their start and end apart: 8, of which 5 were waited for; matrix products, arithmetic and copies ran while one was open for 2% of the time, Pallas kernels for 3%

profile of v1, /device:TPU:0, one launch (start us, length us, event | category | flops | bytes accessed | tf_op | source)
XLA Modules:
  0.0 346.2 jit_solution(15298616052872682817)
XLA Ops:
  0.6 4.6 %first_layer.1 = bf16[4,64,512]{2,1,0:T(8,128)(2,1)} custom-call(s32[64]{0:T(128)} %dst_s.4, s32[64]{0:T(128)} %src_s.3, bf16[64,128,128]{2,1,0:T(8,128)(2,1)} %tile_ref.4, bf16[32,4096]{1,0:T(8,128)(2,1)} %feat_ref.1), custom_call_target="tpu_custom_call" | custom-call | tf_op jit(solution)/shard_map/first_layer/pallas_call | solution.py:65
  5.3 4.2 %all-to-all-start = ((bf16[4,64,512]{2,1,0:T(8,128)(2,1)}), bf16[4,64,512]{2,1,0:T(8,128)(2,1)S(1)}, u32[]{:S(2)}, u32[]{:S(2)}) async-start(bf16[4,64,512]{2,1,0:T(8,128)(2,1)} %first_layer.1), calls=%async_computation | async-start | bytes 524288 | tf_op jit(solution)/shard_map/all_to_all | solution.py:400
  9.5 0.7 compare_select_fusion
  10.2 0.7 pad_maximum_fusion.2
  10.9 0.1 copy.31
  11.0 0.1 reshape.110
  11.1 6.4 %all_gather.6.w_ref = bf16[256,256]{1,0:T(8,128)(2,1)} all-gather(bf16[64,256]{1,0:T(8,128)(2,1)S(1)} %pad_maximum_fusion.2), channel_id=1, replica_groups=mesh['dom'=8,'feat'=4] {'feat'}, dimensions={0}, use_global_device_ids=true | all-gather | bytes 163840 | tf_op jit(solution)/shard_map/all_gather | solution.py:398
  17.5 0.0 all-to-all-done
  17.5 0.7 copy-done
  18.2 2.2 hidden_layer.1
  20.5 3.7 %gather_fusion = bf16[64,128,256]{2,1,0:T(8,128)(2,1)} fusion(bf16[4,128,256]{2,1,0:T(8,128)(2,1)} %bitcast.19, s32[1024]{0:T(1024)S(1)} %pad_clamp_fusion), kind=kCustom, calls=%fused_computation | custom fusion | bytes 8388864 | tf_op jit(solution)/shard_map/gather | solution.py:404
  24.2 6.5 %all-to-all-start.1 = ((bf16[32,2,128,256]{3,2,1,0:T(8,128)(2,1)}), bf16[32,2,128,256]{3,2,1,0:T(8,128)(2,1)}, u32[]{:S(2)}, u32[]{:S(2)}) async-start(bf16[32,2,128,256]{3,2,1,0:T(8,128)(2,1)} %bitcast.21), calls=%async_computation.1 | async-start | bytes 8388608 | tf_op jit(solution)/shard_map/all_to_all | solution.py:405
  30.8 0.9 copy.34.labels_ref
  31.7 0.8 copy.32.ws_ref
  32.4 0.8 copy.33.wn_ref
  33.2 11.1 %row_weights.1.weight_ref = f32[4,128,128]{2,1,0:T(8,128)} custom-call(s32[384]{0:T(512)} %dst_s.7, bf16[384,128,128]{2,1,0:T(8,128)(2,1)} %tile_ref.7), custom_call_target="tpu_custom_call" | custom-call | flops 12582912 | bytes 12582912 | tf_op jit(solution)/shard_map/row_weights/pallas_call | solution.py:138
  44.3 80.8 %all-to-all-done.1 = bf16[32,2,128,256]{3,2,1,0:T(8,128)(2,1)} async-done(((bf16[32,2,128,256]{3,2,1,0:T(8,128)(2,1)}), bf16[32,2,128,256]{3,2,1,0:T(8,128)(2,1)}, u32[]{:S(2)}, u32[]{:S(2)}) %all-to-all-start.1) | async-done | bytes 4194336 | tf_op jit(solution)/shard_map/all_to_all | solution.py:405
  125.1 18.4 %output_layer.1 = (f32[256,172]{1,0:T(8,128)}, f32[256,172]{1,0:T(8,128)}, f32[1,172]{1,0:T(1,128)}, bf16[4,128,256]{2,1,0:T(8,128)(2,1)}, f32[512,256]{1,0:T(8,128)}) custom-call(s32[384]{0:T(512)} %dst_s.7, s32[384]{0:T(512)} %src_s.5, bf16[384,128,128]{2,1,0:T(8,128)(2,1)} %tile_ref.7, bf16[64,128,256]{2,1,0:T(8,128)(2,1)} %bitcast.5.pool_ref, ...), custom_call_target="tpu_custom_call" | custom-call | tf_op jit(solution)/shard_map/output_layer/pallas_call | solution.py:236
  143.5 18.2 %slot_gradients.1 = bf16[64,128,256]{2,1,0:T(8,128)(2,1)} custom-call(s32[384]{0:T(512)} %dst_s.7, s32[384]{0:T(512)} %src_s.5, bf16[384,128,128]{2,1,0:T(8,128)(2,1)} %tile_ref.7, bf16[4,128,256]{2,1,0:T(8,128)(2,1)} %get-tuple-element.28.gnum_ref), custom_call_target="tpu_custom_call" | custom-call | tf_op jit(solution)/shard_map/slot_gradients/pallas_call | solution.py:300
  161.7 5.4 %all-to-all-start.2 = ((bf16[32,2,128,256]{3,2,1,0:T(8,128)(2,1)}), bf16[32,2,128,256]{3,2,1,0:T(8,128)(2,1)}, u32[]{:S(2)}, u32[]{:S(2)}) async-start(bf16[32,2,128,256]{3,2,1,0:T(8,128)(2,1)} %bitcast.20), calls=%async_computation.2 | async-start | bytes 8388608 | tf_op jit(solution)/shard_map/all_to_all | solution.py:418
  167.1 0.1 copy.30
  167.2 0.6 reshape_squeeze.3.want_s
  167.8 0.1 pad.9.clone
  167.9 0.6 compare_reduce_fusion
  168.5 0.6 broadcast_select_fusion
  169.2 92.2 %all-to-all-done.2 = bf16[32,2,128,256]{3,2,1,0:T(8,128)(2,1)} async-done(((bf16[32,2,128,256]{3,2,1,0:T(8,128)(2,1)}), bf16[32,2,128,256]{3,2,1,0:T(8,128)(2,1)}, u32[]{:S(2)}, u32[]{:S(2)}) %all-to-all-start.2) | async-done | bytes 4194336 | tf_op jit(solution)/shard_map/all_to_all | solution.py:418
  261.4 5.3 %first_gradients.1 = (f32[256,256]{1,0:T(8,128)}, f32[8,256]{1,0:T(8,128)}) custom-call(s32[64]{0:T(128)} %reshape_squeeze.3.want_s, bf16[64,128,256]{2,1,0:T(8,128)(2,1)} %bitcast.9.ret_ref, f32[512,256]{1,0:T(8,128)} %get-tuple-element.29.own_ref, f32[512,256]{1,0:T(8,128)} %get-tuple-element.30.pre_ref, bf16[256,512]{1,0:T(8,128)(2,1)} %bitcast.23), custom_call_target="tpu_custom_call" | custom-call | tf_op jit(solution)/shard_map/first_gradients/pallas_call | solution.py:351
  266.8 0.7 slice.37
  267.5 0.1 fusion
  267.6 1.7 pad_maximum_fusion.1
  269.2 3.5 all-to-all-start.3
  272.7 0.8 pad_maximum_fusion
  273.5 5.5 %all-to-all-done.3 = f32[4,72,256]{2,1,0:T(8,128)S(1)} async-done(((f32[4,72,256]{2,1,0:T(8,128)}), f32[4,72,256]{2,1,0:T(8,128)S(1)}, u32[]{:S(2)}, u32[]{:S(2)}) %all-to-all-start.3) | async-done | bytes 294944 | tf_op jit(solution)/shard_map/all_to_all | solution.py:426
  279.0 3.7 %all-to-all-start.4 = ((f32[32,16,172]{2,1,0:T(8,128)}), f32[32,16,172]{2,1,0:T(8,128)S(1)}, u32[]{:S(2)}, u32[]{:S(2)}) async-start(f32[32,16,172]{2,1,0:T(8,128)} %bitcast.12), calls=%async_computation.4 | async-start | bytes 1048576 | tf_op jit(solution)/shard_map/all_to_all | solution.py:414
  282.8 1.8 collective-permute-start
  284.6 13.7 %all-to-all-done.4 = f32[32,16,172]{2,1,0:T(8,128)S(1)} async-done(((f32[32,16,172]{2,1,0:T(8,128)}), f32[32,16,172]{2,1,0:T(8,128)S(1)}, u32[]{:S(2)}, u32[]{:S(2)}) %all-to-all-start.4) | async-done | bytes 352288 | tf_op jit(solution)/shard_map/all_to_all | solution.py:414
  298.3 0.1 reduce_sum.19
  298.4 0.0 collective-permute-done
  298.4 1.3 collective-permute-start.1
  299.7 39.2 %all_gather.7 = f32[512,172]{1,0:T(8,128)S(1)} all-gather(f32[16,172]{1,0:T(8,128)S(1)} %reduce_sum.19), channel_id=1, replica_groups=mesh['dom'=8,'feat'=4] {'dom','feat'}, dimensions={0}, use_global_device_ids=true | all-gather | bytes 363264 | tf_op jit(solution)/shard_map/all_gather | solution.py:415
  338.9 0.0 collective-permute-done.1
  338.9 0.1 collective-permute-start.2
  339.1 0.8 copy.35
  339.8 0.8 copy.36
  340.6 3.8 %collective-permute-done.2 = f32[72,256]{1,0:T(8,128)S(1)} collective-permute-done((f32[72,256]{1,0:T(8,128)S(1)}, f32[72,256]{1,0:T(8,128)S(1)}, u32[]{:S(2)}, u32[]{:S(2)}) %collective-permute-start.2) | collective-permute-done | bytes 73760 | tf_op jit(solution)/shard_map/ppermute | solution.py:378
  344.4 0.6 fusion.3
  345.1 0.6 slice.48
  345.6 0.6 slice.51
  (23 shorter events, 0.1 us)
Async XLA Ops:
  5.3 12.3 %all-to-all-start = ((bf16[4,64,512]{2,1,0:T(8,128)(2,1)}), bf16[4,64,512]{2,1,0:T(8,128)(2,1)S(1)}, u32[]{:S(2)}, u32[]{:S(2)}) async-start(bf16[4,64,512]{2,1,0:T(8,128)(2,1)} %first_layer.1), calls=%async_computation | async-start | bytes 524288 | tf_op jit(solution)/shard_map/all_to_all | solution.py:400
  17.5 0.7 copy-start
  24.2 6.6 %copy-start.6 = (s32[512]{0:T(512)S(1)}, s32[512]{0:T(512)}, u32[]{:S(2)}) copy-start(s32[512]{0:T(512)} %param.31) | copy-start | bytes 6148
  24.2 7.4 %copy-start.3 = (bf16[256,172]{0,1:T(8,128)(2,1)S(1)}, bf16[256,172]{0,1:T(8,128)(2,1)}, u32[]{:S(2)}) copy-start(bf16[256,172]{0,1:T(8,128)(2,1)} %param.28) | copy-start | bytes 264196
  24.2 8.2 %copy-start.4 = (bf16[256,172]{0,1:T(8,128)(2,1)S(1)}, bf16[256,172]{0,1:T(8,128)(2,1)}, u32[]{:S(2)}) copy-start(bf16[256,172]{0,1:T(8,128)(2,1)} %param.29) | copy-start | bytes 264196
  24.2 100.9 %all-to-all-start.1 = ((bf16[32,2,128,256]{3,2,1,0:T(8,128)(2,1)}), bf16[32,2,128,256]{3,2,1,0:T(8,128)(2,1)}, u32[]{:S(2)}, u32[]{:S(2)}) async-start(bf16[32,2,128,256]{3,2,1,0:T(8,128)(2,1)} %bitcast.21), calls=%async_computation.1 | async-start | bytes 8388608 | tf_op jit(solution)/shard_map/all_to_all | solution.py:405
  161.7 5.4 %copy-start.5 = (s32[32,1,2]{0,2,1:T(2,128)S(1)}, s32[32,1,2]{0,2,1:T(2,128)}, u32[]{:S(2)}) copy-start(s32[32,1,2]{0,2,1:T(2,128)} %param.24) | copy-start | bytes 772
  161.7 6.9 %copy-start.7 = (f32[1,172]{1,0:T(1,128)S(1)}, f32[1,172]{1,0:T(1,128)}, u32[]{:S(2)}) copy-start(f32[1,172]{1,0:T(1,128)} %get-tuple-element.33) | copy-start | bytes 2068
  161.7 99.8 %all-to-all-start.2 = ((bf16[32,2,128,256]{3,2,1,0:T(8,128)(2,1)}), bf16[32,2,128,256]{3,2,1,0:T(8,128)(2,1)}, u32[]{:S(2)}, u32[]{:S(2)}) async-start(bf16[32,2,128,256]{3,2,1,0:T(8,128)(2,1)} %bitcast.20), calls=%async_computation.2 | async-start | bytes 8388608 | tf_op jit(solution)/shard_map/all_to_all | solution.py:418
  167.1 105.6 %copy-start.1 = (f32[256,172]{1,0:T(8,128)S(1)}, f32[256,172]{1,0:T(8,128)}, u32[]{:S(2)}) copy-start(f32[256,172]{1,0:T(8,128)} %get-tuple-element.34) | copy-start | bytes 528388
  167.1 105.6 %copy-start.2 = (f32[256,172]{1,0:T(8,128)S(1)}, f32[256,172]{1,0:T(8,128)}, u32[]{:S(2)}) copy-start(f32[256,172]{1,0:T(8,128)} %get-tuple-element.35) | copy-start | bytes 528388
  269.2 9.8 %all-to-all-start.3 = ((f32[4,72,256]{2,1,0:T(8,128)}), f32[4,72,256]{2,1,0:T(8,128)S(1)}, u32[]{:S(2)}, u32[]{:S(2)}) async-start(f32[4,72,256]{2,1,0:T(8,128)} %pad_maximum_fusion.1), calls=%async_computation.3 | async-start | bytes 589824 | tf_op jit(solution)/shard_map/all_to_all | solution.py:426
  279.0 19.3 %all-to-all-start.4 = ((f32[32,16,172]{2,1,0:T(8,128)}), f32[32,16,172]{2,1,0:T(8,128)S(1)}, u32[]{:S(2)}, u32[]{:S(2)}) async-start(f32[32,16,172]{2,1,0:T(8,128)} %bitcast.12), calls=%async_computation.4 | async-start | bytes 1048576 | tf_op jit(solution)/shard_map/all_to_all | solution.py:414
  282.8 15.6 %collective-permute-start = (f32[72,256]{1,0:T(8,128)S(1)}, f32[72,256]{1,0:T(8,128)S(1)}, u32[]{:S(2)}, u32[]{:S(2)}) collective-permute-start(f32[72,256]{1,0:T(8,128)S(1)} %reduce_sum.18), channel_id=1, source_target_pairs={{0,4},{4,0},{8,12},{12,8},{16,20},{20,16},{24,28},{28,24},{1,5},{5... | collective-permute-start | bytes 221192 | tf_op jit(solution)/shard_map/ppermute | solution.py:378
  298.4 40.5 %collective-permute-start.1 = (f32[72,256]{1,0:T(8,128)S(1)}, f32[72,256]{1,0:T(8,128)S(1)}, u32[]{:S(2)}, u32[]{:S(2)}) collective-permute-start(f32[72,256]{1,0:T(8,128)S(1)} %add.28), channel_id=1, source_target_pairs={{0,8},{4,12},{8,0},{12,4},{16,24},{20,28},{24,16},{28,20},{1,9},{5... | collective-permute-start | bytes 221192 | tf_op jit(solution)/shard_map/ppermute | solution.py:378
  338.9 5.5 %collective-permute-start.2 = (f32[72,256]{1,0:T(8,128)S(1)}, f32[72,256]{1,0:T(8,128)S(1)}, u32[]{:S(2)}, u32[]{:S(2)}) collective-permute-start(f32[72,256]{1,0:T(8,128)S(1)} %add.29), channel_id=1, source_target_pairs={{0,16},{4,20},{8,24},{12,28},{16,0},{20,4},{24,8},{28,12},{1,17},{... | collective-permute-start | bytes 221192 | tf_op jit(solution)/shard_map/ppermute | solution.py:378

commit v2 on v1

--- a/solution.py
+++ b/solution.py
@@ -17,7 +17,7 @@
     return math.gcd(count, most)
 
 
-def first_layer(features_t, tiles, dst_ids, src_ids, blocks, owners):
+def first_layer(features_t, tiles, dst_ids, src_ids, me, blocks, owners):
     width, nodes = features_t.shape
     total, side, _ = tiles.shape
     step = group_of(total, 32)
@@ -25,7 +25,8 @@
     steps = total // step
     per_owner = blocks // owners
 
-    def kernel(dst_s, src_s, tile_ref, feat_ref, out_ref, acc):
+    def kernel(dst_s, src_s, me_s, tile_ref, feat_ref, *refs):
+        outs, acc = refs[:-1], refs[-1]
         i = pl.program_id(0)
 
         @pl.when(i == 0)
@@ -53,50 +54,54 @@
 
         @pl.when(i == steps - 1)
         def _():
-            for q in range(owners):
+            rows = per_owner * side
+            for r in range(owners):
+                q = me_s[0] ^ r
                 for b in range(per_owner):
                     block = acc[q * per_owner + b]
                     mean = block[:width] / block[width : width + 1]
-                    out_ref[q, :width, b * side : (b + 1) * side] = mean.astype(BF16)
-                rows = per_owner * side
-                out_ref[q, width:, :] = feat_ref[:, q * rows : (q + 1) * rows]
-
-    shape = (owners, 2 * width, per_owner * side)
+                    outs[r][:width, b * side : (b + 1) * side] = mean.astype(BF16)
+                outs[r][width:, :] = feat_ref[:, pl.ds(pl.multiple_of(q * rows, side), rows)]
+
+    shape = (2 * width, per_owner * side)
     return pl.pallas_call(
         kernel,
         grid_spec=pltpu.PrefetchScalarGridSpec(
-            num_scalar_prefetch=2,
+            num_scalar_prefetch=3,
             grid=(steps,),
             in_specs=[
                 pl.BlockSpec((step, side, side), lambda i, *_: (i, 0, 0)),
                 pl.BlockSpec((width, nodes), lambda i, *_: (0, 0)),
             ],
-            out_specs=pl.BlockSpec(shape, lambda i, *_: (0, 0, 0)),
+            out_specs=[pl.BlockSpec(shape, lambda i, *_: (0, 0))] * owners,
             scratch_shapes=[pltpu.VMEM((blocks, width + 16, side), F32)],
         ),
-        out_shape=jax.ShapeDtypeStruct(shape, BF16),
+        out_shape=[jax.ShapeDtypeStruct(shape, BF16)] * owners,
         compiler_params=BIG,
         name="first_layer",
-    )(dst_ids, src_ids, tiles, features_t)
-
-
-def hidden_layer(parts_t, weights, bias):
-    rows = parts_t.shape[1]
-    width = weights.shape[1]
-
-    def kernel(parts_ref, w_ref, b_ref, pre_ref, hidden_ref):
-        pre = (
-            lax.dot_general(
-                parts_ref[...], w_ref[...], (((0,), (0,)), ((), ())), preferred_element_type=F32
+    )(dst_ids, src_ids, me, tiles, features_t)
+
+
+def hidden_layer(parts, weights, bias):
+    count = len(parts)
+    rows = parts[0].shape[1]
+    width = weights[0].shape[1]
+
+    def kernel(*refs):
+        b_ref, pre_ref, hidden_ref = refs[2 * count :]
+        pre = jnp.zeros((rows, width), F32)
+        for r in range(count):
+            pre = pre + lax.dot_general(
+                refs[r][...], refs[count + r][...], (((0,), (0,)), ((), ())),
+                preferred_element_type=F32,
             )
-            + b_ref[...]
-        )
+        pre = pre + b_ref[...]
         pre_ref[...] = pre
         hidden_ref[...] = jnp.maximum(pre, 0.0).astype(BF16)
 
     return pl.pallas_call(
         kernel,
-        in_specs=[VMEM] * 3,
+        in_specs=[VMEM] * (2 * count + 1),
         out_specs=[VMEM] * 2,
         out_shape=[
             jax.ShapeDtypeStruct((rows, width), F32),
@@ -104,7 +109,7 @@
         ],
         compiler_params=BIG,
         name="hidden_layer",
-    )(parts_t, weights, bias)
+    )(*parts, *weights, bias)
 
 
 def row_weights(tiles, dst_ids, blocks):
@@ -154,11 +159,17 @@
 
 
 def output_layer(
-    tiles, dst_ids, src_ids, pool, weight, hidden, w_self, w_neigh, bias, labels, scale
+    tiles, dst_ids, src_ids, place, me, pools, weight, hidden, w_self, w_neigh, bias, labels,
+    scale, n_feat,
 ):
     total, side, _ = tiles.shape
     blocks = weight.shape[0]
-    width = pool.shape[2]
+    width = hidden.shape[1]
+    count = len(pools)
+    per_pool = pools[0].shape[0]
+    unit = 8 * n_feat
+    share = -(-(2 * width + 8) // unit) * 8
+    half = n_feat // 2
     classes = w_self.shape[1]
     step = group_of(total, 32)
     unroll = group_of(step, 32)
@@ -167,21 +178,38 @@
     last = (((1,), (1,)), ((), ()))
 
     def kernel(
-        dst_s, src_s, tile_ref, pool_ref, weight_ref, hidden_ref, ws_ref, wn_ref, bias_ref,
-        labels_ref, gws_ref, gwn_ref, gb_ref, gnum_ref, own_ref, acc,
+        dst_s, src_s, place_s, me_s, tile_ref, weight_ref, hidden_ref, ws_ref, wn_ref, bias_ref,
+        labels_ref, *refs,
     ):
+        pool_refs = refs[:count]
+        even_ref, odd_ref, gnum_ref, own_ref, acc, pool_ref, sums, sems = refs[count:]
         i = pl.program_id(0)
 
         @pl.when(i == 0)
         def _():
+            copies = [
+                pltpu.make_async_copy(
+                    pool_refs[j], pool_ref.at[pl.ds(j * per_pool, per_pool)], sems.at[j]
+                )
+                for j in range(count)
+            ]
+            for copy in copies:
+                copy.start()
             acc[...] = jnp.zeros_like(acc)
+            sums[...] = jnp.zeros_like(sums)
+            for copy in copies:
+                copy.wait()
 
         def body(g, carry):
             products = []
             for u in range(unroll):
                 t = g * unroll + u
                 products.append(
-                    jnp.dot(tile_ref[t], pool_ref[src_s[i * step + t]], preferred_element_type=F32)
+                    jnp.dot(
+                        tile_ref[t],
+                        pool_ref[place_s[src_s[i * step + t]]],
+                        preferred_element_type=F32,
+                    )
                 )
             for u in range(unroll):
                 acc[dst_s[i * step + g * unroll + u]] += products[u]
@@ -218,45 +246,53 @@
                 own_ref[rows, :] = lax.dot_general(
                     glog, ws_ref[...], last, preferred_element_type=F32
                 )
-            gws_ref[...] = gws
-            gwn_ref[...] = gwn
-            gb_ref[...] = gb
+            sums[:width, :] = gws
+            sums[width : 2 * width, :] = gwn
+            sums[2 * width : 2 * width + 8, :] = jnp.broadcast_to(gb, (8, classes))
+            for r in range(n_feat):
+                start = pl.multiple_of((me_s[0] ^ r) * share, 8)
+                target = odd_ref if r % 2 else even_ref
+                target[r // 2] = sums[pl.ds(start, share), :]
 
     def whole(*shape):
         return pl.BlockSpec(shape, lambda i, *_: (0,) * len(shape))
 
     rows = blocks * side
     out = [
-        ((width, classes), F32),
-        ((width, classes), F32),
-        ((1, classes), F32),
+        ((half, share, classes), F32),
+        ((half, share, classes), F32),
         ((blocks, side, width), BF16),
         ((rows, width), F32),
     ]
     return pl.pallas_call(
         kernel,
         grid_spec=pltpu.PrefetchScalarGridSpec(
-            num_scalar_prefetch=2,
+            num_scalar_prefetch=4,
             grid=(steps,),
             in_specs=[
                 pl.BlockSpec((step, side, side), lambda i, *_: (i, 0, 0)),
-                pl.BlockSpec(memory_space=pltpu.VMEM),
                 whole(blocks, side, side),
                 whole(rows, width),
                 whole(width, classes),
                 whole(width, classes),
                 whole(1, classes),
                 whole(rows, 1),
+            ]
+            + [pl.BlockSpec(memory_space=pl.ANY)] * count,
+            out_specs=[whole(*s) for s, _ in out],
+            scratch_shapes=[
+                pltpu.VMEM((blocks, side, width), F32),
+                pltpu.VMEM((count * per_pool, side, width), BF16),
+                pltpu.VMEM((n_feat * share, classes), F32),
+                pltpu.SemaphoreType.DMA((count,)),
             ],
-            out_specs=[whole(*s) for s, _ in out],
-            scratch_shapes=[pltpu.VMEM((blocks, side, width), F32)],
         ),
         out_shape=[jax.ShapeDtypeStruct(s, d) for s, d in out],
         compiler_params=BIG,
         name="output_layer",
     )(
-        dst_ids, src_ids, tiles, pool, weight, hidden, w_self, w_neigh,
-        bias.reshape(1, classes), labels.reshape(rows, 1),
+        dst_ids, src_ids, place, me, tiles, weight, hidden, w_self, w_neigh,
+        bias.reshape(1, classes), labels.reshape(rows, 1), *pools,
     )
 
 
@@ -319,15 +355,17 @@
     )(dst_ids, src_ids, tiles, gnum)
 
 
-def first_gradients(returned, wanted, own, pre, parts_t):
+def first_gradients(returned, wanted, own, pre, parts):
     slots, side, width = returned.shape
     rows = own.shape[0]
     blocks = rows // side
-    features = parts_t.shape[0]
+    count = len(parts)
+    features = parts[0].shape[0]
     step = group_of(slots, 16)
     steps = slots // step
 
-    def kernel(want_s, ret_ref, own_ref, pre_ref, parts_ref, gw_ref, gb_ref, acc):
+    def kernel(want_s, ret_ref, own_ref, pre_ref, *refs):
+        even_ref, odd_ref, acc = refs[count:]
         i = pl.program_id(0)
 
         @pl.when(i == 0)
@@ -342,12 +380,17 @@
             grad = acc[...].reshape(rows, width) + own_ref[...]
             grad_pre = jnp.where(pre_ref[...] > 0.0, grad, 0.0).astype(BF16)
             gb = jnp.sum(grad_pre.astype(F32), axis=0, keepdims=True)
-            gb_ref[...] = jnp.broadcast_to(gb, gb_ref.shape)
-            gw_ref[...] = jnp.dot(parts_ref[...], grad_pre, preferred_element_type=F32)
+            for r in range(count):
+                target = odd_ref if r % 2 else even_ref
+                target[r // 2, :features] = jnp.dot(
+                    refs[r][...], grad_pre, preferred_element_type=F32
+                )
+                target[r // 2, features:] = jnp.broadcast_to(gb, (8, width))
 
     def whole(*shape):
         return pl.BlockSpec(shape, lambda i, *_: (0,) * len(shape))
 
+    shape = (count // 2, features + 8, width)
     return pl.pallas_call(
         kernel,
         grid_spec=pltpu.PrefetchScalarGridSpec(
@@ -357,25 +400,55 @@
                 pl.BlockSpec((step, side, width), lambda i, *_: (i, 0, 0)),
                 whole(rows, width),
                 whole(rows, width),
-                whole(*parts_t.shape),
-            ],
-            out_specs=[whole(features, width), whole(8, width)],
+            ]
+            + [whole(features, rows)] * count,
+            out_specs=[whole(*shape)] * 2,
             scratch_shapes=[pltpu.VMEM((blocks, side, width), F32)],
         ),
-        out_shape=[
-            jax.ShapeDtypeStruct((features, width), F32),
-            jax.ShapeDtypeStruct((8, width), F32),
-        ],
+        out_shape=[jax.ShapeDtypeStruct(shape, F32)] * 2,
         compiler_params=BIG,
         name="first_gradients",
-    )(wanted, returned, own, pre, parts_t)
+    )(wanted, returned, own, pre, *parts)
+
+
+def swap(value, axis, mask):
+    return lax.ppermute(value, axis, [(k, k ^ mask) for k in range(lax.axis_size(axis))])
+
+
+def feat_sum(even, odd):
+    value = even + swap(odd, "feat", 1)
+    mask = 2
+    while value.shape[0] > 1:
+        value = value[0::2] + swap(value[1::2], "feat", mask)
+        mask *= 2
+    return value[0]
+
+
+def gather_blocks(value, planes, across):
+    n_dom = lax.axis_size("dom")
+    down = lax.axis_size("feat") // 2
+    held = []
+    shifted = [value] + [swap(value, "dom", across * k) for k in range(1, planes)]
+    for k, own in enumerate(shifted):
+        aside = [own] + [swap(own, "dom", i) for i in range(1, across)]
+        below = [own] + [swap(own, "feat", 2 * j) for j in range(1, down)]
+        pieces = list(aside)
+        for j in range(1, down):
+            pieces.append(below[j])
+            for i in range(1, across):
+                if k % 2 == 0:
+                    pieces.append(swap(aside[i], "feat", 2 * j))
+                else:
+                    pieces.append(swap(below[j], "dom", i))
+        held.append(jnp.concatenate(pieces))
+    return held + [swap(piece, "feat", 1) for piece in held]
 
 
 def doubling_sum(value, axis):
     size = lax.axis_size(axis)
     reach = 1
     while reach < size:
-        value = value + lax.ppermute(value, axis, [(k, k ^ reach) for k in range(size)])
+        value = value + swap(value, axis, reach)
         reach *= 2
     return value
 
@@ -395,44 +468,51 @@
     classes = output_self_weight.shape[1]
     scale = 1.0 / math.sqrt(devices * rows_dev)
 
-    weights = lax.all_gather(jnp.concatenate([w1_neigh, w1_self]), "feat", axis=0, tiled=True)
-    parts = first_layer(inputs_t, tiles_first, first_dst, first_src, n_feat * blocks, n_feat)
-    parts = lax.all_to_all(parts, "feat", split_axis=0, concat_axis=0, tiled=True)
-    parts_t = parts.reshape(n_feat * 2 * features, rows_dev)
-    pre, hidden = hidden_layer(parts_t, weights, bias_first.reshape(1, width))
+    me_dom, me_feat = lax.axis_index("dom"), lax.axis_index("feat")
+    me = me_feat.astype(jnp.int32).reshape(1)
+    planes = math.gcd(lax.axis_size("dom"), 4)
+    across = lax.axis_size("dom") // planes
+
+    weights = jnp.concatenate([w1_neigh, w1_self])
+    weights = [weights] + [swap(weights, "feat", r) for r in range(1, n_feat)]
+    parts = first_layer(inputs_t, tiles_first, first_dst, first_src, me, n_feat * blocks, n_feat)
+    parts = [parts[0]] + [swap(parts[r], "feat", r) for r in range(1, n_feat)]
+    pre, hidden = hidden_layer(parts, weights, bias_first.reshape(1, width))
     wanted = fetch_ids[:, 0, :]
-    outgoing = hidden.reshape(blocks, side, width)[wanted]
-    pool = lax.all_to_all(outgoing, every, split_axis=0, concat_axis=0, tiled=True)
-    pool = pool.reshape(devices * slots_peer, side, width)
+    pools = gather_blocks(hidden, planes, across)
+    pools = [pool.reshape(-1, side, width) for pool in pools]
+    owner = jnp.arange(devices, dtype=jnp.int32)[:, None]
+    off_dom = (owner // n_feat) ^ me_dom
+    off_feat = (owner % n_feat) ^ me_feat
+    place = (off_feat % 2) * planes + off_dom // across
+    place = (place * (n_feat // 2) + off_feat // 2) * across + off_dom % across
+    lists = lax.all_gather(wanted.reshape(1, -1), every, axis=0, tiled=True)
+    index = (me_dom * n_feat + me_feat) * slots_peer
+    mine = lax.dynamic_slice_in_dim(lists, index, slots_peer, axis=1)
+    place = (place * blocks + mine).reshape(-1)
     weight = row_weights(tiles_out, out_dst, blocks)
-    gws, gwn, gb3, gnum, own = output_layer(
-        tiles_out, out_dst, out_src, pool, weight, hidden, output_self_weight,
-        output_neighbour_weight, bias_out, labels, scale,
+    even, odd, gnum, own = output_layer(
+        tiles_out, out_dst, out_src, place, me, pools, weight, hidden, output_self_weight,
+        output_neighbour_weight, bias_out, labels, scale, n_feat,
     )
-    part = jnp.concatenate([gws, gwn], axis=0)
-    part = part.reshape(devices, 2 * width // devices, classes)
-    part = lax.all_to_all(part, every, split_axis=0, concat_axis=0, tiled=True)
-    both = lax.all_gather(jnp.sum(part, axis=0), every, axis=0, tiled=True)
+    third = doubling_sum(feat_sum(even, odd), "dom")
+    third = jnp.stack([third] + [swap(third, "feat", r) for r in range(1, n_feat)])
+    third = jnp.take(third, jnp.arange(n_feat) ^ me_feat, axis=0).reshape(-1, classes)
     slot_grad = slot_gradients(tiles_out, out_dst, out_src, gnum, devices * slots_peer)
     slot_grad = slot_grad.reshape(devices, slots_peer, side, width)
     returned = lax.all_to_all(slot_grad, every, split_axis=0, concat_axis=0, tiled=True)
-    gw1, gb1 = first_gradients(
-        returned.reshape(devices * slots_peer, side, width), wanted.reshape(-1), own, pre, parts_t
+    even, odd = first_gradients(
+        returned.reshape(devices * slots_peer, side, width), wanted.reshape(-1), own, pre, parts
     )
-    row = jnp.zeros((1, width), F32).at[:, :classes].set(gb3)
-    small = jnp.concatenate([gb1[:1], row, jnp.zeros((6, width), F32)])
-    small = jnp.broadcast_to(small, (n_feat, 8, width))
-    last = jnp.concatenate([gw1.reshape(n_feat, 2 * features, width), small], axis=1)
-    last = lax.all_to_all(last, "feat", split_axis=0, concat_axis=0, tiled=True)
-    last = doubling_sum(jnp.sum(last, axis=0), "dom")
+    last = doubling_sum(feat_sum(even, odd), "dom")
     edge = 2 * features
     return (
         last[features:edge],
         last[:features],
         last[edge],
-        both[:width],
-        both[width:],
-        last[edge + 1, :classes],
+        third[:width],
+        third[width : 2 * width],
+        third[2 * width],
     )
 
 

time: 348 us -> 297 us (0.85)
  waiting for transfers between devices: 196 us -> 134 us
  starting transfers between devices: 26.6 us -> 41.1 us
  other arithmetic: 5.39 us -> 1.23 us
  blocking collectives: 45.6 us -> 41.9 us
    ppermute x3 -> x38, waiting for transfers between devices: 3.79 us -> 113 us  [swap(): lax.ppermute(value, axis, [(k, k ^ mask) for k in range(lax.axis_size(axi...]
    all_to_all x4 -> x0, waiting for transfers between devices: 100 us -> none  [the longest x1 80.8 us: on_device(): lax.all_to_all(outgoing, every, split_axis=0, concat_axis=0, tiled=True)]
    all_to_all x1, waiting for transfers between devices: 92.2 us -> 22 us  [on_device(): lax.all_to_all(slot_grad, every, split_axis=0, concat_axis=0, tiled=True)]
    ppermute x3 -> x38, starting transfers between devices: 3.23 us -> 37.3 us  [swap(): lax.ppermute(value, axis, [(k, k ^ mask) for k in range(lax.axis_size(axi...]
    all_to_all x4 -> x0, starting transfers between devices: 18 us -> none  [the longest x1 6.53 us: on_device(): lax.all_to_all(outgoing, every, split_axis=0, concat_axis=0, tiled=True)]
    all_gather x2 -> x1, blocking collectives: 45.6 us -> 41.9 us  [on_device(): lists = lax.all_gather(wanted.reshape(1, -1), every, axis=0, tiled=True)]
  transfers between devices with their start and end apart: 8 -> 39, of which waited for: 5 -> 21; matrix products, arithmetic and copies ran while one was open for 2% -> 4% of each run, Pallas kernels for 3% -> 6%
where the time goes in v2:
time: 297 us; the launch traced here: 296 us
  waiting for transfers between devices  134 us (45%)
  Pallas kernels  62.3 us (21%)
  blocking collectives  41.9 us (14%)
  starting transfers between devices  41.1 us (14%)
  local copies, waits for them, and re-layouts  13.9 us (5%)
    ppermute x38, waiting for transfers between devices, swap(): lax.ppermute(value, axis, [(k, k ^ mask) for k in range(lax.axis_size(axi...  113 us
    all_gather x1, blocking collectives, on_device(): lists = lax.all_gather(wanted.reshape(1, -1), every, axis=0, tiled=True)  41.9 us
    ppermute x38, starting transfers between devices, swap(): lax.ppermute(value, axis, [(k, k ^ mask) for k in range(lax.axis_size(axi...  37.3 us
    all_to_all x1, waiting for transfers between devices, on_device(): lax.all_to_all(slot_grad, every, split_axis=0, concat_axis=0, tiled=True)  22 us
    pallas_call x1, Pallas kernels, output_layer(): pl.pallas_call(kernel, grid_spec=pltpu.PrefetchScalarGridSpec(num_scalar_...  20.6 us
    pallas_call x1, Pallas kernels, slot_gradients(): pl.pallas_call(kernel, grid_spec=pltpu.PrefetchScalarGridSpec(num_scalar_...  18.2 us
    pallas_call x1, Pallas kernels, row_weights(): pl.pallas_call(kernel, grid_spec=pltpu.PrefetchScalarGridSpec(num_scalar_...  11.1 us
    unnamed x49, local copies, waits for them, and re-layouts  6.48 us
  transfers between devices with their start and end apart: 39, of which 21 were waited for; matrix products, arithmetic and copies ran while one was open for 4% of the time, Pallas kernels for 6%

profile of v2, /device:TPU:0, one launch (start us, length us, event | category | flops | bytes accessed | tf_op | source)
XLA Modules:
  0.0 296.0 jit_solution(9676289512823793567)
XLA Ops:
  0.6 4.7 %first_layer.1 = (bf16[64,512]{1,0:T(8,128)(2,1)}, bf16[64,512]{1,0:T(8,128)(2,1)}, bf16[64,512]{1,0:T(8,128)(2,1)}, bf16[64,512]{1,0:T(8,128)(2,1)}) custom-call(s32[64]{0:T(128)} %dst_s.5, s32[64]{0:T(128)} %src_s.3, s32[1]{0:T(128)} %bitcast.1.me_s, bf16[64,128,128]{2,1,0:T(8,128)(2,1)} %tile_ref.5, bf16[32,4096]{1,0:T(8,128)(2,1)} %feat_ref.1), custom_call_target="tpu_custom_call" | custom-call | tf_op jit(solution)/shard_map/first_layer/pallas_call | solution.py:67
  7.2 3.0 %collective-permute-start.1 = (bf16[64,512]{1,0:T(8,128)(2,1)}, bf16[64,512]{1,0:T(8,128)(2,1)S(1)}, u32[]{:S(2)}, u32[]{:S(2)}) collective-permute-start(bf16[64,512]{1,0:T(8,128)(2,1)} %get-tuple-element.20), channel_id=1, source_target_pairs={{0,2},{1,3},{2,0},{3,1},{4,6},{5,7},{6,4},{7,5},{8,10},{9,11},{10,... | collective-permute-start | bytes 196616 | tf_op jit(solution)/shard_map/ppermute | solution.py:415
  10.2 1.4 collective-permute-start.4
  12.0 3.3 %collective-permute-done.4.refs_6_ = bf16[64,256]{1,0:T(8,128)(2,1)S(1)} collective-permute-done((bf16[64,256]{1,0:T(8,128)(2,1)S(1)}, bf16[64,256]{1,0:T(8,128)(2,1)S(1)}, u32[]{:S(2)}, u32[]{:S(2)}) %collective-permute-start.4) | collective-permute-done | bytes 32800 | tf_op jit(solution)/shard_map/ppermute | solution.py:415
  16.8 2.4 hidden_layer.1
  19.2 1.6 collective-permute-start.9
  20.8 1.5 collective-permute-start.6
  22.3 2.6 collective-permute-start.13
  24.9 1.7 constant_dynamic-update-slice_fusion.5
  26.6 1.0 collective-permute-start.7
  27.8 4.0 %collective-permute-done.9 = bf16[512,256]{1,0:T(8,128)(2,1)S(1)} collective-permute-done((bf16[512,256]{1,0:T(8,128)(2,1)}, bf16[512,256]{1,0:T(8,128)(2,1)S(1)}, u32[]{:S(2)}, u32[]{:S(2)}) %collective-permute-start.9) | collective-permute-done | bytes 262176 | tf_op jit(solution)/shard_map/ppermute | solution.py:415
  31.8 2.1 collective-permute-start.10
  33.9 1.2 collective-permute-start.8
  35.8 8.0 %collective-permute-done.13 = bf16[512,256]{1,0:T(8,128)(2,1)S(1)} collective-permute-done((bf16[512,256]{1,0:T(8,128)(2,1)}, bf16[512,256]{1,0:T(8,128)(2,1)S(1)}, u32[]{:S(2)}, u32[]{:S(2)}) %collective-permute-start.13) | collective-permute-done | bytes 262176 | tf_op jit(solution)/shard_map/ppermute | solution.py:415
  43.9 0.9 collective-permute-start.11
  45.5 1.1 collective-permute-start.15
  47.4 1.5 collective-permute-start.18
  49.6 0.9 collective-permute-start.19
  50.6 1.9 collective-permute-done.11
  52.5 0.9 collective-permute-start.12
  54.2 1.0 collective-permute-start.16
  55.2 4.5 %collective-permute-done.19 = bf16[512,256]{1,0:T(8,128)(2,1)S(1)} collective-permute-done((bf16[512,256]{1,0:T(8,128)(2,1)S(1)}, bf16[512,256]{1,0:T(8,128)(2,1)S(1)}, u32[]{:S(2)}, u32[]{:S(2)}) %collective-permute-start.19) | collective-permute-done | bytes 262176 | tf_op jit(solution)/shard_map/ppermute | solution.py:415
  59.7 1.1 collective-permute-start.20
  61.7 1.9 collective-permute-done.16
  63.8 3.1 %collective-permute-done.20 = bf16[512,256]{1,0:T(8,128)(2,1)S(1)} collective-permute-done((bf16[512,256]{1,0:T(8,128)(2,1)S(1)}, bf16[512,256]{1,0:T(8,128)(2,1)S(1)}, u32[]{:S(2)}, u32[]{:S(2)}) %collective-permute-start.20) | collective-permute-done | bytes 262176 | tf_op jit(solution)/shard_map/ppermute | solution.py:415
  67.2 41.9 %all-gather = s32[32,1,64]{2,1,0:T(1,128)S(1)} all-gather(s32[1,1,64]{2,1,0:T(1,128)S(1)} %reshape.273), channel_id=1, replica_groups=mesh['dom'=8,'feat'=4] {'dom','feat'}, dimensions={0}, use_global_device_ids=true | all-gather | bytes 8448 | tf_op jit(solution)/shard_map/all_gather | solution.py:489
  111.6 0.8 copy.42.labels_ref
  112.4 11.1 %row_weights.1.weight_ref = f32[4,128,128]{2,1,0:T(8,128)} custom-call(s32[384]{0:T(512)} %dst_s.7, bf16[384,128,128]{2,1,0:T(8,128)(2,1)} %tile_ref.7), custom_call_target="tpu_custom_call" | custom-call | flops 12582912 | bytes 12582912 | tf_op jit(solution)/shard_map/row_weights/pallas_call | solution.py:143
  123.6 20.6 %output_layer.1 = (f32[2,136,172]{2,1,0:T(8,128)}, f32[2,136,172]{2,1,0:T(8,128)}, bf16[4,128,256]{2,1,0:T(8,128)(2,1)}, f32[512,256]{1,0:T(8,128)}) custom-call(s32[384]{0:T(512)} %dst_s.7, s32[384]{0:T(512)} %src_s.5, s32[64]{0:T(128)} %reshape.250.place_s, s32[1]{0:T(128)} %bitcast.1.me_s, bf16[384,128,128]{2,1,0:T(8,128)(2,1)} %tile_ref.7, ...), custom_call_target="tpu_custom_call" | custom-call | tf_op jit(solution)/shard_map/output_layer/pallas_call | solution.py:267
  144.2 18.2 %slot_gradients.1 = bf16[64,128,256]{2,1,0:T(8,128)(2,1)} custom-call(s32[384]{0:T(512)} %dst_s.7, s32[384]{0:T(512)} %src_s.5, bf16[384,128,128]{2,1,0:T(8,128)(2,1)} %tile_ref.7, bf16[4,128,256]{2,1,0:T(8,128)(2,1)} %get-tuple-element.23.gnum_ref), custom_call_target="tpu_custom_call" | custom-call | tf_op jit(solution)/shard_map/slot_gradients/pallas_call | solution.py:336
  162.4 3.7 %all-to-all-start = ((bf16[32,2,128,256]{3,2,1,0:T(8,128)(2,1)}), bf16[32,2,128,256]{3,2,1,0:T(8,128)(2,1)}, u32[]{:S(2)}, u32[]{:S(2)}) async-start(bf16[32,2,128,256]{3,2,1,0:T(8,128)(2,1)} %bitcast.32), calls=%async_computation | async-start | bytes 8388608 | tf_op jit(solution)/shard_map/all_to_all | solution.py:503
  166.2 1.5 collective-permute-done.30
  167.8 1.6 collective-permute-start.31
  169.4 26.8 %collective-permute-done.31 = f32[1,136,172]{2,1,0:T(8,128)S(1)} collective-permute-done((f32[1,136,172]{2,1,0:T(8,128)S(1)}, f32[1,136,172]{2,1,0:T(8,128)S(1)}, u32[]{:S(2)}, u32[]{:S(2)}) %collective-permute-start.31) | collective-permute-done | bytes 93600 | tf_op jit(solution)/shard_map/ppermute | solution.py:415
  196.3 3.2 %collective-permute-start.32 = (f32[136,172]{1,0:T(8,128)S(1)}, f32[136,172]{1,0:T(8,128)S(1)}, u32[]{:S(2)}, u32[]{:S(2)}) collective-permute-start(f32[136,172]{1,0:T(8,128)S(1)} %fusion), channel_id=1, source_target_pairs={{0,4},{4,0},{8,12},{12,8},{16,20},{20,16},{24,28},{28,24},{1,5},{5... | collective-permute-start | bytes 280712 | tf_op jit(solution)/shard_map/ppermute | solution.py:415
  200.0 7.2 %collective-permute-done.32 = f32[136,172]{1,0:T(8,128)S(1)} collective-permute-done((f32[136,172]{1,0:T(8,128)S(1)}, f32[136,172]{1,0:T(8,128)S(1)}, u32[]{:S(2)}, u32[]{:S(2)}) %collective-permute-start.32) | collective-permute-done | bytes 93600 | tf_op jit(solution)/shard_map/ppermute | solution.py:415
  207.3 31.1 %collective-permute-done.33 = f32[136,172]{1,0:T(8,128)S(1)} collective-permute-done((f32[136,172]{1,0:T(8,128)S(1)}, f32[136,172]{1,0:T(8,128)S(1)}, u32[]{:S(2)}, u32[]{:S(2)}) %collective-permute-start.33) | collective-permute-done | bytes 93600 | tf_op jit(solution)/shard_map/ppermute | solution.py:415
  238.5 3.7 %collective-permute-start.34 = (f32[136,172]{1,0:T(8,128)S(1)}, f32[136,172]{1,0:T(8,128)S(1)}, u32[]{:S(2)}, u32[]{:S(2)}) collective-permute-start(f32[136,172]{1,0:T(8,128)S(1)} %add.149), channel_id=1, source_target_pairs={{0,16},{4,20},{8,24},{12,28},{16,0},{20,4},{24,8},{28,12},{1,17},{... | collective-permute-start | bytes 280712 | tf_op jit(solution)/shard_map/ppermute | solution.py:415
  242.2 22.0 %all-to-all-done = bf16[32,2,128,256]{3,2,1,0:T(8,128)(2,1)} async-done(((bf16[32,2,128,256]{3,2,1,0:T(8,128)(2,1)}), bf16[32,2,128,256]{3,2,1,0:T(8,128)(2,1)}, u32[]{:S(2)}, u32[]{:S(2)}) %all-to-all-start) | async-done | bytes 4194336 | tf_op jit(solution)/shard_map/all_to_all | solution.py:503
  264.1 5.4 %first_gradients.1 = (f32[2,72,256]{2,1,0:T(8,128)}, f32[2,72,256]{2,1,0:T(8,128)}) custom-call(s32[64]{0:T(128)} %reshape_squeeze.6.want_s, bf16[64,128,256]{2,1,0:T(8,128)(2,1)} %bitcast.14.ret_ref, f32[512,256]{1,0:T(8,128)} %get-tuple-element.24.own_ref, f32[512,256]{1,0:T(8,128)} %get-tuple-element.25.pre_ref, ...), custom_call_target="tpu_custom_call" | custom-call | tf_op jit(solution)/shard_map/first_gradients/pallas_call | solution.py:394
  270.5 1.5 collective-permute-start.36
  271.9 0.9 add.140
  273.5 1.6 collective-permute-done.37
  275.1 4.3 %collective-permute-done.36 = f32[136,172]{1,0:T(8,128)S(1)} collective-permute-done((f32[136,172]{1,0:T(8,128)S(1)}, f32[136,172]{1,0:T(8,128)S(1)}, u32[]{:S(2)}, u32[]{:S(2)}) %collective-permute-start.36) | collective-permute-done | bytes 93600 | tf_op jit(solution)/shard_map/ppermute | solution.py:415
  280.3 1.3 collective-permute-start.27
  281.7 3.1 %collective-permute-done.27 = f32[72,256]{1,0:T(8,128)S(1)} collective-permute-done((f32[72,256]{1,0:T(8,128)S(1)}, f32[72,256]{1,0:T(8,128)S(1)}, u32[]{:S(2)}, u32[]{:S(2)}) %collective-permute-start.27) | collective-permute-done | bytes 73760 | tf_op jit(solution)/shard_map/ppermute | solution.py:415
  285.6 3.6 %collective-permute-done.28 = f32[72,256]{1,0:T(8,128)S(1)} collective-permute-done((f32[72,256]{1,0:T(8,128)S(1)}, f32[72,256]{1,0:T(8,128)S(1)}, u32[]{:S(2)}, u32[]{:S(2)}) %collective-permute-start.28) | collective-permute-done | bytes 73760 | tf_op jit(solution)/shard_map/ppermute | solution.py:415
  290.4 4.3 %collective-permute-done.29 = f32[72,256]{1,0:T(8,128)S(1)} collective-permute-done((f32[72,256]{1,0:T(8,128)S(1)}, f32[72,256]{1,0:T(8,128)S(1)}, u32[]{:S(2)}, u32[]{:S(2)}) %collective-permute-start.29) | collective-permute-done | bytes 73760 | tf_op jit(solution)/shard_map/ppermute | solution.py:415
  (124 shorter events, 18.3 us)
Async XLA Ops:
  5.3 10.8 %collective-permute-start = (bf16[64,512]{1,0:T(8,128)(2,1)}, bf16[64,512]{1,0:T(8,128)(2,1)S(1)}, u32[]{:S(2)}, u32[]{:S(2)}) collective-permute-start(bf16[64,512]{1,0:T(8,128)(2,1)} %get-tuple-element.19), channel_id=1, source_target_pairs={{0,1},{1,0},{2,3},{3,2},{4,5},{5,4},{6,7},{7,6},{8,9},{9,8},{10,11... | collective-permute-start | bytes 196616 | tf_op jit(solution)/shard_map/ppermute | solution.py:415
  7.2 9.0 %copy-start.9 = (bf16[64,256]{1,0:T(8,128)(2,1)}, bf16[64,256]{1,0:T(8,128)(2,1)S(1)}, u32[]{:S(2)}) copy-start(bf16[64,256]{1,0:T(8,128)(2,1)S(1)} %constant_dynamic-update-slice_fusion.refs_4_) | copy-start | bytes 98308
  7.2 4.4 %collective-permute-start.3 = (bf16[64,256]{1,0:T(8,128)(2,1)S(1)}, bf16[64,256]{1,0:T(8,128)(2,1)S(1)}, u32[]{:S(2)}, u32[]{:S(2)}) collective-permute-start(bf16[64,256]{1,0:T(8,128)(2,1)S(1)} %constant_dynamic-update-slice_fusion.refs_4_), channel_id=1, source_target_pairs={{0,1},{1,0},{2,3},{3,2},{4,5},{5,4},{6,7},{7,6},{8,9},{9,8},{10,11... | collective-permute-start | bytes 98312 | tf_op jit(solution)/shard_map/ppermute | solution.py:415
  7.2 8.9 %collective-permute-start.1 = (bf16[64,512]{1,0:T(8,128)(2,1)}, bf16[64,512]{1,0:T(8,128)(2,1)S(1)}, u32[]{:S(2)}, u32[]{:S(2)}) collective-permute-start(bf16[64,512]{1,0:T(8,128)(2,1)} %get-tuple-element.20), channel_id=1, source_target_pairs={{0,2},{1,3},{2,0},{3,1},{4,6},{5,7},{6,4},{7,5},{8,10},{9,11},{10,... | collective-permute-start | bytes 196616 | tf_op jit(solution)/shard_map/ppermute | solution.py:415
  10.2 5.9 %collective-permute-start.2 = (bf16[64,512]{1,0:T(8,128)(2,1)}, bf16[64,512]{1,0:T(8,128)(2,1)S(1)}, u32[]{:S(2)}, u32[]{:S(2)}) collective-permute-start(bf16[64,512]{1,0:T(8,128)(2,1)} %get-tuple-element.21), channel_id=1, source_target_pairs={{0,3},{1,2},{2,1},{3,0},{4,7},{5,6},{6,5},{7,4},{8,11},{9,10},{10,... | collective-permute-start | bytes 196616 | tf_op jit(solution)/shard_map/ppermute | solution.py:415
  10.2 5.1 %collective-permute-start.4 = (bf16[64,256]{1,0:T(8,128)(2,1)S(1)}, bf16[64,256]{1,0:T(8,128)(2,1)S(1)}, u32[]{:S(2)}, u32[]{:S(2)}) collective-permute-start(bf16[64,256]{1,0:T(8,128)(2,1)S(1)} %constant_dynamic-update-slice_fusion.refs_4_), channel_id=1, source_target_pairs={{0,2},{1,3},{2,0},{3,1},{4,6},{5,7},{6,4},{7,5},{8,10},{9,11},{10,... | collective-permute-start | bytes 98312 | tf_op jit(solution)/shard_map/ppermute | solution.py:415
  11.6 4.6 %collective-permute-start.5 = (bf16[64,256]{1,0:T(8,128)(2,1)S(1)}, bf16[64,256]{1,0:T(8,128)(2,1)S(1)}, u32[]{:S(2)}, u32[]{:S(2)}) collective-permute-start(bf16[64,256]{1,0:T(8,128)(2,1)S(1)} %constant_dynamic-update-slice_fusion.refs_4_), channel_id=1, source_target_pairs={{0,3},{1,2},{2,1},{3,0},{4,7},{5,6},{6,5},{7,4},{8,11},{9,10},{10,... | collective-permute-start | bytes 98312 | tf_op jit(solution)/shard_map/ppermute | solution.py:415
  19.2 47.8 %copy-start.14 = (s32[32,1,2]{0,2,1:T(2,128)S(1)}, s32[32,1,2]{0,2,1:T(2,128)}, u32[]{:S(2)}) copy-start(s32[32,1,2]{0,2,1:T(2,128)} %param.22) | copy-start | bytes 772
  19.2 90.9 %copy-start.7 = (bf16[256,172]{0,1:T(8,128)(2,1)S(1)}, bf16[256,172]{0,1:T(8,128)(2,1)}, u32[]{:S(2)}) copy-start(bf16[256,172]{0,1:T(8,128)(2,1)} %param.26) | copy-start | bytes 264196
  19.2 12.7 %collective-permute-start.9 = (bf16[512,256]{1,0:T(8,128)(2,1)}, bf16[512,256]{1,0:T(8,128)(2,1)S(1)}, u32[]{:S(2)}, u32[]{:S(2)}) collective-permute-start(bf16[512,256]{1,0:T(8,128)(2,1)} %get-tuple-element.22.hidden_ref), channel_id=1, source_target_pairs={{0,8},{4,12},{8,0},{12,4},{16,24},{20,28},{24,16},{28,20},{1,9},{5... | collective-permute-start | bytes 786440 | tf_op jit(solution)/shard_map/ppermute | solution.py:415
  20.8 13.1 %collective-permute-start.6 = (bf16[512,256]{1,0:T(8,128)(2,1)}, bf16[512,256]{1,0:T(8,128)(2,1)S(1)}, u32[]{:S(2)}, u32[]{:S(2)}) collective-permute-start(bf16[512,256]{1,0:T(8,128)(2,1)} %get-tuple-element.22.hidden_ref), channel_id=1, source_target_pairs={{0,4},{4,0},{8,12},{12,8},{16,20},{20,16},{24,28},{28,24},{1,5},{5... | collective-permute-start | bytes 786440 | tf_op jit(solution)/shard_map/ppermute | solution.py:415
  22.3 21.6 %collective-permute-start.13 = (bf16[512,256]{1,0:T(8,128)(2,1)}, bf16[512,256]{1,0:T(8,128)(2,1)S(1)}, u32[]{:S(2)}, u32[]{:S(2)}) collective-permute-start(bf16[512,256]{1,0:T(8,128)(2,1)} %get-tuple-element.22.hidden_ref), channel_id=1, source_target_pairs={{0,16},{4,20},{8,24},{12,28},{16,0},{20,4},{24,8},{28,12},{1,17},{... | collective-permute-start | bytes 786440 | tf_op jit(solution)/shard_map/ppermute | solution.py:415
  26.6 84.2 %copy-start.8 = (bf16[256,172]{0,1:T(8,128)(2,1)S(1)}, bf16[256,172]{0,1:T(8,128)(2,1)}, u32[]{:S(2)}) copy-start(bf16[256,172]{0,1:T(8,128)(2,1)} %param.27) | copy-start | bytes 264196
  26.6 85.0 %copy-start.13 = (s32[512]{0:T(512)S(1)}, s32[512]{0:T(512)}, u32[]{:S(2)}) copy-start(s32[512]{0:T(512)} %param.29) | copy-start | bytes 6148
  26.6 18.9 %collective-permute-start.7 = (bf16[512,256]{1,0:T(8,128)(2,1)}, bf16[512,256]{1,0:T(8,128)(2,1)S(1)}, u32[]{:S(2)}, u32[]{:S(2)}) collective-permute-start(bf16[512,256]{1,0:T(8,128)(2,1)} %get-tuple-element.22.hidden_ref), channel_id=1, source_target_pairs={{0,2},{1,3},{2,0},{3,1},{4,6},{5,7},{6,4},{7,5},{8,10},{9,11},{10,... | collective-permute-start | bytes 786440 | tf_op jit(solution)/shard_map/ppermute | solution.py:415
  27.6 17.3 %collective-permute-start.17 = (bf16[512,256]{1,0:T(8,128)(2,1)}, bf16[512,256]{1,0:T(8,128)(2,1)S(1)}, u32[]{:S(2)}, u32[]{:S(2)}) collective-permute-start(bf16[512,256]{1,0:T(8,128)(2,1)} %get-tuple-element.22.hidden_ref), channel_id=1, source_target_pairs={{0,24},{4,28},{8,16},{12,20},{16,8},{20,12},{24,0},{28,4},{1,25},{... | collective-permute-start | bytes 786440 | tf_op jit(solution)/shard_map/ppermute | solution.py:415
  31.8 17.7 %collective-permute-start.10 = (bf16[512,256]{1,0:T(8,128)(2,1)S(1)}, bf16[512,256]{1,0:T(8,128)(2,1)S(1)}, u32[]{:S(2)}, u32[]{:S(2)}) collective-permute-start(bf16[512,256]{1,0:T(8,128)(2,1)S(1)} %collective-permute-done.9), channel_id=1, source_target_pairs={{0,4},{4,0},{8,12},{12,8},{16,20},{20,16},{24,28},{28,24},{1,5},{5... | collective-permute-start | bytes 786440 | tf_op jit(solution)/shard_map/ppermute | solution.py:415
  33.9 13.5 %collective-permute-start.8 = (bf16[512,256]{1,0:T(8,128)(2,1)S(1)}, bf16[512,256]{1,0:T(8,128)(2,1)S(1)}, u32[]{:S(2)}, u32[]{:S(2)}) collective-permute-start(bf16[512,256]{1,0:T(8,128)(2,1)S(1)} %collective-permute-done.6), channel_id=1, source_target_pairs={{0,2},{1,3},{2,0},{3,1},{4,6},{5,7},{6,4},{7,5},{8,10},{9,11},{10,... | collective-permute-start | bytes 786440 | tf_op jit(solution)/shard_map/ppermute | solution.py:415
  43.9 8.6 %collective-permute-start.11 = (bf16[512,256]{1,0:T(8,128)(2,1)S(1)}, bf16[512,256]{1,0:T(8,128)(2,1)S(1)}, u32[]{:S(2)}, u32[]{:S(2)}) collective-permute-start(bf16[512,256]{1,0:T(8,128)(2,1)S(1)} %collective-permute-done.9), channel_id=1, source_target_pairs={{0,2},{1,3},{2,0},{3,1},{4,6},{5,7},{6,4},{7,5},{8,10},{9,11},{10,... | collective-permute-start | bytes 786440 | tf_op jit(solution)/shard_map/ppermute | solution.py:415
  44.8 7.6 %collective-permute-start.14 = (bf16[512,256]{1,0:T(8,128)(2,1)S(1)}, bf16[512,256]{1,0:T(8,128)(2,1)S(1)}, u32[]{:S(2)}, u32[]{:S(2)}) collective-permute-start(bf16[512,256]{1,0:T(8,128)(2,1)S(1)} %collective-permute-done.13), channel_id=1, source_target_pairs={{0,4},{4,0},{8,12},{12,8},{16,20},{20,16},{24,28},{28,24},{1,5},{5... | collective-permute-start | bytes 786440 | tf_op jit(solution)/shard_map/ppermute | solution.py:415
  45.5 15.4 %collective-permute-start.15 = (bf16[512,256]{1,0:T(8,128)(2,1)S(1)}, bf16[512,256]{1,0:T(8,128)(2,1)S(1)}, u32[]{:S(2)}, u32[]{:S(2)}) collective-permute-start(bf16[512,256]{1,0:T(8,128)(2,1)S(1)} %collective-permute-done.13), channel_id=1, source_target_pairs={{0,2},{1,3},{2,0},{3,1},{4,6},{5,7},{6,4},{7,5},{8,10},{9,11},{10,... | collective-permute-start | bytes 786440 | tf_op jit(solution)/shard_map/ppermute | solution.py:415
  47.4 6.8 %collective-permute-start.18 = (bf16[512,256]{1,0:T(8,128)(2,1)S(1)}, bf16[512,256]{1,0:T(8,128)(2,1)S(1)}, u32[]{:S(2)}, u32[]{:S(2)}) collective-permute-start(bf16[512,256]{1,0:T(8,128)(2,1)S(1)} %collective-permute-done.17), channel_id=1, source_target_pairs={{0,4},{4,0},{8,12},{12,8},{16,20},{20,16},{24,28},{28,24},{1,5},{5... | collective-permute-start | bytes 786440 | tf_op jit(solution)/shard_map/ppermute | solution.py:415
  49.6 10.1 %collective-permute-start.19 = (bf16[512,256]{1,0:T(8,128)(2,1)S(1)}, bf16[512,256]{1,0:T(8,128)(2,1)S(1)}, u32[]{:S(2)}, u32[]{:S(2)}) collective-permute-start(bf16[512,256]{1,0:T(8,128)(2,1)S(1)} %collective-permute-done.17), channel_id=1, source_target_pairs={{0,2},{1,3},{2,0},{3,1},{4,6},{5,7},{6,4},{7,5},{8,10},{9,11},{10,... | collective-permute-start | bytes 786440 | tf_op jit(solution)/shard_map/ppermute | solution.py:415
  52.4 71.1 %collective-permute-start.21 = (bf16[2048,256]{1,0:T(8,128)(2,1)}, bf16[2048,256]{1,0:T(8,128)(2,1)}, u32[]{:S(2)}, u32[]{:S(2)}) collective-permute-start(bf16[2048,256]{1,0:T(8,128)(2,1)} %constant_dynamic-update-slice_fusion.2), channel_id=1, source_target_pairs={{0,1},{1,0},{2,3},{3,2},{4,5},{5,4},{6,7},{7,6},{8,9},{9,8},{10,11... | collective-permute-start | bytes 3145736 | tf_op jit(solution)/shard_map/ppermute | solution.py:415
  52.5 9.2 %collective-permute-start.12 = (bf16[512,256]{1,0:T(8,128)(2,1)S(1)}, bf16[512,256]{1,0:T(8,128)(2,1)S(1)}, u32[]{:S(2)}, u32[]{:S(2)}) collective-permute-start(bf16[512,256]{1,0:T(8,128)(2,1)S(1)} %collective-permute-done.11), channel_id=1, source_target_pairs={{0,4},{4,0},{8,12},{12,8},{16,20},{20,16},{24,28},{28,24},{1,5},{5... | collective-permute-start | bytes 786440 | tf_op jit(solution)/shard_map/ppermute | solution.py:415
  54.2 9.5 %collective-permute-start.16 = (bf16[512,256]{1,0:T(8,128)(2,1)S(1)}, bf16[512,256]{1,0:T(8,128)(2,1)S(1)}, u32[]{:S(2)}, u32[]{:S(2)}) collective-permute-start(bf16[512,256]{1,0:T(8,128)(2,1)S(1)} %collective-permute-done.14), channel_id=1, source_target_pairs={{0,2},{1,3},{2,0},{3,1},{4,6},{5,7},{6,4},{7,5},{8,10},{9,11},{10,... | collective-permute-start | bytes 786440 | tf_op jit(solution)/shard_map/ppermute | solution.py:415
  59.7 7.1 %collective-permute-start.20 = (bf16[512,256]{1,0:T(8,128)(2,1)S(1)}, bf16[512,256]{1,0:T(8,128)(2,1)S(1)}, u32[]{:S(2)}, u32[]{:S(2)}) collective-permute-start(bf16[512,256]{1,0:T(8,128)(2,1)S(1)} %collective-permute-done.19), channel_id=1, source_target_pairs={{0,4},{4,0},{8,12},{12,8},{16,20},{20,16},{24,28},{28,24},{1,5},{5... | collective-permute-start | bytes 786440 | tf_op jit(solution)/shard_map/ppermute | solution.py:415
  61.7 61.9 %copy-start.1 = (bf16[2048,256]{1,0:T(8,128)(2,1)}, bf16[2048,256]{1,0:T(8,128)(2,1)S(1)}, u32[]{:S(2)}) copy-start(bf16[2048,256]{1,0:T(8,128)(2,1)S(1)} %constant_dynamic-update-slice_fusion.6) | copy-start | bytes 3145732
  61.7 61.9 %collective-permute-start.22 = (bf16[2048,256]{1,0:T(8,128)(2,1)S(1)}, bf16[2048,256]{1,0:T(8,128)(2,1)}, u32[]{:S(2)}, u32[]{:S(2)}) collective-permute-start(bf16[2048,256]{1,0:T(8,128)(2,1)S(1)} %constant_dynamic-update-slice_fusion.6), channel_id=1, source_target_pairs={{0,1},{1,0},{2,3},{3,2},{4,5},{5,4},{6,7},{7,6},{8,9},{9,8},{10,11... | collective-permute-start | bytes 3145736 | tf_op jit(solution)/shard_map/ppermute | solution.py:415
  63.7 59.8 %copy-start.2 = (bf16[2048,256]{1,0:T(8,128)(2,1)}, bf16[2048,256]{1,0:T(8,128)(2,1)S(1)}, u32[]{:S(2)}) copy-start(bf16[2048,256]{1,0:T(8,128)(2,1)S(1)} %constant_dynamic-update-slice_fusion.10) | copy-start | bytes 3145732
  63.7 59.9 %collective-permute-start.23 = (bf16[2048,256]{1,0:T(8,128)(2,1)S(1)}, bf16[2048,256]{1,0:T(8,128)(2,1)}, u32[]{:S(2)}, u32[]{:S(2)}) collective-permute-start(bf16[2048,256]{1,0:T(8,128)(2,1)S(1)} %constant_dynamic-update-slice_fusion.10), channel_id=1, source_target_pairs={{0,1},{1,0},{2,3},{3,2},{4,5},{5,4},{6,7},{7,6},{8,9},{9,8},{10,11... | collective-permute-start | bytes 3145736 | tf_op jit(solution)/shard_map/ppermute | solution.py:415
  66.9 56.6 %copy-start = (bf16[2048,256]{1,0:T(8,128)(2,1)}, bf16[2048,256]{1,0:T(8,128)(2,1)S(1)}, u32[]{:S(2)}) copy-start(bf16[2048,256]{1,0:T(8,128)(2,1)S(1)} %constant_dynamic-update-slice_fusion.14) | copy-start | bytes 3145732
  66.9 56.7 %collective-permute-start.24 = (bf16[2048,256]{1,0:T(8,128)(2,1)S(1)}, bf16[2048,256]{1,0:T(8,128)(2,1)}, u32[]{:S(2)}, u32[]{:S(2)}) collective-permute-start(bf16[2048,256]{1,0:T(8,128)(2,1)S(1)} %constant_dynamic-update-slice_fusion.14), channel_id=1, source_target_pairs={{0,1},{1,0},{2,3},{3,2},{4,5},{5,4},{6,7},{7,6},{8,9},{9,8},{10,11... | collective-permute-start | bytes 3145736 | tf_op jit(solution)/shard_map/ppermute | solution.py:415
  162.4 5.4 %copy-start.3 = (f32[2,136,172]{2,1,0:T(8,128)S(1)}, f32[2,136,172]{2,1,0:T(8,128)}, u32[]{:S(2)}) copy-start(f32[2,136,172]{2,1,0:T(8,128)} %get-tuple-element.28) | copy-start | bytes 561412
  162.4 101.7 %all-to-all-start = ((bf16[32,2,128,256]{3,2,1,0:T(8,128)(2,1)}), bf16[32,2,128,256]{3,2,1,0:T(8,128)(2,1)}, u32[]{:S(2)}, u32[]{:S(2)}) async-start(bf16[32,2,128,256]{3,2,1,0:T(8,128)(2,1)} %bitcast.32), calls=%async_computation | async-start | bytes 8388608 | tf_op jit(solution)/shard_map/all_to_all | solution.py:503
  166.1 1.6 collective-permute-start.30
  167.8 28.4 %collective-permute-start.31 = (f32[1,136,172]{2,1,0:T(8,128)S(1)}, f32[1,136,172]{2,1,0:T(8,128)S(1)}, u32[]{:S(2)}, u32[]{:S(2)}) collective-permute-start(f32[1,136,172]{2,1,0:T(8,128)S(1)} %slice.52), channel_id=1, source_target_pairs={{0,2},{1,3},{2,0},{3,1},{4,6},{5,7},{6,4},{7,5},{8,10},{9,11},{10,... | collective-permute-start | bytes 280712 | tf_op jit(solution)/shard_map/ppermute | solution.py:415
  196.3 11.0 %collective-permute-start.32 = (f32[136,172]{1,0:T(8,128)S(1)}, f32[136,172]{1,0:T(8,128)S(1)}, u32[]{:S(2)}, u32[]{:S(2)}) collective-permute-start(f32[136,172]{1,0:T(8,128)S(1)} %fusion), channel_id=1, source_target_pairs={{0,4},{4,0},{8,12},{12,8},{16,20},{20,16},{24,28},{28,24},{1,5},{5... | collective-permute-start | bytes 280712 | tf_op jit(solution)/shard_map/ppermute | solution.py:415
  207.2 31.2 %collective-permute-start.33 = (f32[136,172]{1,0:T(8,128)S(1)}, f32[136,172]{1,0:T(8,128)S(1)}, u32[]{:S(2)}, u32[]{:S(2)}) collective-permute-start(f32[136,172]{1,0:T(8,128)S(1)} %add.148), channel_id=1, source_target_pairs={{0,8},{4,12},{8,0},{12,4},{16,24},{20,28},{24,16},{28,20},{1,9},{5... | collective-permute-start | bytes 280712 | tf_op jit(solution)/shard_map/ppermute | solution.py:415
  238.5 31.2 %collective-permute-start.34 = (f32[136,172]{1,0:T(8,128)S(1)}, f32[136,172]{1,0:T(8,128)S(1)}, u32[]{:S(2)}, u32[]{:S(2)}) collective-permute-start(f32[136,172]{1,0:T(8,128)S(1)} %add.149), channel_id=1, source_target_pairs={{0,16},{4,20},{8,24},{12,28},{16,0},{20,4},{24,8},{28,12},{1,17},{... | collective-permute-start | bytes 280712 | tf_op jit(solution)/shard_map/ppermute | solution.py:415
  269.5 2.4 collective-permute-start.25
  269.7 5.4 %collective-permute-start.37 = (f32[136,172]{1,0:T(8,128)S(1)}, f32[136,172]{1,0:T(8,128)S(1)}, u32[]{:S(2)}, u32[]{:S(2)}) collective-permute-start(f32[136,172]{1,0:T(8,128)S(1)} %add.150), channel_id=1, source_target_pairs={{0,3},{1,2},{2,1},{3,0},{4,7},{5,6},{6,5},{7,4},{8,11},{9,10},{10,... | collective-permute-start | bytes 280712 | tf_op jit(solution)/shard_map/ppermute | solution.py:415
  270.5 8.9 %collective-permute-start.36 = (f32[136,172]{1,0:T(8,128)S(1)}, f32[136,172]{1,0:T(8,128)S(1)}, u32[]{:S(2)}, u32[]{:S(2)}) collective-permute-start(f32[136,172]{1,0:T(8,128)S(1)} %add.150), channel_id=1, source_target_pairs={{0,2},{1,3},{2,0},{3,1},{4,6},{5,7},{6,4},{7,5},{8,10},{9,11},{10,... | collective-permute-start | bytes 280712 | tf_op jit(solution)/shard_map/ppermute | solution.py:415
  271.9 7.5 %collective-permute-start.35 = (f32[136,172]{1,0:T(8,128)S(1)}, f32[136,172]{1,0:T(8,128)S(1)}, u32[]{:S(2)}, u32[]{:S(2)}) collective-permute-start(f32[136,172]{1,0:T(8,128)S(1)} %add.150), channel_id=1, source_target_pairs={{0,1},{1,0},{2,3},{3,2},{4,5},{5,4},{6,7},{7,6},{8,9},{9,8},{10,11... | collective-permute-start | bytes 280712 | tf_op jit(solution)/shard_map/ppermute | solution.py:415
  272.9 7.4 %collective-permute-start.26 = (f32[1,72,256]{2,1,0:T(8,128)S(1)}, f32[1,72,256]{2,1,0:T(8,128)S(1)}, u32[]{:S(2)}, u32[]{:S(2)}) collective-permute-start(f32[1,72,256]{2,1,0:T(8,128)S(1)} %slice.47), channel_id=1, source_target_pairs={{0,2},{1,3},{2,0},{3,1},{4,6},{5,7},{6,4},{7,5},{8,10},{9,11},{10,... | collective-permute-start | bytes 221192 | tf_op jit(solution)/shard_map/ppermute | solution.py:415
  280.3 4.4 %collective-permute-start.27 = (f32[72,256]{1,0:T(8,128)S(1)}, f32[72,256]{1,0:T(8,128)S(1)}, u32[]{:S(2)}, u32[]{:S(2)}) collective-permute-start(f32[72,256]{1,0:T(8,128)S(1)} %fusion.1), channel_id=1, source_target_pairs={{0,4},{4,0},{8,12},{12,8},{16,20},{20,16},{24,28},{28,24},{1,5},{5... | collective-permute-start | bytes 221192 | tf_op jit(solution)/shard_map/ppermute | solution.py:415
  284.8 4.4 %collective-permute-start.28 = (f32[72,256]{1,0:T(8,128)S(1)}, f32[72,256]{1,0:T(8,128)S(1)}, u32[]{:S(2)}, u32[]{:S(2)}) collective-permute-start(f32[72,256]{1,0:T(8,128)S(1)} %add.142), channel_id=1, source_target_pairs={{0,8},{4,12},{8,0},{12,4},{16,24},{20,28},{24,16},{28,20},{1,9},{5... | collective-permute-start | bytes 221192 | tf_op jit(solution)/shard_map/ppermute | solution.py:415
  289.2 5.5 %collective-permute-start.29 = (f32[72,256]{1,0:T(8,128)S(1)}, f32[72,256]{1,0:T(8,128)S(1)}, u32[]{:S(2)}, u32[]{:S(2)}) collective-permute-start(f32[72,256]{1,0:T(8,128)S(1)} %add.143), channel_id=1, source_target_pairs={{0,16},{4,20},{8,24},{12,28},{16,0},{20,4},{24,8},{28,12},{1,17},{... | collective-permute-start | bytes 221192 | tf_op jit(solution)/shard_map/ppermute | solution.py:415
  (7 other events, 11.7 us)

commit v3 on v2

--- a/solution.py
+++ b/solution.py
@@ -296,119 +296,120 @@
     )
 
 
-def slot_gradients(tiles, dst_ids, src_ids, gnum, slots):
+def slot_gradients(tiles, dst_ids, src_ids, owners, mine, gnum, arrays):
     total, side, _ = tiles.shape
-    width = gnum.shape[2]
+    blocks, _, width = gnum.shape
+    slots = mine.shape[0]
+    devices = owners.shape[0]
+    each = slots // devices
+    plane = devices // arrays
     step = group_of(total, 32)
     unroll = group_of(step, 32)
     steps = total // step
-    piece = group_of(slots, 8)
-
-    def kernel(dst_s, src_s, tile_ref, gnum_ref, out_ref, acc):
+
+    def kernel(dst_s, src_s, owner_s, mine_s, tile_ref, gnum_ref, *refs):
+        outs = refs[:arrays]
+        acc, stage, sems = refs[arrays:]
         i = pl.program_id(0)
 
         @pl.when(i == 0)
         def _():
             acc[...] = jnp.zeros_like(acc)
 
-        @pl.when(i < steps)
-        def _():
-            def body(g, carry):
-                products = []
-                for u in range(unroll):
-                    t = g * unroll + u
-                    products.append(
-                        lax.dot_general(
-                            tile_ref[t], gnum_ref[dst_s[i * step + t]],
-                            (((0,), (0,)), ((), ())), preferred_element_type=F32,
-                        )
+        def body(g, carry):
+            products = []
+            for u in range(unroll):
+                t = g * unroll + u
+                products.append(
+                    lax.dot_general(
+                        tile_ref[t], gnum_ref[dst_s[i * step + t]],
+                        (((0,), (0,)), ((), ())), preferred_element_type=F32,
                     )
-                for u in range(unroll):
-                    acc[src_s[i * step + g * unroll + u]] += products[u]
-                return carry
-
-            lax.fori_loop(0, step // unroll, body, 0)
-
-        @pl.when(i >= steps)
-        def _():
-            out_ref[...] = acc[pl.ds((i - steps) * piece, piece)].astype(BF16)
-
+                )
+            for u in range(unroll):
+                acc[src_s[i * step + g * unroll + u]] += products[u]
+            return carry
+
+        lax.fori_loop(0, step // unroll, body, 0)
+
+        @pl.when(i == steps - 1)
+        def _():
+            copies = [
+                pltpu.make_async_copy(stage.at[a % 2], outs[a], sems.at[a]) for a in range(arrays)
+            ]
+            for a in range(arrays):
+                if a >= 2:
+                    copies[a - 2].wait()
+
+                def place(p, carry, a=a):
+                    first = owner_s[a * plane + p] * each
+                    for b in range(blocks):
+                        stage[a % 2, p * blocks + b] = jnp.zeros((side, width), BF16)
+                    for c in range(each):
+                        target = p * blocks + mine_s[first + c]
+                        stage[a % 2, target] = acc[first + c].astype(BF16)
+                    return carry
+
+                lax.fori_loop(0, plane, place, 0)
+                copies[a].start()
+            for a in range(max(arrays - 2, 0), arrays):
+                copies[a].wait()
+
+    shape = (plane * blocks, side, width)
     return pl.pallas_call(
         kernel,
         grid_spec=pltpu.PrefetchScalarGridSpec(
-            num_scalar_prefetch=2,
-            grid=(steps + slots // piece,),
+            num_scalar_prefetch=4,
+            grid=(steps,),
             in_specs=[
-                pl.BlockSpec(
-                    (step, side, side), lambda i, *_: (jnp.minimum(i, steps - 1), 0, 0)
-                ),
+                pl.BlockSpec((step, side, side), lambda i, *_: (i, 0, 0)),
                 pl.BlockSpec(gnum.shape, lambda i, *_: (0, 0, 0)),
             ],
-            out_specs=pl.BlockSpec(
-                (piece, side, width), lambda i, *_: (jnp.maximum(i - steps, 0), 0, 0)
-            ),
-            scratch_shapes=[pltpu.VMEM((slots, side, width), F32)],
+            out_specs=[pl.BlockSpec(memory_space=pl.ANY)] * arrays,
+            scratch_shapes=[
+                pltpu.VMEM((slots, side, width), F32),
+                pltpu.VMEM((2,) + shape, BF16),
+                pltpu.SemaphoreType.DMA((arrays,)),
+            ],
         ),
-        out_shape=jax.ShapeDtypeStruct((slots, side, width), BF16),
+        out_shape=[jax.ShapeDtypeStruct(shape, BF16)] * arrays,
         compiler_params=BIG,
         name="slot_gradients",
-    )(dst_ids, src_ids, tiles, gnum)
-
-
-def first_gradients(returned, wanted, own, pre, parts):
-    slots, side, width = returned.shape
-    rows = own.shape[0]
-    blocks = rows // side
+    )(dst_ids, src_ids, owners, mine, tiles, gnum)
+
+
+def first_gradients(returned, own, pre, parts):
+    terms = len(returned)
+    rows, width = own.shape
     count = len(parts)
     features = parts[0].shape[0]
-    step = group_of(slots, 16)
-    steps = slots // step
-
-    def kernel(want_s, ret_ref, own_ref, pre_ref, *refs):
-        even_ref, odd_ref, acc = refs[count:]
-        i = pl.program_id(0)
-
-        @pl.when(i == 0)
-        def _():
-            acc[...] = jnp.zeros_like(acc)
-
-        for s in range(step):
-            acc[want_s[i * step + s]] += ret_ref[s].astype(F32)
-
-        @pl.when(i == steps - 1)
-        def _():
-            grad = acc[...].reshape(rows, width) + own_ref[...]
-            grad_pre = jnp.where(pre_ref[...] > 0.0, grad, 0.0).astype(BF16)
-            gb = jnp.sum(grad_pre.astype(F32), axis=0, keepdims=True)
-            for r in range(count):
-                target = odd_ref if r % 2 else even_ref
-                target[r // 2, :features] = jnp.dot(
-                    refs[r][...], grad_pre, preferred_element_type=F32
-                )
-                target[r // 2, features:] = jnp.broadcast_to(gb, (8, width))
-
-    def whole(*shape):
-        return pl.BlockSpec(shape, lambda i, *_: (0,) * len(shape))
+
+    def kernel(*refs):
+        own_ref, pre_ref = refs[terms : terms + 2]
+        part_refs = refs[terms + 2 : terms + 2 + count]
+        even_ref, odd_ref = refs[terms + 2 + count :]
+        grad = refs[0][...].astype(F32)
+        for term in range(1, terms):
+            grad = grad + refs[term][...].astype(F32)
+        grad = grad + own_ref[...]
+        grad_pre = jnp.where(pre_ref[...] > 0.0, grad, 0.0).astype(BF16)
+        gb = jnp.sum(grad_pre.astype(F32), axis=0, keepdims=True)
+        for r in range(count):
+            target = odd_ref if r % 2 else even_ref
+            target[r // 2, :features] = jnp.dot(
+                part_refs[r][...], grad_pre, preferred_element_type=F32
+            )
+            target[r // 2, features:] = jnp.broadcast_to(gb, (8, width))
 
     shape = (count // 2, features + 8, width)
     return pl.pallas_call(
         kernel,
-        grid_spec=pltpu.PrefetchScalarGridSpec(
-            num_scalar_prefetch=1,
-            grid=(steps,),
-            in_specs=[
-                pl.BlockSpec((step, side, width), lambda i, *_: (i, 0, 0)),
-                whole(rows, width),
-                whole(rows, width),
-            ]
-            + [whole(features, rows)] * count,
-            out_specs=[whole(*shape)] * 2,
-            scratch_shapes=[pltpu.VMEM((blocks, side, width), F32)],
-        ),
+        in_specs=[VMEM] * (terms + 2 + count),
+        out_specs=[VMEM] * 2,
         out_shape=[jax.ShapeDtypeStruct(shape, F32)] * 2,
         compiler_params=BIG,
         name="first_gradients",
-    )(wanted, returned, own, pre, *parts)
+    )(*returned, own, pre, *parts)
 
 
 def swap(value, axis, mask):
@@ -424,12 +425,14 @@
     return value[0]
 
 
-def gather_blocks(value, planes, across):
+def gather_blocks(value, planes, across, beside):
     n_dom = lax.axis_size("dom")
     down = lax.axis_size("feat") // 2
     held = []
     shifted = [value] + [swap(value, "dom", across * k) for k in range(1, planes)]
     for k, own in enumerate(shifted):
+        if k > 0:
+            own, beside = lax.optimization_barrier((own, beside))
         aside = [own] + [swap(own, "dom", i) for i in range(1, across)]
         below = [own] + [swap(own, "feat", 2 * j) for j in range(1, down)]
         pieces = list(aside)
@@ -442,6 +445,42 @@
                     pieces.append(swap(below[j], "dom", i))
         held.append(jnp.concatenate(pieces))
     return held + [swap(piece, "feat", 1) for piece in held]
+
+
+def total_of(values):
+    total = values[0].astype(F32)
+    for value in values[1:]:
+        total = total + value.astype(F32)
+    return total.astype(BF16)
+
+
+def return_blocks(arrays, planes, across):
+    down = lax.axis_size("feat") // 2
+    size = arrays[0].shape[0] // (across * down)
+    width = arrays[0].shape[-1]
+    terms = []
+    for k in list(range(1, planes)) + [0]:
+        other = swap(arrays[planes + k], "feat", 1)
+        pair = {}
+        for j in reversed(range(down)):
+            for i in reversed(range(across)):
+                at = slice((j * across + i) * size, (j * across + i + 1) * size)
+                pair[i, j] = total_of([arrays[k][at], other[at]]).reshape(-1, width)
+        parts = [pair[0, 0]]
+        for i in range(1, across):
+            piece = [pair[i, 0]]
+            if k % 2 == 0:
+                piece += [swap(pair[i, j], "feat", 2 * j) for j in range(1, down)]
+            parts.append(swap(total_of(piece), "dom", i))
+        for j in range(1, down):
+            piece = [pair[0, j]]
+            if k % 2 == 1:
+                piece += [swap(pair[i, j], "dom", i) for i in range(1, across)]
+            parts.append(swap(total_of(piece), "feat", 2 * j))
+        if k > 0:
+            parts = [swap(total_of(parts), "dom", across * k)]
+        terms += parts
+    return terms
 
 
 def doubling_sum(value, axis):
@@ -473,24 +512,22 @@
     planes = math.gcd(lax.axis_size("dom"), 4)
     across = lax.axis_size("dom") // planes
 
+    mine = lax.all_to_all(fetch_ids[:, 0, :], every, split_axis=0, concat_axis=0, tiled=True)
     weights = jnp.concatenate([w1_neigh, w1_self])
     weights = [weights] + [swap(weights, "feat", r) for r in range(1, n_feat)]
     parts = first_layer(inputs_t, tiles_first, first_dst, first_src, me, n_feat * blocks, n_feat)
     parts = [parts[0]] + [swap(parts[r], "feat", r) for r in range(1, n_feat)]
+    weights[0], mine = lax.optimization_barrier((weights[0], mine))
     pre, hidden = hidden_layer(parts, weights, bias_first.reshape(1, width))
-    wanted = fetch_ids[:, 0, :]
-    pools = gather_blocks(hidden, planes, across)
+    weight = row_weights(tiles_out, out_dst, blocks)
+    pools = gather_blocks(hidden, planes, across, weight)
     pools = [pool.reshape(-1, side, width) for pool in pools]
     owner = jnp.arange(devices, dtype=jnp.int32)[:, None]
     off_dom = (owner // n_feat) ^ me_dom
     off_feat = (owner % n_feat) ^ me_feat
     place = (off_feat % 2) * planes + off_dom // across
     place = (place * (n_feat // 2) + off_feat // 2) * across + off_dom % across
-    lists = lax.all_gather(wanted.reshape(1, -1), every, axis=0, tiled=True)
-    index = (me_dom * n_feat + me_feat) * slots_peer
-    mine = lax.dynamic_slice_in_dim(lists, index, slots_peer, axis=1)
     place = (place * blocks + mine).reshape(-1)
-    weight = row_weights(tiles_out, out_dst, blocks)
     even, odd, gnum, own = output_layer(
         tiles_out, out_dst, out_src, place, me, pools, weight, hidden, output_self_weight,
         output_neighbour_weight, bias_out, labels, scale, n_feat,
@@ -498,12 +535,16 @@
     third = doubling_sum(feat_sum(even, odd), "dom")
     third = jnp.stack([third] + [swap(third, "feat", r) for r in range(1, n_feat)])
     third = jnp.take(third, jnp.arange(n_feat) ^ me_feat, axis=0).reshape(-1, classes)
-    slot_grad = slot_gradients(tiles_out, out_dst, out_src, gnum, devices * slots_peer)
-    slot_grad = slot_grad.reshape(devices, slots_peer, side, width)
-    returned = lax.all_to_all(slot_grad, every, split_axis=0, concat_axis=0, tiled=True)
-    even, odd = first_gradients(
-        returned.reshape(devices * slots_peer, side, width), wanted.reshape(-1), own, pre, parts
+    index = jnp.arange(devices, dtype=jnp.int32)
+    plane = devices // (2 * planes)
+    to_dom = me_dom ^ (index // plane % planes * across + index % across)
+    to_feat = me_feat ^ (index % plane // across * 2 + index // (plane * planes))
+    owners = (to_dom * n_feat + to_feat).astype(jnp.int32)
+    arrays = slot_gradients(
+        tiles_out, out_dst, out_src, owners, mine.reshape(-1), gnum, 2 * planes
     )
+    terms = return_blocks(arrays, planes, across)
+    even, odd = first_gradients(terms, own, pre, parts)
     last = doubling_sum(feat_sum(even, odd), "dom")
     edge = 2 * features
     return (

time: 297 us -> 230 us (0.77)
  waiting for transfers between devices: 134 us -> 80.2 us
  blocking collectives: 41.9 us -> 13 us
  starting transfers between devices: 41.1 us -> 57.3 us
  other arithmetic: 1.23 us -> 4.61 us
    all_gather x1 -> x0, blocking collectives: 41.9 us -> none  [on_device(): lists = lax.all_gather(wanted.reshape(1, -1), every, axis=0, tiled=True)]
    ppermute x38 -> x57, waiting for transfers between devices: 113 us -> 80.2 us  [swap(): lax.ppermute(value, axis, [(k, k ^ mask) for k in range(lax.axis_size(axi...]
    all_to_all x1 -> x0, waiting for transfers between devices: 22 us -> none  [on_device(): lax.all_to_all(slot_grad, every, split_axis=0, concat_axis=0, tiled=True)]
    ppermute x38 -> x57, starting transfers between devices: 37.3 us -> 57.3 us  [swap(): lax.ppermute(value, axis, [(k, k ^ mask) for k in range(lax.axis_size(axi...]
    all_to_all x0 -> x1, blocking collectives: none -> 13 us  [on_device(): lax.all_to_all(fetch_ids[:, 0, :], every, split_axis=0, concat_axis=0, ti...]
    all_to_all x1 -> x0, starting transfers between devices: 3.71 us -> none  [on_device(): lax.all_to_all(slot_grad, every, split_axis=0, concat_axis=0, tiled=True)]
    unnamed x49 -> x66, local copies, waits for them, and re-layouts: 6.48 us -> 5.49 us
  transfers between devices with their start and end apart: 39 -> 57, of which waited for: 21 -> 24; matrix products, arithmetic and copies ran while one was open for 4% -> 6% of each run, Pallas kernels for 6% -> 6%
where the time goes in v3:
time: 230 us
  waiting for transfers between devices  80.2 us (35%)
  Pallas kernels  61 us (27%)
  starting transfers between devices  57.3 us (25%)
  blocking collectives  13 us (6%)
  local copies, waits for them, and re-layouts  12.2 us (5%)
  other arithmetic  4.61 us (2%)
    ppermute x57, waiting for transfers between devices, swap(): lax.ppermute(value, axis, [(k, k ^ mask) for k in range(lax.axis_size(axi...  80.2 us
    ppermute x57, starting transfers between devices, swap(): lax.ppermute(value, axis, [(k, k ^ mask) for k in range(lax.axis_size(axi...  57.3 us
    pallas_call x1, Pallas kernels, output_layer(): pl.pallas_call(kernel, grid_spec=pltpu.PrefetchScalarGridSpec(num_scalar_...  20.6 us
    pallas_call x1, Pallas kernels, slot_gradients(): pl.pallas_call(kernel, grid_spec=pltpu.PrefetchScalarGridSpec(num_scalar_...  19.3 us
    all_to_all x1, blocking collectives, on_device(): lax.all_to_all(fetch_ids[:, 0, :], every, split_axis=0, concat_axis=0, ti...  13 us
    pallas_call x1, Pallas kernels, row_weights(): pl.pallas_call(kernel, grid_spec=pltpu.PrefetchScalarGridSpec(num_scalar_...  11.1 us
    unnamed x66, local copies, waits for them, and re-layouts  5.49 us
    pallas_call x1, Pallas kernels, first_layer(): pl.pallas_call(kernel, grid_spec=pltpu.PrefetchScalarGridSpec(num_scalar_...  4.78 us
  transfers between devices with their start and end apart: 57, of which 24 were waited for; matrix products, arithmetic and copies ran while one was open for 6% of the time, Pallas kernels for 6%

profile of v3, /device:TPU:0, one launch (start us, length us, event | category | flops | bytes accessed | tf_op | source)
XLA Modules:
  0.0 229.5 jit_solution(9733117303229726695)
XLA Ops:
  0.7 4.8 %first_layer.1 = (bf16[64,512]{1,0:T(8,128)(2,1)}, bf16[64,512]{1,0:T(8,128)(2,1)}, bf16[64,512]{1,0:T(8,128)(2,1)}, bf16[64,512]{1,0:T(8,128)(2,1)}) custom-call(s32[64]{0:T(128)} %dst_s.5, s32[64]{0:T(128)} %src_s.3, s32[1]{0:T(128)} %bitcast.1.me_s, bf16[64,128,128]{2,1,0:T(8,128)(2,1)} %tile_ref.5, bf16[32,4096]{1,0:T(8,128)(2,1)} %feat_ref.1), custom_call_target="tpu_custom_call" | custom-call | tf_op jit(solution)/shard_map/first_layer/pallas_call | solution.py:67
  6.0 3.0 %collective-permute-start.1 = (bf16[64,512]{1,0:T(8,128)(2,1)}, bf16[64,512]{1,0:T(8,128)(2,1)S(1)}, u32[]{:S(2)}, u32[]{:S(2)}) collective-permute-start(bf16[64,512]{1,0:T(8,128)(2,1)} %get-tuple-element.32), channel_id=1, source_target_pairs={{0,2},{1,3},{2,0},{3,1},{4,6},{5,7},{6,4},{7,5},{8,10},{9,11},{10,... | collective-permute-start | bytes 196616 | tf_op jit(solution)/shard_map/ppermute | solution.py:416
  9.0 1.4 collective-permute-start.4
  10.9 13.0 %all_to_all.9 = s32[32,1,2]{2,1,0:T(1,128)S(1)} all-to-all(s32[32,1,2]{2,1,0:T(1,128)S(1)} %copy.32), channel_id=1, replica_groups=mesh['dom'=8,'feat'=4] {'dom','feat'}, dimensions={0} | all-to-all | bytes 512 | tf_op jit(solution)/shard_map/all_to_all | solution.py:515
  24.7 2.3 %hidden_layer.1 = (f32[512,256]{1,0:T(8,128)}, bf16[512,256]{1,0:T(8,128)(2,1)}) custom-call(bf16[64,512]{1,0:T(8,128)(2,1)} %get-tuple-element.30.refs_0_.refs_8_, bf16[64,512]{1,0:T(8,128)(2,1)} %copy-done.9, bf16[64,512]{1,0:T(8,128)(2,1)} %copy-done.10, bf16[64,512]{1,0:T(8,128)(2,1)} %copy-done.11, bf16[64,256]{1,0:T(8,128)(2,1)} %copy-done.19, ...), custom_call_target="tpu_custom_call" | custom-call | tf_op jit(solution)/shard_map/hidden_layer/pallas_call | solution.py:102
  28.7 11.1 %row_weights.1.weight_ref = f32[4,128,128]{2,1,0:T(8,128)} custom-call(s32[384]{0:T(512)} %dst_s.7, bf16[384,128,128]{2,1,0:T(8,128)(2,1)} %tile_ref.7), custom_call_target="tpu_custom_call" | custom-call | flops 12582912 | bytes 12582912 | tf_op jit(solution)/shard_map/row_weights/pallas_call | solution.py:143
  41.1 3.3 %collective-permute-start.17 = (bf16[512,256]{1,0:T(8,128)(2,1)S(1)}, bf16[512,256]{1,0:T(8,128)(2,1)S(1)}, u32[]{:S(2)}, u32[]{:S(2)}) collective-permute-start(bf16[512,256]{1,0:T(8,128)(2,1)S(1)} %copy-done.3), channel_id=1, source_target_pairs={{0,24},{4,28},{8,16},{12,20},{16,8},{20,12},{24,0},{28,4},{1,25},{... | collective-permute-start | bytes 786440 | tf_op jit(solution)/shard_map/ppermute | solution.py:416
  45.8 1.5 collective-permute-start.11
  51.4 2.3 collective-permute-done.10
  55.1 1.5 collective-permute-start.12
  56.5 2.7 %collective-permute-done.14 = bf16[512,256]{1,0:T(8,128)(2,1)S(1)} collective-permute-done((bf16[512,256]{1,0:T(8,128)(2,1)S(1)}, bf16[512,256]{1,0:T(8,128)(2,1)S(1)}, u32[]{:S(2)}, u32[]{:S(2)}) %collective-permute-start.14) | collective-permute-done | bytes 262176 | tf_op jit(solution)/shard_map/ppermute | solution.py:416
  60.8 1.5 collective-permute-start.18
  63.0 8.9 %collective-permute-done.19 = bf16[512,256]{1,0:T(8,128)(2,1)S(1)} collective-permute-done((bf16[512,256]{1,0:T(8,128)(2,1)S(1)}, bf16[512,256]{1,0:T(8,128)(2,1)S(1)}, u32[]{:S(2)}, u32[]{:S(2)}) %collective-permute-start.19) | collective-permute-done | bytes 262176 | tf_op jit(solution)/shard_map/ppermute | solution.py:416
  72.9 2.2 collective-permute-done.16
  75.3 5.4 %collective-permute-done.20 = bf16[512,256]{1,0:T(8,128)(2,1)S(1)} collective-permute-done((bf16[512,256]{1,0:T(8,128)(2,1)S(1)}, bf16[512,256]{1,0:T(8,128)(2,1)S(1)}, u32[]{:S(2)}, u32[]{:S(2)}) %collective-permute-start.20) | collective-permute-done | bytes 262176 | tf_op jit(solution)/shard_map/ppermute | solution.py:416
  85.4 20.6 %output_layer.1 = (f32[2,136,172]{2,1,0:T(8,128)}, f32[2,136,172]{2,1,0:T(8,128)}, bf16[4,128,256]{2,1,0:T(8,128)(2,1)}, f32[512,256]{1,0:T(8,128)}) custom-call(s32[384]{0:T(512)} %dst_s.7, s32[384]{0:T(512)} %src_s.5, s32[64]{0:T(128)} %reshape.299.place_s, s32[1]{0:T(128)} %bitcast.1.me_s, bf16[384,128,128]{2,1,0:T(8,128)(2,1)} %tile_ref.7, ...), custom_call_target="tpu_custom_call" | custom-call | tf_op jit(solution)/shard_map/output_layer/pallas_call | solution.py:267
  106.0 19.3 %slot_gradients.1 = (bf16[16,128,256]{2,1,0:T(8,128)(2,1)}, bf16[16,128,256]{2,1,0:T(8,128)(2,1)}, bf16[16,128,256]{2,1,0:T(8,128)(2,1)}, bf16[16,128,256]{2,1,0...) custom-call(s32[384]{0:T(512)} %dst_s.7, ...), custom_call_target="tpu_custom_call" | custom-call | tf_op jit(solution)/shard_map/slot_gradients/pallas_call | solution.py:359
  126.4 2.4 %collective-permute-done.49 = f32[2,136,172]{2,1,0:T(8,128)S(1)} collective-permute-done((f32[2,136,172]{2,1,0:T(8,128)S(1)}, f32[2,136,172]{2,1,0:T(8,128)S(1)}, u32[]{:S(2)}, u32[]{:S(2)}) %collective-permute-start.49) | collective-permute-done | bytes 187168 | tf_op jit(solution)/shard_map/ppermute | solution.py:416
  128.9 1.5 collective-permute-start.50
  130.5 4.4 %collective-permute-done.50 = f32[1,136,172]{2,1,0:T(8,128)S(1)} collective-permute-done((f32[1,136,172]{2,1,0:T(8,128)S(1)}, f32[1,136,172]{2,1,0:T(8,128)S(1)}, u32[]{:S(2)}, u32[]{:S(2)}) %collective-permute-start.50) | collective-permute-done | bytes 93600 | tf_op jit(solution)/shard_map/ppermute | solution.py:416
  135.6 4.5 %collective-permute-done.51 = f32[136,172]{1,0:T(8,128)S(1)} collective-permute-done((f32[136,172]{1,0:T(8,128)S(1)}, f32[136,172]{1,0:T(8,128)S(1)}, u32[]{:S(2)}, u32[]{:S(2)}) %collective-permute-start.51) | collective-permute-done | bytes 93600 | tf_op jit(solution)/shard_map/ppermute | solution.py:416
  141.6 1.5 collective-permute-start.27
  144.8 1.7 collective-permute-start.31
  147.6 3.3 %collective-permute-done.27 = bf16[512,256]{1,0:T(8,128)(2,1)S(1)} collective-permute-done((bf16[512,256]{1,0:T(8,128)(2,1)S(1)}, bf16[512,256]{1,0:T(8,128)(2,1)S(1)}, u32[]{:S(2)}, u32[]{:S(2)}) %collective-permute-start.27) | collective-permute-done | bytes 262176 | tf_op jit(solution)/shard_map/ppermute | solution.py:416
  150.9 1.4 collective-permute-start.37
  152.4 3.7 %collective-permute-done.31 = bf16[512,256]{1,0:T(8,128)(2,1)S(1)} collective-permute-done((bf16[512,256]{1,0:T(8,128)(2,1)S(1)}, bf16[512,256]{1,0:T(8,128)(2,1)S(1)}, u32[]{:S(2)}, u32[]{:S(2)}) %collective-permute-start.31) | collective-permute-done | bytes 262176 | tf_op jit(solution)/shard_map/ppermute | solution.py:416
  156.7 2.5 %collective-permute-done.37 = bf16[512,256]{1,0:T(8,128)(2,1)S(1)} collective-permute-done((bf16[512,256]{1,0:T(8,128)(2,1)S(1)}, bf16[512,256]{1,0:T(8,128)(2,1)S(1)}, u32[]{:S(2)}, u32[]{:S(2)}) %collective-permute-start.37) | collective-permute-done | bytes 262176 | tf_op jit(solution)/shard_map/ppermute | solution.py:416
  160.2 4.3 %collective-permute-done.41 = bf16[512,256]{1,0:T(8,128)(2,1)S(1)} collective-permute-done((bf16[512,256]{1,0:T(8,128)(2,1)S(1)}, bf16[512,256]{1,0:T(8,128)(2,1)S(1)}, u32[]{:S(2)}, u32[]{:S(2)}) %collective-permute-start.41) | collective-permute-done | bytes 262176 | tf_op jit(solution)/shard_map/ppermute | solution.py:416
  164.5 1.4 collective-permute-start.32
  169.8 3.2 %collective-permute-done.32 = bf16[512,256]{1,0:T(8,128)(2,1)S(1)} collective-permute-done((bf16[512,256]{1,0:T(8,128)(2,1)S(1)}, bf16[512,256]{1,0:T(8,128)(2,1)S(1)}, u32[]{:S(2)}, u32[]{:S(2)}) %collective-permute-start.32) | collective-permute-done | bytes 262176 | tf_op jit(solution)/shard_map/ppermute | solution.py:416
  173.0 2.1 collective-permute-start.42
  176.5 1.6 collective-permute-start.29
  178.1 1.4 collective-permute-start.34
  179.6 1.4 collective-permute-start.39
  181.1 1.5 collective-permute-start.53
  182.6 3.4 %collective-permute-done.29.refs_0_ = bf16[512,256]{1,0:T(8,128)(2,1)S(1)} collective-permute-done((bf16[512,256]{1,0:T(8,128)(2,1)S(1)}, bf16[512,256]{1,0:T(8,128)(2,1)S(1)}, u32[]{:S(2)}, u32[]{:S(2)}) %collective-permute-start.29) | collective-permute-done | bytes 262176 | tf_op jit(solution)/shard_map/ppermute | solution.py:416
  186.0 9.3 %collective-permute-done.34.refs_1_ = bf16[512,256]{1,0:T(8,128)(2,1)S(1)} collective-permute-done((bf16[512,256]{1,0:T(8,128)(2,1)S(1)}, bf16[512,256]{1,0:T(8,128)(2,1)S(1)}, u32[]{:S(2)}, u32[]{:S(2)}) %collective-permute-start.34) | collective-permute-done | bytes 262176 | tf_op jit(solution)/shard_map/ppermute | solution.py:416
  196.1 2.9 %first_gradients.1 = (f32[2,72,256]{2,1,0:T(8,128)}, f32[2,72,256]{2,1,0:T(8,128)}) custom-call(bf16[512,256]{1,0:T(8,128)(2,1)} %copy-done.14, bf16[512,256]{1,0:T(8,128)(2,1)} %copy-done.15, bf16[512,256]{1,0:T(8,128)(2,1)} %copy-done.16, bf16[512,256]{1,0:T(8,128)(2,1)} %bitcast.59, bf16[512,256]{1,0:T(8,128)(2,1)} %copy-done.13, ...), custom_call_target="tpu_custom_call" | custom-call | tf_op jit(solution)/shard_map/first_gradients/pallas_call | solution.py:405
  199.3 2.9 %collective-permute-done.53 = f32[136,172]{1,0:T(8,128)S(1)} collective-permute-done((f32[136,172]{1,0:T(8,128)S(1)}, f32[136,172]{1,0:T(8,128)S(1)}, u32[]{:S(2)}, u32[]{:S(2)}) %collective-permute-start.53) | collective-permute-done | bytes 93600 | tf_op jit(solution)/shard_map/ppermute | solution.py:416
  202.3 1.5 collective-permute-start.55
  205.1 1.5 collective-permute-start.45
  206.6 1.6 collective-permute-done.56
  208.2 3.0 %collective-permute-done.55 = f32[136,172]{1,0:T(8,128)S(1)} collective-permute-done((f32[136,172]{1,0:T(8,128)S(1)}, f32[136,172]{1,0:T(8,128)S(1)}, u32[]{:S(2)}, u32[]{:S(2)}) %collective-permute-start.55) | collective-permute-done | bytes 93600 | tf_op jit(solution)/shard_map/ppermute | solution.py:416
  213.4 3.9 %collective-permute-done.46 = f32[72,256]{1,0:T(8,128)S(1)} collective-permute-done((f32[72,256]{1,0:T(8,128)S(1)}, f32[72,256]{1,0:T(8,128)S(1)}, u32[]{:S(2)}, u32[]{:S(2)}) %collective-permute-start.46) | collective-permute-done | bytes 73760 | tf_op jit(solution)/shard_map/ppermute | solution.py:416
  217.3 3.0 %collective-permute-start.47 = (f32[72,256]{1,0:T(8,128)S(1)}, f32[72,256]{1,0:T(8,128)S(1)}, u32[]{:S(2)}, u32[]{:S(2)}) collective-permute-start(f32[72,256]{1,0:T(8,128)S(1)} %add.269), channel_id=1, source_target_pairs={{0,8},{4,12},{8,0},{12,4},{16,24},{20,28},{24,16},{28,20},{1,9},{5... | collective-permute-start | bytes 221192 | tf_op jit(solution)/shard_map/ppermute | solution.py:416
  221.0 1.6 collective-permute-done.47
  222.6 3.4 %collective-permute-start.48 = (f32[72,256]{1,0:T(8,128)S(1)}, f32[72,256]{1,0:T(8,128)S(1)}, u32[]{:S(2)}, u32[]{:S(2)}) collective-permute-start(f32[72,256]{1,0:T(8,128)S(1)} %add.270), channel_id=1, source_target_pairs={{0,16},{4,20},{8,24},{12,28},{16,0},{20,4},{24,8},{28,12},{1,17},{... | collective-permute-start | bytes 221192 | tf_op jit(solution)/shard_map/ppermute | solution.py:416
  226.7 1.7 collective-permute-done.48
  (188 shorter events, 39.8 us)
Async XLA Ops:
  5.4 18.5 %collective-permute-start = (bf16[64,512]{1,0:T(8,128)(2,1)}, bf16[64,512]{1,0:T(8,128)(2,1)S(1)}, u32[]{:S(2)}, u32[]{:S(2)}) collective-permute-start(bf16[64,512]{1,0:T(8,128)(2,1)} %get-tuple-element.31), channel_id=1, source_target_pairs={{0,1},{1,0},{2,3},{3,2},{4,5},{5,4},{6,7},{7,6},{8,9},{9,8},{10,11... | collective-permute-start | bytes 196616 | tf_op jit(solution)/shard_map/ppermute | solution.py:416
  6.0 18.0 %collective-permute-start.1 = (bf16[64,512]{1,0:T(8,128)(2,1)}, bf16[64,512]{1,0:T(8,128)(2,1)S(1)}, u32[]{:S(2)}, u32[]{:S(2)}) collective-permute-start(bf16[64,512]{1,0:T(8,128)(2,1)} %get-tuple-element.32), channel_id=1, source_target_pairs={{0,2},{1,3},{2,0},{3,1},{4,6},{5,7},{6,4},{7,5},{8,10},{9,11},{10,... | collective-permute-start | bytes 196616 | tf_op jit(solution)/shard_map/ppermute | solution.py:416
  9.0 15.0 %collective-permute-start.2 = (bf16[64,512]{1,0:T(8,128)(2,1)}, bf16[64,512]{1,0:T(8,128)(2,1)S(1)}, u32[]{:S(2)}, u32[]{:S(2)}) collective-permute-start(bf16[64,512]{1,0:T(8,128)(2,1)} %get-tuple-element.33), channel_id=1, source_target_pairs={{0,3},{1,2},{2,1},{3,0},{4,7},{5,6},{6,5},{7,4},{8,11},{9,10},{10,... | collective-permute-start | bytes 196616 | tf_op jit(solution)/shard_map/ppermute | solution.py:416
  9.0 15.0 %collective-permute-start.4 = (bf16[64,256]{1,0:T(8,128)(2,1)S(1)}, bf16[64,256]{1,0:T(8,128)(2,1)S(1)}, u32[]{:S(2)}, u32[]{:S(2)}) collective-permute-start(bf16[64,256]{1,0:T(8,128)(2,1)S(1)} %constant_dynamic-update-slice_fusion.refs_4_), channel_id=1, source_target_pairs={{0,2},{1,3},{2,0},{3,1},{4,6},{5,7},{6,4},{7,5},{8,10},{9,11},{10,... | collective-permute-start | bytes 98312 | tf_op jit(solution)/shard_map/ppermute | solution.py:416
  10.4 13.5 %collective-permute-start.5 = (bf16[64,256]{1,0:T(8,128)(2,1)S(1)}, bf16[64,256]{1,0:T(8,128)(2,1)S(1)}, u32[]{:S(2)}, u32[]{:S(2)}) collective-permute-start(bf16[64,256]{1,0:T(8,128)(2,1)S(1)} %constant_dynamic-update-slice_fusion.refs_4_), channel_id=1, source_target_pairs={{0,3},{1,2},{2,1},{3,0},{4,7},{5,6},{6,5},{7,4},{8,11},{9,10},{10,... | collective-permute-start | bytes 98312 | tf_op jit(solution)/shard_map/ppermute | solution.py:416
  27.0 17.4 %collective-permute-start.9 = (bf16[512,256]{1,0:T(8,128)(2,1)}, bf16[512,256]{1,0:T(8,128)(2,1)S(1)}, u32[]{:S(2)}, u32[]{:S(2)}) collective-permute-start(bf16[512,256]{1,0:T(8,128)(2,1)} %get-tuple-element.35.hidden_ref), channel_id=1, source_target_pairs={{0,8},{4,12},{8,0},{12,4},{16,24},{20,28},{24,16},{28,20},{1,9},{5... | collective-permute-start | bytes 786440 | tf_op jit(solution)/shard_map/ppermute | solution.py:416
  27.6 18.2 %collective-permute-start.13 = (bf16[512,256]{1,0:T(8,128)(2,1)}, bf16[512,256]{1,0:T(8,128)(2,1)S(1)}, u32[]{:S(2)}, u32[]{:S(2)}) collective-permute-start(bf16[512,256]{1,0:T(8,128)(2,1)} %get-tuple-element.35.hidden_ref), channel_id=1, source_target_pairs={{0,16},{4,20},{8,24},{12,28},{16,0},{20,4},{24,8},{28,12},{1,17},{... | collective-permute-start | bytes 786440 | tf_op jit(solution)/shard_map/ppermute | solution.py:416
  28.1 19.2 %collective-permute-start.6 = (bf16[512,256]{1,0:T(8,128)(2,1)}, bf16[512,256]{1,0:T(8,128)(2,1)S(1)}, u32[]{:S(2)}, u32[]{:S(2)}) collective-permute-start(bf16[512,256]{1,0:T(8,128)(2,1)} %get-tuple-element.35.hidden_ref), channel_id=1, source_target_pairs={{0,4},{4,0},{8,12},{12,8},{16,20},{20,16},{24,28},{28,24},{1,5},{5... | collective-permute-start | bytes 786440 | tf_op jit(solution)/shard_map/ppermute | solution.py:416
  39.8 8.9 %collective-permute-start.7 = (bf16[512,256]{1,0:T(8,128)(2,1)S(1)}, bf16[512,256]{1,0:T(8,128)(2,1)S(1)}, u32[]{:S(2)}, u32[]{:S(2)}) collective-permute-start(bf16[512,256]{1,0:T(8,128)(2,1)S(1)} %copy-done.3), channel_id=1, source_target_pairs={{0,2},{1,3},{2,0},{3,1},{4,6},{5,7},{6,4},{7,5},{8,10},{9,11},{10,... | collective-permute-start | bytes 786440 | tf_op jit(solution)/shard_map/ppermute | solution.py:416
  41.1 8.9 %collective-permute-start.17 = (bf16[512,256]{1,0:T(8,128)(2,1)S(1)}, bf16[512,256]{1,0:T(8,128)(2,1)S(1)}, u32[]{:S(2)}, u32[]{:S(2)}) collective-permute-start(bf16[512,256]{1,0:T(8,128)(2,1)S(1)} %copy-done.3), channel_id=1, source_target_pairs={{0,24},{4,28},{8,16},{12,20},{16,8},{20,12},{24,0},{28,4},{1,25},{... | collective-permute-start | bytes 786440 | tf_op jit(solution)/shard_map/ppermute | solution.py:416
  44.4 9.2 %collective-permute-start.10 = (bf16[512,256]{1,0:T(8,128)(2,1)S(1)}, bf16[512,256]{1,0:T(8,128)(2,1)S(1)}, u32[]{:S(2)}, u32[]{:S(2)}) collective-permute-start(bf16[512,256]{1,0:T(8,128)(2,1)S(1)} %collective-permute-done.9), channel_id=1, source_target_pairs={{0,4},{4,0},{8,12},{12,8},{16,20},{20,16},{24,28},{28,24},{1,5},{5... | collective-permute-start | bytes 786440 | tf_op jit(solution)/shard_map/ppermute | solution.py:416
  45.8 9.3 %collective-permute-start.11 = (bf16[512,256]{1,0:T(8,128)(2,1)S(1)}, bf16[512,256]{1,0:T(8,128)(2,1)S(1)}, u32[]{:S(2)}, u32[]{:S(2)}) collective-permute-start(bf16[512,256]{1,0:T(8,128)(2,1)S(1)} %collective-permute-done.9), channel_id=1, source_target_pairs={{0,2},{1,3},{2,0},{3,1},{4,6},{5,7},{6,4},{7,5},{8,10},{9,11},{10,... | collective-permute-start | bytes 786440 | tf_op jit(solution)/shard_map/ppermute | solution.py:416
  47.3 12.0 %collective-permute-start.14 = (bf16[512,256]{1,0:T(8,128)(2,1)S(1)}, bf16[512,256]{1,0:T(8,128)(2,1)S(1)}, u32[]{:S(2)}, u32[]{:S(2)}) collective-permute-start(bf16[512,256]{1,0:T(8,128)(2,1)S(1)} %collective-permute-done.13), channel_id=1, source_target_pairs={{0,4},{4,0},{8,12},{12,8},{16,20},{20,16},{24,28},{28,24},{1,5},{5... | collective-permute-start | bytes 786440 | tf_op jit(solution)/shard_map/ppermute | solution.py:416
  48.6 12.1 %collective-permute-start.8 = (bf16[512,256]{1,0:T(8,128)(2,1)S(1)}, bf16[512,256]{1,0:T(8,128)(2,1)S(1)}, u32[]{:S(2)}, u32[]{:S(2)}) collective-permute-start(bf16[512,256]{1,0:T(8,128)(2,1)S(1)} %collective-permute-done.6), channel_id=1, source_target_pairs={{0,2},{1,3},{2,0},{3,1},{4,6},{5,7},{6,4},{7,5},{8,10},{9,11},{10,... | collective-permute-start | bytes 786440 | tf_op jit(solution)/shard_map/ppermute | solution.py:416
  50.0 22.6 %collective-permute-start.15 = (bf16[512,256]{1,0:T(8,128)(2,1)S(1)}, bf16[512,256]{1,0:T(8,128)(2,1)S(1)}, u32[]{:S(2)}, u32[]{:S(2)}) collective-permute-start(bf16[512,256]{1,0:T(8,128)(2,1)S(1)} %collective-permute-done.13), channel_id=1, source_target_pairs={{0,2},{1,3},{2,0},{3,1},{4,6},{5,7},{6,4},{7,5},{8,10},{9,11},{10,... | collective-permute-start | bytes 786440 | tf_op jit(solution)/shard_map/ppermute | solution.py:416
  53.7 18.3 %collective-permute-start.19 = (bf16[512,256]{1,0:T(8,128)(2,1)S(1)}, bf16[512,256]{1,0:T(8,128)(2,1)S(1)}, u32[]{:S(2)}, u32[]{:S(2)}) collective-permute-start(bf16[512,256]{1,0:T(8,128)(2,1)S(1)} %collective-permute-done.17), channel_id=1, source_target_pairs={{0,2},{1,3},{2,0},{3,1},{4,6},{5,7},{6,4},{7,5},{8,10},{9,11},{10,... | collective-permute-start | bytes 786440 | tf_op jit(solution)/shard_map/ppermute | solution.py:416
  55.1 16.9 %collective-permute-start.12 = (bf16[512,256]{1,0:T(8,128)(2,1)S(1)}, bf16[512,256]{1,0:T(8,128)(2,1)S(1)}, u32[]{:S(2)}, u32[]{:S(2)}) collective-permute-start(bf16[512,256]{1,0:T(8,128)(2,1)S(1)} %collective-permute-done.11), channel_id=1, source_target_pairs={{0,4},{4,0},{8,12},{12,8},{16,20},{20,16},{24,28},{28,24},{1,5},{5... | collective-permute-start | bytes 786440 | tf_op jit(solution)/shard_map/ppermute | solution.py:416
  59.3 15.8 %collective-permute-start.16 = (bf16[512,256]{1,0:T(8,128)(2,1)S(1)}, bf16[512,256]{1,0:T(8,128)(2,1)S(1)}, u32[]{:S(2)}, u32[]{:S(2)}) collective-permute-start(bf16[512,256]{1,0:T(8,128)(2,1)S(1)} %collective-permute-done.14), channel_id=1, source_target_pairs={{0,2},{1,3},{2,0},{3,1},{4,6},{5,7},{6,4},{7,5},{8,10},{9,11},{10,... | collective-permute-start | bytes 786440 | tf_op jit(solution)/shard_map/ppermute | solution.py:416
  60.8 14.5 %collective-permute-start.18 = (bf16[512,256]{1,0:T(8,128)(2,1)S(1)}, bf16[512,256]{1,0:T(8,128)(2,1)S(1)}, u32[]{:S(2)}, u32[]{:S(2)}) collective-permute-start(bf16[512,256]{1,0:T(8,128)(2,1)S(1)} %collective-permute-done.17), channel_id=1, source_target_pairs={{0,4},{4,0},{8,12},{12,8},{16,20},{20,16},{24,28},{28,24},{1,5},{5... | collective-permute-start | bytes 786440 | tf_op jit(solution)/shard_map/ppermute | solution.py:416
  71.9 13.4 %collective-permute-start.21 = (bf16[2048,256]{1,0:T(8,128)(2,1)}, bf16[2048,256]{1,0:T(8,128)(2,1)}, u32[]{:S(2)}, u32[]{:S(2)}) collective-permute-start(bf16[2048,256]{1,0:T(8,128)(2,1)} %constant_dynamic-update-slice_fusion.2), channel_id=1, source_target_pairs={{0,1},{1,0},{2,3},{3,2},{4,5},{5,4},{6,7},{7,6},{8,9},{9,8},{10,11... | collective-permute-start | bytes 3145736 | tf_op jit(solution)/shard_map/ppermute | solution.py:416
  71.9 8.7 %collective-permute-start.20 = (bf16[512,256]{1,0:T(8,128)(2,1)S(1)}, bf16[512,256]{1,0:T(8,128)(2,1)S(1)}, u32[]{:S(2)}, u32[]{:S(2)}) collective-permute-start(bf16[512,256]{1,0:T(8,128)(2,1)S(1)} %collective-permute-done.19), channel_id=1, source_target_pairs={{0,4},{4,0},{8,12},{12,8},{16,20},{20,16},{24,28},{28,24},{1,5},{5... | collective-permute-start | bytes 786440 | tf_op jit(solution)/shard_map/ppermute | solution.py:416
  72.6 12.7 %collective-permute-start.22 = (bf16[2048,256]{1,0:T(8,128)(2,1)S(1)}, bf16[2048,256]{1,0:T(8,128)(2,1)}, u32[]{:S(2)}, u32[]{:S(2)}) collective-permute-start(bf16[2048,256]{1,0:T(8,128)(2,1)S(1)} %constant_dynamic-update-slice_fusion.6), channel_id=1, source_target_pairs={{0,1},{1,0},{2,3},{3,2},{4,5},{5,4},{6,7},{7,6},{8,9},{9,8},{10,11... | collective-permute-start | bytes 3145736 | tf_op jit(solution)/shard_map/ppermute | solution.py:416
  75.2 10.1 %collective-permute-start.23 = (bf16[2048,256]{1,0:T(8,128)(2,1)S(1)}, bf16[2048,256]{1,0:T(8,128)(2,1)}, u32[]{:S(2)}, u32[]{:S(2)}) collective-permute-start(bf16[2048,256]{1,0:T(8,128)(2,1)S(1)} %pad_maximum_fusion), channel_id=1, source_target_pairs={{0,1},{1,0},{2,3},{3,2},{4,5},{5,4},{6,7},{7,6},{8,9},{9,8},{10,11... | collective-permute-start | bytes 3145736 | tf_op jit(solution)/shard_map/ppermute | solution.py:416
  125.3 16.0 %collective-permute-start.25 = (bf16[16,128,256]{2,1,0:T(8,128)(2,1)}, bf16[16,128,256]{2,1,0:T(8,128)(2,1)S(1)}, u32[]{:S(2)}, u32[]{:S(2)}) collective-permute-start(bf16[16,128,256]{2,1,0:T(8,128)(2,1)} %get-tuple-element.39), channel_id=1, source_target_pairs={{0,1},{1,0},{2,3},{3,2},{4,5},{5,4},{6,7},{7,6},{8,9},{9,8},{10,11... | collective-permute-start | bytes 3145736 | tf_op jit(solution)/shard_map/ppermute | solution.py:416
  125.7 17.4 %collective-permute-start.30 = (bf16[16,128,256]{2,1,0:T(8,128)(2,1)}, bf16[16,128,256]{2,1,0:T(8,128)(2,1)S(1)}, u32[]{:S(2)}, u32[]{:S(2)}) collective-permute-start(bf16[16,128,256]{2,1,0:T(8,128)(2,1)} %get-tuple-element.41), channel_id=1, source_target_pairs={{0,1},{1,0},{2,3},{3,2},{4,5},{5,4},{6,7},{7,6},{8,9},{9,8},{10,11... | collective-permute-start | bytes 3145736 | tf_op jit(solution)/shard_map/ppermute | solution.py:416
  126.2 17.8 %collective-permute-start.35 = (bf16[16,128,256]{2,1,0:T(8,128)(2,1)}, bf16[16,128,256]{2,1,0:T(8,128)(2,1)S(1)}, u32[]{:S(2)}, u32[]{:S(2)}) collective-permute-start(bf16[16,128,256]{2,1,0:T(8,128)(2,1)} %get-tuple-element.43), channel_id=1, source_target_pairs={{0,1},{1,0},{2,3},{3,2},{4,5},{5,4},{6,7},{7,6},{8,9},{9,8},{10,11... | collective-permute-start | bytes 3145736 | tf_op jit(solution)/shard_map/ppermute | solution.py:416
  130.4 14.4 %collective-permute-start.40 = (bf16[16,128,256]{2,1,0:T(8,128)(2,1)}, bf16[16,128,256]{2,1,0:T(8,128)(2,1)S(1)}, u32[]{:S(2)}, u32[]{:S(2)}) collective-permute-start(bf16[16,128,256]{2,1,0:T(8,128)(2,1)} %get-tuple-element.45), channel_id=1, source_target_pairs={{0,1},{1,0},{2,3},{3,2},{4,5},{5,4},{6,7},{7,6},{8,9},{9,8},{10,11... | collective-permute-start | bytes 3145736 | tf_op jit(solution)/shard_map/ppermute | solution.py:416
  140.1 39.5 %collective-permute-start.52 = (f32[136,172]{1,0:T(8,128)S(1)}, f32[136,172]{1,0:T(8,128)S(1)}, u32[]{:S(2)}, u32[]{:S(2)}) collective-permute-start(f32[136,172]{1,0:T(8,128)S(1)} %add.275), channel_id=1, source_target_pairs={{0,8},{4,12},{8,0},{12,4},{16,24},{20,28},{24,16},{28,20},{1,9},{5... | collective-permute-start | bytes 280712 | tf_op jit(solution)/shard_map/ppermute | solution.py:416
  141.6 9.3 %collective-permute-start.27 = (bf16[512,256]{1,0:T(8,128)(2,1)S(1)}, bf16[512,256]{1,0:T(8,128)(2,1)S(1)}, u32[]{:S(2)}, u32[]{:S(2)}) collective-permute-start(bf16[512,256]{1,0:T(8,128)(2,1)S(1)} %bitcast.65), channel_id=1, source_target_pairs={{0,4},{4,0},{8,12},{12,8},{16,20},{20,16},{24,28},{28,24},{1,5},{5... | collective-permute-start | bytes 786440 | tf_op jit(solution)/shard_map/ppermute | solution.py:416
  143.1 22.9 %collective-permute-start.26 = (bf16[512,256]{1,0:T(8,128)(2,1)S(1)}, bf16[512,256]{1,0:T(8,128)(2,1)S(1)}, u32[]{:S(2)}, u32[]{:S(2)}) collective-permute-start(bf16[512,256]{1,0:T(8,128)(2,1)S(1)} %bitcast.64), channel_id=1, source_target_pairs={{0,4},{4,0},{8,12},{12,8},{16,20},{20,16},{24,28},{28,24},{1,5},{5... | collective-permute-start | bytes 786440 | tf_op jit(solution)/shard_map/ppermute | solution.py:416
  144.0 24.7 %collective-permute-start.33 = (bf16[512,256]{1,0:T(8,128)(2,1)S(1)}, bf16[512,256]{1,0:T(8,128)(2,1)S(1)}, u32[]{:S(2)}, u32[]{:S(2)}) collective-permute-start(bf16[512,256]{1,0:T(8,128)(2,1)S(1)} %bitcast.63), channel_id=1, source_target_pairs={{0,2},{1,3},{2,0},{3,1},{4,6},{5,7},{6,4},{7,5},{8,10},{9,11},{10,... | collective-permute-start | bytes 786440 | tf_op jit(solution)/shard_map/ppermute | solution.py:416
  144.8 11.4 %collective-permute-start.31 = (bf16[512,256]{1,0:T(8,128)(2,1)S(1)}, bf16[512,256]{1,0:T(8,128)(2,1)S(1)}, u32[]{:S(2)}, u32[]{:S(2)}) collective-permute-start(bf16[512,256]{1,0:T(8,128)(2,1)S(1)} %bitcast.66), channel_id=1, source_target_pairs={{0,2},{1,3},{2,0},{3,1},{4,6},{5,7},{6,4},{7,5},{8,10},{9,11},{10,... | collective-permute-start | bytes 786440 | tf_op jit(solution)/shard_map/ppermute | solution.py:416
  150.9 8.3 %collective-permute-start.37 = (bf16[512,256]{1,0:T(8,128)(2,1)S(1)}, bf16[512,256]{1,0:T(8,128)(2,1)S(1)}, u32[]{:S(2)}, u32[]{:S(2)}) collective-permute-start(bf16[512,256]{1,0:T(8,128)(2,1)S(1)} %bitcast.67), channel_id=1, source_target_pairs={{0,4},{4,0},{8,12},{12,8},{16,20},{20,16},{24,28},{28,24},{1,5},{5... | collective-permute-start | bytes 786440 | tf_op jit(solution)/shard_map/ppermute | solution.py:416
  156.2 8.3 %collective-permute-start.41 = (bf16[512,256]{1,0:T(8,128)(2,1)S(1)}, bf16[512,256]{1,0:T(8,128)(2,1)S(1)}, u32[]{:S(2)}, u32[]{:S(2)}) collective-permute-start(bf16[512,256]{1,0:T(8,128)(2,1)S(1)} %bitcast.68), channel_id=1, source_target_pairs={{0,2},{1,3},{2,0},{3,1},{4,6},{5,7},{6,4},{7,5},{8,10},{9,11},{10,... | collective-permute-start | bytes 786440 | tf_op jit(solution)/shard_map/ppermute | solution.py:416
  159.2 8.4 %collective-permute-start.28 = (bf16[512,256]{1,0:T(8,128)(2,1)S(1)}, bf16[512,256]{1,0:T(8,128)(2,1)S(1)}, u32[]{:S(2)}, u32[]{:S(2)}) collective-permute-start(bf16[512,256]{1,0:T(8,128)(2,1)S(1)} %fusion.7), channel_id=1, source_target_pairs={{0,2},{1,3},{2,0},{3,1},{4,6},{5,7},{6,4},{7,5},{8,10},{9,11},{10,... | collective-permute-start | bytes 786440 | tf_op jit(solution)/shard_map/ppermute | solution.py:416
  164.5 8.5 %collective-permute-start.32 = (bf16[512,256]{1,0:T(8,128)(2,1)S(1)}, bf16[512,256]{1,0:T(8,128)(2,1)S(1)}, u32[]{:S(2)}, u32[]{:S(2)}) collective-permute-start(bf16[512,256]{1,0:T(8,128)(2,1)S(1)} %fusion.4), channel_id=1, source_target_pairs={{0,4},{4,0},{8,12},{12,8},{16,20},{20,16},{24,28},{28,24},{1,5},{5... | collective-permute-start | bytes 786440 | tf_op jit(solution)/shard_map/ppermute | solution.py:416
  166.0 10.4 %collective-permute-start.36 = (bf16[512,256]{1,0:T(8,128)(2,1)S(1)}, bf16[512,256]{1,0:T(8,128)(2,1)S(1)}, u32[]{:S(2)}, u32[]{:S(2)}) collective-permute-start(bf16[512,256]{1,0:T(8,128)(2,1)S(1)} %bitcast.62), channel_id=1, source_target_pairs={{0,4},{4,0},{8,12},{12,8},{16,20},{20,16},{24,28},{28,24},{1,5},{5... | collective-permute-start | bytes 786440 | tf_op jit(solution)/shard_map/ppermute | solution.py:416
  167.5 10.5 %collective-permute-start.38 = (bf16[512,256]{1,0:T(8,128)(2,1)S(1)}, bf16[512,256]{1,0:T(8,128)(2,1)S(1)}, u32[]{:S(2)}, u32[]{:S(2)}) collective-permute-start(bf16[512,256]{1,0:T(8,128)(2,1)S(1)} %fusion.1), channel_id=1, source_target_pairs={{0,2},{1,3},{2,0},{3,1},{4,6},{5,7},{6,4},{7,5},{8,10},{9,11},{10,... | collective-permute-start | bytes 786440 | tf_op jit(solution)/shard_map/ppermute | solution.py:416
  168.7 12.4 %collective-permute-start.43 = (bf16[512,256]{1,0:T(8,128)(2,1)S(1)}, bf16[512,256]{1,0:T(8,128)(2,1)S(1)}, u32[]{:S(2)}, u32[]{:S(2)}) collective-permute-start(bf16[512,256]{1,0:T(8,128)(2,1)S(1)} %bitcast.61), channel_id=1, source_target_pairs={{0,2},{1,3},{2,0},{3,1},{4,6},{5,7},{6,4},{7,5},{8,10},{9,11},{10,... | collective-permute-start | bytes 786440 | tf_op jit(solution)/shard_map/ppermute | solution.py:416
  173.0 9.6 %collective-permute-start.42 = (bf16[512,256]{1,0:T(8,128)(2,1)S(1)}, bf16[512,256]{1,0:T(8,128)(2,1)S(1)}, u32[]{:S(2)}, u32[]{:S(2)}) collective-permute-start(bf16[512,256]{1,0:T(8,128)(2,1)S(1)} %fusion), channel_id=1, source_target_pairs={{0,4},{4,0},{8,12},{12,8},{16,20},{20,16},{24,28},{28,24},{1,5},{5... | collective-permute-start | bytes 786440 | tf_op jit(solution)/shard_map/ppermute | solution.py:416
  176.5 9.6 %collective-permute-start.29 = (bf16[512,256]{1,0:T(8,128)(2,1)S(1)}, bf16[512,256]{1,0:T(8,128)(2,1)S(1)}, u32[]{:S(2)}, u32[]{:S(2)}) collective-permute-start(bf16[512,256]{1,0:T(8,128)(2,1)S(1)} %fusion.9), channel_id=1, source_target_pairs={{0,8},{4,12},{8,0},{12,4},{16,24},{20,28},{24,16},{28,20},{1,9},{5... | collective-permute-start | bytes 786440 | tf_op jit(solution)/shard_map/ppermute | solution.py:416
  178.1 17.3 %collective-permute-start.34 = (bf16[512,256]{1,0:T(8,128)(2,1)S(1)}, bf16[512,256]{1,0:T(8,128)(2,1)S(1)}, u32[]{:S(2)}, u32[]{:S(2)}) collective-permute-start(bf16[512,256]{1,0:T(8,128)(2,1)S(1)} %fusion.6), channel_id=1, source_target_pairs={{0,16},{4,20},{8,24},{12,28},{16,0},{20,4},{24,8},{28,12},{1,17},{... | collective-permute-start | bytes 786440 | tf_op jit(solution)/shard_map/ppermute | solution.py:416
  179.6 15.7 %collective-permute-start.39 = (bf16[512,256]{1,0:T(8,128)(2,1)S(1)}, bf16[512,256]{1,0:T(8,128)(2,1)S(1)}, u32[]{:S(2)}, u32[]{:S(2)}) collective-permute-start(bf16[512,256]{1,0:T(8,128)(2,1)S(1)} %fusion.3), channel_id=1, source_target_pairs={{0,24},{4,28},{8,16},{12,20},{16,8},{20,12},{24,0},{28,4},{1,25},{... | collective-permute-start | bytes 786440 | tf_op jit(solution)/shard_map/ppermute | solution.py:416
  181.1 21.1 %collective-permute-start.53 = (f32[136,172]{1,0:T(8,128)S(1)}, f32[136,172]{1,0:T(8,128)S(1)}, u32[]{:S(2)}, u32[]{:S(2)}) collective-permute-start(f32[136,172]{1,0:T(8,128)S(1)} %add.276), channel_id=1, source_target_pairs={{0,16},{4,20},{8,24},{12,28},{16,0},{20,4},{24,8},{28,12},{1,17},{... | collective-permute-start | bytes 280712 | tf_op jit(solution)/shard_map/ppermute | solution.py:416
  202.2 6.0 %collective-permute-start.56 = (f32[136,172]{1,0:T(8,128)S(1)}, f32[136,172]{1,0:T(8,128)S(1)}, u32[]{:S(2)}, u32[]{:S(2)}) collective-permute-start(f32[136,172]{1,0:T(8,128)S(1)} %add.277), channel_id=1, source_target_pairs={{0,3},{1,2},{2,1},{3,0},{4,7},{5,6},{6,5},{7,4},{8,11},{9,10},{10,... | collective-permute-start | bytes 280712 | tf_op jit(solution)/shard_map/ppermute | solution.py:416
  202.3 9.0 %collective-permute-start.55 = (f32[136,172]{1,0:T(8,128)S(1)}, f32[136,172]{1,0:T(8,128)S(1)}, u32[]{:S(2)}, u32[]{:S(2)}) collective-permute-start(f32[136,172]{1,0:T(8,128)S(1)} %add.277), channel_id=1, source_target_pairs={{0,2},{1,3},{2,0},{3,1},{4,6},{5,7},{6,4},{7,5},{8,10},{9,11},{10,... | collective-permute-start | bytes 280712 | tf_op jit(solution)/shard_map/ppermute | solution.py:416
  203.8 7.4 %collective-permute-start.54 = (f32[136,172]{1,0:T(8,128)S(1)}, f32[136,172]{1,0:T(8,128)S(1)}, u32[]{:S(2)}, u32[]{:S(2)}) collective-permute-start(f32[136,172]{1,0:T(8,128)S(1)} %add.277), channel_id=1, source_target_pairs={{0,1},{1,0},{2,3},{3,2},{4,5},{5,4},{6,7},{7,6},{8,9},{9,8},{10,11... | collective-permute-start | bytes 280712 | tf_op jit(solution)/shard_map/ppermute | solution.py:416
  205.1 7.7 %collective-permute-start.45 = (f32[1,72,256]{2,1,0:T(8,128)S(1)}, f32[1,72,256]{2,1,0:T(8,128)S(1)}, u32[]{:S(2)}, u32[]{:S(2)}) collective-permute-start(f32[1,72,256]{2,1,0:T(8,128)S(1)} %slice.191), channel_id=1, source_target_pairs={{0,2},{1,3},{2,0},{3,1},{4,6},{5,7},{6,4},{7,5},{8,10},{9,11},{10,... | collective-permute-start | bytes 221192 | tf_op jit(solution)/shard_map/ppermute | solution.py:416
  (37 other events, 279.1 us)

commit v4 on v3

--- a/solution.py
+++ b/solution.py
@@ -1,3 +1,4 @@
+import functools
 import math
 
 import jax
@@ -15,6 +16,14 @@
 
 def group_of(count, most):
     return math.gcd(count, most)
+
+
+def products_cost(total, side, width):
+    return pl.CostEstimate(
+        flops=8 * total * side * side * width,
+        bytes_accessed=2 * total * side * side,
+        transcendentals=0,
+    )
 
 
 def first_layer(features_t, tiles, dst_ids, src_ids, me, blocks, owners):
@@ -84,7 +93,7 @@
 
 def hidden_layer(parts, weights, bias):
     count = len(parts)
-    rows = parts[0].shape[1]
+    features, rows = parts[0].shape
     width = weights[0].shape[1]
 
     def kernel(*refs):
@@ -92,12 +101,18 @@
         pre = jnp.zeros((rows, width), F32)
         for r in range(count):
             pre = pre + lax.dot_general(
-                refs[r][...], refs[count + r][...], (((0,), (0,)), ((), ())),
+                refs[r][...], refs[count + r][:features, :], (((0,), (0,)), ((), ())),
                 preferred_element_type=F32,
             )
         pre = pre + b_ref[...]
         pre_ref[...] = pre
-        hidden_ref[...] = jnp.maximum(pre, 0.0).astype(BF16)
+        hidden_ref[:rows, :] = jnp.maximum(pre, 0.0).astype(BF16)
+        row = lax.broadcasted_iota(jnp.int32, (16, width), 0)
+        lists = jnp.zeros((16, width), F32)
+        for r in range(count):
+            one = refs[count + r][features:, :].astype(F32)[:1]
+            lists = jnp.where(row == r, one, lists)
+        hidden_ref[rows:, :] = lists.astype(BF16)
 
     return pl.pallas_call(
         kernel,
@@ -105,7 +120,7 @@
         out_specs=[VMEM] * 2,
         out_shape=[
             jax.ShapeDtypeStruct((rows, width), F32),
-            jax.ShapeDtypeStruct((rows, width), BF16),
+            jax.ShapeDtypeStruct((rows + 16, width), BF16),
         ],
         compiler_params=BIG,
         name="hidden_layer",
@@ -167,10 +182,9 @@
     width = hidden.shape[1]
     count = len(pools)
     per_pool = pools[0].shape[0]
-    unit = 8 * n_feat
-    share = -(-(2 * width + 8) // unit) * 8
-    half = n_feat // 2
-    classes = w_self.shape[1]
+    classes = w_self.shape[0]
+    second = -(-classes // 8) * 8
+    share = -(-(2 * second + 8) // (8 * n_feat)) * 8
     step = group_of(total, 32)
     unroll = group_of(step, 32)
     steps = total // step
@@ -182,7 +196,8 @@
         labels_ref, *refs,
     ):
         pool_refs = refs[:count]
-        even_ref, odd_ref, gnum_ref, own_ref, acc, pool_ref, sums, sems = refs[count:]
+        third_refs = refs[count : count + n_feat]
+        gnum_ref, own_ref, acc, pool_ref, sums_ref, sems = refs[count + n_feat :]
         i = pl.program_id(0)
 
         @pl.when(i == 0)
@@ -196,7 +211,6 @@
             for copy in copies:
                 copy.start()
             acc[...] = jnp.zeros_like(acc)
-            sums[...] = jnp.zeros_like(sums)
             for copy in copies:
                 copy.wait()
 
@@ -219,8 +233,8 @@
 
         @pl.when(i == steps - 1)
         def _():
-            gws = jnp.zeros((width, classes), F32)
-            gwn = jnp.zeros((width, classes), F32)
+            gws = jnp.zeros((classes, width), F32)
+            gwn = jnp.zeros((classes, width), F32)
             gb = jnp.zeros((1, classes), F32)
             for b in range(blocks):
                 rows = slice(b * side, (b + 1) * side)
@@ -228,8 +242,8 @@
                 mean = (acc[b] / under).astype(BF16)
                 own = hidden_ref[rows, :]
                 logits = (
-                    jnp.dot(own, ws_ref[...], preferred_element_type=F32)
-                    + jnp.dot(mean, wn_ref[...], preferred_element_type=F32)
+                    lax.dot_general(own, ws_ref[...], last, preferred_element_type=F32)
+                    + lax.dot_general(mean, wn_ref[...], last, preferred_element_type=F32)
                     + bias_ref[...]
                 )
                 expo = jnp.exp(logits - jnp.max(logits, axis=1, keepdims=True))
@@ -239,28 +253,24 @@
                 grad = (prob - onehot) * scale
                 glog = grad.astype(BF16)
                 gb = gb + jnp.sum(grad, axis=0, keepdims=True)
-                gws = gws + lax.dot_general(own, glog, lead, preferred_element_type=F32)
-                gwn = gwn + lax.dot_general(mean, glog, lead, preferred_element_type=F32)
-                back = lax.dot_general(glog, wn_ref[...], last, preferred_element_type=F32)
+                gws = gws + lax.dot_general(glog, own, lead, preferred_element_type=F32)
+                gwn = gwn + lax.dot_general(glog, mean, lead, preferred_element_type=F32)
+                back = jnp.dot(glog, wn_ref[...], preferred_element_type=F32)
                 gnum_ref[b] = (back / under).astype(BF16)
-                own_ref[rows, :] = lax.dot_general(
-                    glog, ws_ref[...], last, preferred_element_type=F32
-                )
-            sums[:width, :] = gws
-            sums[width : 2 * width, :] = gwn
-            sums[2 * width : 2 * width + 8, :] = jnp.broadcast_to(gb, (8, classes))
+                own_ref[rows, :] = jnp.dot(glog, ws_ref[...], preferred_element_type=F32)
+            sums_ref[...] = jnp.zeros_like(sums_ref)
+            sums_ref[:classes, :] = gws
+            sums_ref[second : second + classes, :] = gwn
+            sums_ref[2 * second : 2 * second + 1, :classes] = gb
             for r in range(n_feat):
                 start = pl.multiple_of((me_s[0] ^ r) * share, 8)
-                target = odd_ref if r % 2 else even_ref
-                target[r // 2] = sums[pl.ds(start, share), :]
+                third_refs[r][...] = sums_ref[pl.ds(start, share), :]
 
     def whole(*shape):
         return pl.BlockSpec(shape, lambda i, *_: (0,) * len(shape))
 
     rows = blocks * side
-    out = [
-        ((half, share, classes), F32),
-        ((half, share, classes), F32),
+    out = [((share, width), F32)] * n_feat + [
         ((blocks, side, width), BF16),
         ((rows, width), F32),
     ]
@@ -272,9 +282,9 @@
             in_specs=[
                 pl.BlockSpec((step, side, side), lambda i, *_: (i, 0, 0)),
                 whole(blocks, side, side),
-                whole(rows, width),
-                whole(width, classes),
-                whole(width, classes),
+                whole(rows + 16, width),
+                whole(classes, width),
+                whole(classes, width),
                 whole(1, classes),
                 whole(rows, 1),
             ]
@@ -283,16 +293,17 @@
             scratch_shapes=[
                 pltpu.VMEM((blocks, side, width), F32),
                 pltpu.VMEM((count * per_pool, side, width), BF16),
-                pltpu.VMEM((n_feat * share, classes), F32),
+                pltpu.VMEM((n_feat * share, width), F32),
                 pltpu.SemaphoreType.DMA((count,)),
             ],
         ),
         out_shape=[jax.ShapeDtypeStruct(s, d) for s, d in out],
         compiler_params=BIG,
+        cost_estimate=products_cost(total, side, width),
         name="output_layer",
     )(
         dst_ids, src_ids, place, me, tiles, weight, hidden, w_self, w_neigh,
-        bias.reshape(1, classes), labels.reshape(rows, 1), *pools,
+        bias.reshape(1, classes), labels, *pools,
     )
 
 
@@ -374,6 +385,7 @@
         ),
         out_shape=[jax.ShapeDtypeStruct(shape, BF16)] * arrays,
         compiler_params=BIG,
+        cost_estimate=products_cost(total, side, width),
         name="slot_gradients",
     )(dst_ids, src_ids, owners, mine, tiles, gnum)
 
@@ -425,10 +437,10 @@
     return value[0]
 
 
-def gather_blocks(value, planes, across, beside):
+def gather_blocks(value, planes, across, rows, beside):
     n_dom = lax.axis_size("dom")
     down = lax.axis_size("feat") // 2
-    held = []
+    held, tails = [], []
     shifted = [value] + [swap(value, "dom", across * k) for k in range(1, planes)]
     for k, own in enumerate(shifted):
         if k > 0:
@@ -443,8 +455,9 @@
                     pieces.append(swap(aside[i], "feat", 2 * j))
                 else:
                     pieces.append(swap(below[j], "dom", i))
-        held.append(jnp.concatenate(pieces))
-    return held + [swap(piece, "feat", 1) for piece in held]
+        held.append(jnp.concatenate([piece[:rows] for piece in pieces]))
+        tails += [piece[rows:] for piece in aside]
+    return held + [swap(piece, "feat", 1) for piece in held], jnp.stack(tails)
 
 
 def total_of(values):
@@ -496,7 +509,6 @@
     inputs_t, tiles_first, first_dst, first_src, w1_self, w1_neigh, bias_first, fetch_ids,
     tiles_out, out_dst, out_src, output_self_weight, output_neighbour_weight, bias_out, labels,
 ):
-    every = ("dom", "feat")
     n_feat = lax.axis_size("feat")
     devices = lax.axis_size("dom") * n_feat
     side = tiles_out.shape[1]
@@ -512,37 +524,46 @@
     planes = math.gcd(lax.axis_size("dom"), 4)
     across = lax.axis_size("dom") // planes
 
-    mine = lax.all_to_all(fetch_ids[:, 0, :], every, split_axis=0, concat_axis=0, tiled=True)
-    weights = jnp.concatenate([w1_neigh, w1_self])
+    listed = jnp.pad(
+        fetch_ids.reshape(1, -1).astype(BF16), ((0, 15), (0, width - devices * slots_peer))
+    )
+    weights = jnp.concatenate([w1_neigh, w1_self, listed])
     weights = [weights] + [swap(weights, "feat", r) for r in range(1, n_feat)]
     parts = first_layer(inputs_t, tiles_first, first_dst, first_src, me, n_feat * blocks, n_feat)
     parts = [parts[0]] + [swap(parts[r], "feat", r) for r in range(1, n_feat)]
-    weights[0], mine = lax.optimization_barrier((weights[0], mine))
     pre, hidden = hidden_layer(parts, weights, bias_first.reshape(1, width))
-    weight = row_weights(tiles_out, out_dst, blocks)
-    pools = gather_blocks(hidden, planes, across, weight)
-    pools = [pool.reshape(-1, side, width) for pool in pools]
-    owner = jnp.arange(devices, dtype=jnp.int32)[:, None]
-    off_dom = (owner // n_feat) ^ me_dom
-    off_feat = (owner % n_feat) ^ me_feat
-    place = (off_feat % 2) * planes + off_dom // across
-    place = (place * (n_feat // 2) + off_feat // 2) * across + off_dom % across
-    place = (place * blocks + mine).reshape(-1)
-    even, odd, gnum, own = output_layer(
-        tiles_out, out_dst, out_src, place, me, pools, weight, hidden, output_self_weight,
-        output_neighbour_weight, bias_out, labels, scale, n_feat,
-    )
-    third = doubling_sum(feat_sum(even, odd), "dom")
-    third = jnp.stack([third] + [swap(third, "feat", r) for r in range(1, n_feat)])
-    third = jnp.take(third, jnp.arange(n_feat) ^ me_feat, axis=0).reshape(-1, classes)
+    hidden, dst = lax.optimization_barrier((hidden, out_dst))
+    weight = row_weights(tiles_out, dst, blocks)
     index = jnp.arange(devices, dtype=jnp.int32)
     plane = devices // (2 * planes)
     to_dom = me_dom ^ (index // plane % planes * across + index % across)
     to_feat = me_feat ^ (index % plane // across * 2 + index // (plane * planes))
     owners = (to_dom * n_feat + to_feat).astype(jnp.int32)
+    here = me_dom * n_feat + me_feat
+    pools, lists = gather_blocks(hidden, planes, across, rows_dev, weight)
+    pools = [pool.reshape(-1, side, width) for pool in pools]
+    mine = lax.dynamic_slice_in_dim(lists[:, :n_feat], here * slots_peer, slots_peer, axis=2)
+    mine = mine.reshape(devices, slots_peer).astype(jnp.int32)
+    mine = jnp.take(mine, index ^ here, axis=0)
+    off = index[:, None] ^ here
+    place = off % 2 * planes + off // n_feat // across
+    place = (place * (n_feat // 2) + off % n_feat // 2) * across + off // n_feat % across
+    place = (place * blocks + mine).reshape(-1)
+    mine = mine.reshape(-1)
+    column = labels.reshape(rows_dev, 1)
+    *third, gnum, own = output_layer(
+        tiles_out, out_dst, out_src, place, me, pools, weight, hidden, output_self_weight.T,
+        output_neighbour_weight.T, bias_out, column, scale, n_feat,
+    )
+    third = [third[0]] + [swap(third[r], "feat", r) for r in range(1, n_feat)]
     arrays = slot_gradients(
-        tiles_out, out_dst, out_src, owners, mine.reshape(-1), gnum, 2 * planes
-    )
+        tiles_out, out_dst, out_src, owners, mine, gnum, 2 * planes
+    )
+    arrays, third = lax.optimization_barrier((arrays, third))
+    third = doubling_sum(functools.reduce(jnp.add, third), "dom")
+    third = jnp.stack([third] + [swap(third, "feat", r) for r in range(1, n_feat)])
+    third = jnp.take(third, jnp.arange(n_feat) ^ me_feat, axis=0).reshape(-1, width)
+    second = -(-classes // 8) * 8
     terms = return_blocks(arrays, planes, across)
     even, odd = first_gradients(terms, own, pre, parts)
     last = doubling_sum(feat_sum(even, odd), "dom")
@@ -551,9 +572,9 @@
         last[features:edge],
         last[:features],
         last[edge],
-        third[:width],
-        third[width : 2 * width],
-        third[2 * width],
+        third[:classes].T,
+        third[second : second + classes].T,
+        third[2 * second, :classes],
     )
 
 

time: 230 us -> 223 us (0.970)
  waiting for transfers between devices: 80.2 us -> 95.1 us
  blocking collectives: 13 us -> 0 us
  starting transfers between devices: 57.3 us -> 47.2 us
  other arithmetic: 4.61 us -> 9.04 us
  local copies, waits for them, and re-layouts: 12.2 us -> 8.77 us
    ppermute x57 -> x58, waiting for transfers between devices: 80.2 us -> 95.1 us  [swap(): lax.ppermute(value, axis, [(k, k ^ mask) for k in range(lax.axis_size(axi...]
    all_to_all x1 -> x0, blocking collectives: 13 us -> none  [on_device(): lax.all_to_all(fetch_ids[:, 0, :], every, split_axis=0, concat_axis=0, ti...]
    ppermute x57 -> x58, starting transfers between devices: 57.3 us -> 47.2 us  [swap(): lax.ppermute(value, axis, [(k, k ^ mask) for k in range(lax.axis_size(axi...]
    unnamed x66 -> x49, local copies, waits for them, and re-layouts: 5.49 us -> 2.21 us
  transfers between devices with their start and end apart: 57 -> 58, of which waited for: 24 -> 24; matrix products, arithmetic and copies ran while one was open for 6% -> 6% of each run, Pallas kernels for 6% -> 17%
where the time goes in v4:
time: 223 us; the launch traced here: 222 us
  waiting for transfers between devices  95.1 us (43%)
  Pallas kernels  60.9 us (27%)
  starting transfers between devices  47.2 us (21%)
  other arithmetic  9.04 us (4%)
  local copies, waits for them, and re-layouts  8.77 us (4%)
    ppermute x58, waiting for transfers between devices, swap(): lax.ppermute(value, axis, [(k, k ^ mask) for k in range(lax.axis_size(axi...  95.1 us
    ppermute x58, starting transfers between devices, swap(): lax.ppermute(value, axis, [(k, k ^ mask) for k in range(lax.axis_size(axi...  47.2 us
    pallas_call x1, Pallas kernels, output_layer(): pl.pallas_call(kernel, grid_spec=pltpu.PrefetchScalarGridSpec(num_scalar_...  20.6 us
    pallas_call x1, Pallas kernels, slot_gradients(): pl.pallas_call(kernel, grid_spec=pltpu.PrefetchScalarGridSpec(num_scalar_...  19.2 us
    pallas_call x1, Pallas kernels, row_weights(): pl.pallas_call(kernel, grid_spec=pltpu.PrefetchScalarGridSpec(num_scalar_...  11.1 us
    pallas_call x1, Pallas kernels, first_layer(): pl.pallas_call(kernel, grid_spec=pltpu.PrefetchScalarGridSpec(num_scalar_...  4.63 us
  transfers between devices with their start and end apart: 58, of which 24 were waited for; matrix products, arithmetic and copies ran while one was open for 6% of the time, Pallas kernels for 17%

profile of v4, /device:TPU:0, one launch (start us, length us, event | category | flops | bytes accessed | tf_op | source)
XLA Modules:
  0.0 222.2 jit_solution(15789547227160887232)
XLA Ops:
  2.8 2.6 %collective-permute-start.4 = (bf16[80,256]{1,0:T(8,128)(2,1)S(1)}, bf16[80,256]{1,0:T(8,128)(2,1)S(1)}, u32[]{:S(2)}, u32[]{:S(2)}) collective-permute-start(bf16[80,256]{1,0:T(8,128)(2,1)S(1)} %fusion.12.refs_4_), channel_id=1, source_target_pairs={{0,2},{1,3},{2,0},{3,1},{4,6},{5,7},{6,4},{7,5},{8,10},{9,11},{10,... | collective-permute-start | bytes 122888 | tf_op jit(solution)/shard_map/ppermute | solution.py:428
  5.5 4.6 %first_layer.1 = (bf16[64,512]{1,0:T(8,128)(2,1)}, bf16[64,512]{1,0:T(8,128)(2,1)}, bf16[64,512]{1,0:T(8,128)(2,1)}, bf16[64,512]{1,0:T(8,128)(2,1)}) custom-call(s32[64]{0:T(128)} %dst_s.3, s32[64]{0:T(128)} %src_s.3, s32[1]{0:T(128)} %bitcast.me_s, bf16[64,128,128]{2,1,0:T(8,128)(2,1)} %tile_ref.4, bf16[32,4096]{1,0:T(8,128)(2,1)} %feat_ref.1), custom_call_target="tpu_custom_call" | custom-call | tf_op jit(solution)/shard_map/first_layer/pallas_call | solution.py:76
  10.2 1.9 collective-permute-start.1
  12.4 2.5 %collective-permute-done.1.refs_2_.refs_10_ = bf16[64,512]{1,0:T(8,128)(2,1)S(1)} collective-permute-done((bf16[64,512]{1,0:T(8,128)(2,1)}, bf16[64,512]{1,0:T(8,128)(2,1)S(1)}, u32[]{:S(2)}, u32[]{:S(2)}) %collective-permute-start.1) | collective-permute-done | bytes 65568 | tf_op jit(solution)/shard_map/ppermute | solution.py:428
  14.9 1.9 collective-permute-done.2.refs_3_.refs_11_
  17.5 2.3 %hidden_layer.1 = (f32[512,256]{1,0:T(8,128)}, bf16[528,256]{1,0:T(8,128)(2,1)}) custom-call(bf16[64,512]{1,0:T(8,128)(2,1)} %get-tuple-element.43.refs_0_.refs_8_, bf16[64,512]{1,0:T(8,128)(2,1)} %copy-done.6, bf16[64,512]{1,0:T(8,128)(2,1)} %copy-done.7, bf16[64,512]{1,0:T(8,128)(2,1)} %copy-done.8, bf16[80,256]{1,0:T(8,128)(2,1)} %copy-done.14, ...), custom_call_target="tpu_custom_call" | custom-call | tf_op jit(solution)/shard_map/hidden_layer/pallas_call | solution.py:117
  19.8 1.6 collective-permute-start.7
  21.4 1.5 collective-permute-start.6
  22.9 2.6 %collective-permute-start.9 = (bf16[528,256]{1,0:T(8,128)(2,1)}, bf16[528,256]{1,0:T(8,128)(2,1)S(1)}, u32[]{:S(2)}, u32[]{:S(2)}) collective-permute-start(bf16[528,256]{1,0:T(8,128)(2,1)} %get-tuple-element.48.hidden_ref), channel_id=1, source_target_pairs={{0,16},{4,20},{8,24},{12,28},{16,0},{20,4},{24,8},{28,12},{1,17},{... | collective-permute-start | bytes 811016 | tf_op jit(solution)/shard_map/ppermute | solution.py:428
  29.6 11.1 %row_weights.1.weight_ref = f32[4,128,128]{2,1,0:T(8,128)} custom-call(s32[384]{0:T(512)} %dst_s.6, bf16[384,128,128]{2,1,0:T(8,128)(2,1)} %tile_ref.7), custom_call_target="tpu_custom_call" | custom-call | flops 12582912 | bytes 12582912 | tf_op jit(solution)/shard_map/row_weights/pallas_call | solution.py:158
  40.7 1.4 collective-permute-start.15
  42.7 2.3 %collective-permute-done.9 = bf16[528,256]{1,0:T(8,128)(2,1)S(1)} collective-permute-done((bf16[528,256]{1,0:T(8,128)(2,1)}, bf16[528,256]{1,0:T(8,128)(2,1)S(1)}, u32[]{:S(2)}, u32[]{:S(2)}) %collective-permute-start.9) | collective-permute-done | bytes 270368 | tf_op jit(solution)/shard_map/ppermute | solution.py:428
  46.1 1.6 collective-permute-start.12
  47.7 6.3 %collective-permute-done.14 = bf16[528,256]{1,0:T(8,128)(2,1)S(1)} collective-permute-done((bf16[528,256]{1,0:T(8,128)(2,1)S(1)}, bf16[528,256]{1,0:T(8,128)(2,1)S(1)}, u32[]{:S(2)}, u32[]{:S(2)}) %collective-permute-start.14) | collective-permute-done | bytes 270368 | tf_op jit(solution)/shard_map/ppermute | solution.py:428
  54.0 1.1 collective-permute-start.17
  55.1 1.0 collective-permute-start.19
  58.0 11.2 %collective-permute-done.19 = bf16[528,256]{1,0:T(8,128)(2,1)S(1)} collective-permute-done((bf16[528,256]{1,0:T(8,128)(2,1)S(1)}, bf16[528,256]{1,0:T(8,128)(2,1)S(1)}, u32[]{:S(2)}, u32[]{:S(2)}) %collective-permute-start.19) | collective-permute-done | bytes 270368 | tf_op jit(solution)/shard_map/ppermute | solution.py:428
  70.3 1.8 collective-permute-done.18
  72.4 5.8 %collective-permute-done.20 = bf16[528,256]{1,0:T(8,128)(2,1)S(1)} collective-permute-done((bf16[528,256]{1,0:T(8,128)(2,1)S(1)}, bf16[528,256]{1,0:T(8,128)(2,1)S(1)}, u32[]{:S(2)}, u32[]{:S(2)}) %collective-permute-start.20) | collective-permute-done | bytes 270368 | tf_op jit(solution)/shard_map/ppermute | solution.py:428
  78.2 1.1 pad_maximum_fusion.3
  80.7 1.6 collective-permute-done.24
  82.3 20.6 %output_layer.1 = (f32[96,256]{1,0:T(8,128)}, f32[96,256]{1,0:T(8,128)}, f32[96,256]{1,0:T(8,128)}, f32[96,256]{1,0:T(8,128)}, bf16[4,128,256]{2,1,0:T(8,128)(2,1)}, /*index=5*/f32[512,256]{1,0:T(8,128)}) custom-call(s32[384]{0:T(512)} %dst_s.6, s32[384]{0:T(512)} %src_s.5, s32[64]{0:T(128)} %add.283.place_s, s32[1]{0:T(128)} %bitcast.me_s, ...), custom_call_target="tpu_custom_call" | custom-call | flops 12884901888 | bytes 12582912 | tf_op jit(solution)/shard_map/output_layer/pallas_call | solution.py:277
  104.9 19.2 %slot_gradients.1 = (bf16[16,128,256]{2,1,0:T(8,128)(2,1)}, bf16[16,128,256]{2,1,0:T(8,128)(2,1)}, bf16[16,128,256]{2,1,0:T(8,128)(2,1)}, bf16[16,128,256]{2,1,0...) custom-call(s32[384]{0:T(512)} %dst_s.6, ...), custom_call_target="tpu_custom_call" | custom-call | flops 12884901888 | bytes 12582912 | tf_op jit(solution)/shard_map/slot_gradients/pallas_call | solution.py:370
  125.2 1.9 collective-permute-done.43
  127.2 2.2 add_convert_fusion
  130.2 1.2 collective-permute-start.46
  132.4 1.5 collective-permute-start.39
  135.4 3.1 %collective-permute-done.44 = bf16[512,256]{1,0:T(8,128)(2,1)S(1)} collective-permute-done((bf16[512,256]{1,0:T(8,128)(2,1)S(1)}, bf16[512,256]{1,0:T(8,128)(2,1)S(1)}, u32[]{:S(2)}, u32[]{:S(2)}) %collective-permute-start.44) | collective-permute-done | bytes 262176 | tf_op jit(solution)/shard_map/ppermute | solution.py:428
  139.4 1.6 collective-permute-done.40
  141.7 8.1 %collective-permute-done.34 = bf16[512,256]{1,0:T(8,128)(2,1)S(1)} collective-permute-done((bf16[512,256]{1,0:T(8,128)(2,1)S(1)}, bf16[512,256]{1,0:T(8,128)(2,1)S(1)}, u32[]{:S(2)}, u32[]{:S(2)}) %collective-permute-start.34) | collective-permute-done | bytes 262176 | tf_op jit(solution)/shard_map/ppermute | solution.py:428
  151.7 1.5 collective-permute-start.29
  153.3 7.2 %collective-permute-done.41 = bf16[512,256]{1,0:T(8,128)(2,1)S(1)} collective-permute-done((bf16[512,256]{1,0:T(8,128)(2,1)S(1)}, bf16[512,256]{1,0:T(8,128)(2,1)S(1)}, u32[]{:S(2)}, u32[]{:S(2)}) %collective-permute-start.41) | collective-permute-done | bytes 262176 | tf_op jit(solution)/shard_map/ppermute | solution.py:428
  162.0 3.5 %collective-permute-start.42 = (bf16[512,256]{1,0:T(8,128)(2,1)S(1)}, bf16[512,256]{1,0:T(8,128)(2,1)S(1)}, u32[]{:S(2)}, u32[]{:S(2)}) collective-permute-start(bf16[512,256]{1,0:T(8,128)(2,1)S(1)} %fusion.3), channel_id=1, source_target_pairs={{0,24},{4,28},{8,16},{12,20},{16,8},{20,12},{24,0},{28,4},{1,25},{... | collective-permute-start | bytes 786440 | tf_op jit(solution)/shard_map/ppermute | solution.py:428
  166.0 2.2 collective-permute-done.31
  169.7 3.4 %collective-permute-done.42.refs_2_ = bf16[512,256]{1,0:T(8,128)(2,1)S(1)} collective-permute-done((bf16[512,256]{1,0:T(8,128)(2,1)S(1)}, bf16[512,256]{1,0:T(8,128)(2,1)S(1)}, u32[]{:S(2)}, u32[]{:S(2)}) %collective-permute-start.42) | collective-permute-done | bytes 262176 | tf_op jit(solution)/shard_map/ppermute | solution.py:428
  173.1 12.9 %collective-permute-done.37.refs_1_ = bf16[512,256]{1,0:T(8,128)(2,1)S(1)} collective-permute-done((bf16[512,256]{1,0:T(8,128)(2,1)S(1)}, bf16[512,256]{1,0:T(8,128)(2,1)S(1)}, u32[]{:S(2)}, u32[]{:S(2)}) %collective-permute-start.37) | collective-permute-done | bytes 262176 | tf_op jit(solution)/shard_map/ppermute | solution.py:428
  186.9 2.9 %first_gradients.1 = (f32[2,72,256]{2,1,0:T(8,128)}, f32[2,72,256]{2,1,0:T(8,128)}) custom-call(bf16[512,256]{1,0:T(8,128)(2,1)} %copy-done.13, bf16[512,256]{1,0:T(8,128)(2,1)} %copy-done.12, bf16[512,256]{1,0:T(8,128)(2,1)} %copy-done.11, bf16[512,256]{1,0:T(8,128)(2,1)} %bitcast.97, bf16[512,256]{1,0:T(8,128)(2,1)} %copy-done.10, ...), custom_call_target="tpu_custom_call" | custom-call | tf_op jit(solution)/shard_map/first_gradients/pallas_call | solution.py:417
  190.1 5.2 %collective-permute-done.53 = f32[96,256]{1,0:T(8,128)S(1)} collective-permute-done((f32[96,256]{1,0:T(8,128)S(1)}, f32[96,256]{1,0:T(8,128)S(1)}, u32[]{:S(2)}, u32[]{:S(2)}) %collective-permute-start.53) | collective-permute-done | bytes 98336 | tf_op jit(solution)/shard_map/ppermute | solution.py:428
  195.3 1.4 collective-permute-start.54
  197.6 1.3 collective-permute-start.48
  198.9 3.8 %collective-permute-done.54 = f32[96,256]{1,0:T(8,128)S(1)} collective-permute-done((f32[96,256]{1,0:T(8,128)S(1)}, f32[96,256]{1,0:T(8,128)S(1)}, u32[]{:S(2)}, u32[]{:S(2)}) %collective-permute-start.54) | collective-permute-done | bytes 98336 | tf_op jit(solution)/shard_map/ppermute | solution.py:428
  202.8 1.4 collective-permute-start.56
  204.7 1.5 collective-permute-start.49
  206.2 2.2 %collective-permute-done.56 = f32[96,256]{1,0:T(8,128)S(1)} collective-permute-done((f32[96,256]{1,0:T(8,128)S(1)}, f32[96,256]{1,0:T(8,128)S(1)}, u32[]{:S(2)}, u32[]{:S(2)}) %collective-permute-start.56) | collective-permute-done | bytes 98336 | tf_op jit(solution)/shard_map/ppermute | solution.py:428
  208.5 1.2 collective-permute-done.57
  210.5 4.3 %collective-permute-done.50 = f32[72,256]{1,0:T(8,128)S(1)} collective-permute-done((f32[72,256]{1,0:T(8,128)S(1)}, f32[72,256]{1,0:T(8,128)S(1)}, u32[]{:S(2)}, u32[]{:S(2)}) %collective-permute-start.50) | collective-permute-done | bytes 73760 | tf_op jit(solution)/shard_map/ppermute | solution.py:428
  214.8 1.4 collective-permute-start.51
  217.5 3.5 %collective-permute-done.51 = f32[72,256]{1,0:T(8,128)S(1)} collective-permute-done((f32[72,256]{1,0:T(8,128)S(1)}, f32[72,256]{1,0:T(8,128)S(1)}, u32[]{:S(2)}, u32[]{:S(2)}) %collective-permute-start.51) | collective-permute-done | bytes 73760 | tf_op jit(solution)/shard_map/ppermute | solution.py:428
  (196 shorter events, 32.8 us)
Async XLA Ops:
  2.3 9.9 %collective-permute-start.3 = (bf16[80,256]{1,0:T(8,128)(2,1)S(1)}, bf16[80,256]{1,0:T(8,128)(2,1)S(1)}, u32[]{:S(2)}, u32[]{:S(2)}) collective-permute-start(bf16[80,256]{1,0:T(8,128)(2,1)S(1)} %fusion.12.refs_4_), channel_id=1, source_target_pairs={{0,1},{1,0},{2,3},{3,2},{4,5},{5,4},{6,7},{7,6},{8,9},{9,8},{10,11... | collective-permute-start | bytes 122888 | tf_op jit(solution)/shard_map/ppermute | solution.py:428
  2.8 9.5 %collective-permute-start.4 = (bf16[80,256]{1,0:T(8,128)(2,1)S(1)}, bf16[80,256]{1,0:T(8,128)(2,1)S(1)}, u32[]{:S(2)}, u32[]{:S(2)}) collective-permute-start(bf16[80,256]{1,0:T(8,128)(2,1)S(1)} %fusion.12.refs_4_), channel_id=1, source_target_pairs={{0,2},{1,3},{2,0},{3,1},{4,6},{5,7},{6,4},{7,5},{8,10},{9,11},{10,... | collective-permute-start | bytes 122888 | tf_op jit(solution)/shard_map/ppermute | solution.py:428
  5.4 7.0 %collective-permute-start.5 = (bf16[80,256]{1,0:T(8,128)(2,1)S(1)}, bf16[80,256]{1,0:T(8,128)(2,1)S(1)}, u32[]{:S(2)}, u32[]{:S(2)}) collective-permute-start(bf16[80,256]{1,0:T(8,128)(2,1)S(1)} %fusion.12.refs_4_), channel_id=1, source_target_pairs={{0,3},{1,2},{2,1},{3,0},{4,7},{5,6},{6,5},{7,4},{8,11},{9,10},{10,... | collective-permute-start | bytes 122888 | tf_op jit(solution)/shard_map/ppermute | solution.py:428
  19.8 20.9 %collective-permute-start.7 = (bf16[528,256]{1,0:T(8,128)(2,1)}, bf16[528,256]{1,0:T(8,128)(2,1)S(1)}, u32[]{:S(2)}, u32[]{:S(2)}) collective-permute-start(bf16[528,256]{1,0:T(8,128)(2,1)} %get-tuple-element.48.hidden_ref), channel_id=1, source_target_pairs={{0,8},{4,12},{8,0},{12,4},{16,24},{20,28},{24,16},{28,20},{1,9},{5... | collective-permute-start | bytes 811016 | tf_op jit(solution)/shard_map/ppermute | solution.py:428
  21.4 20.7 %collective-permute-start.6 = (bf16[528,256]{1,0:T(8,128)(2,1)}, bf16[528,256]{1,0:T(8,128)(2,1)S(1)}, u32[]{:S(2)}, u32[]{:S(2)}) collective-permute-start(bf16[528,256]{1,0:T(8,128)(2,1)} %get-tuple-element.48.hidden_ref), channel_id=1, source_target_pairs={{0,4},{4,0},{8,12},{12,8},{16,20},{20,16},{24,28},{28,24},{1,5},{5... | collective-permute-start | bytes 811016 | tf_op jit(solution)/shard_map/ppermute | solution.py:428
  22.9 22.1 %collective-permute-start.9 = (bf16[528,256]{1,0:T(8,128)(2,1)}, bf16[528,256]{1,0:T(8,128)(2,1)S(1)}, u32[]{:S(2)}, u32[]{:S(2)}) collective-permute-start(bf16[528,256]{1,0:T(8,128)(2,1)} %get-tuple-element.48.hidden_ref), channel_id=1, source_target_pairs={{0,16},{4,20},{8,24},{12,28},{16,0},{20,4},{24,8},{28,12},{1,17},{... | collective-permute-start | bytes 811016 | tf_op jit(solution)/shard_map/ppermute | solution.py:428
  27.0 18.5 %collective-permute-start.11 = (bf16[528,256]{1,0:T(8,128)(2,1)}, bf16[528,256]{1,0:T(8,128)(2,1)S(1)}, u32[]{:S(2)}, u32[]{:S(2)}) collective-permute-start(bf16[528,256]{1,0:T(8,128)(2,1)} %get-tuple-element.48.hidden_ref), channel_id=1, source_target_pairs={{0,24},{4,28},{8,16},{12,20},{16,8},{20,12},{24,0},{28,4},{1,25},{... | collective-permute-start | bytes 811016 | tf_op jit(solution)/shard_map/ppermute | solution.py:428
  28.0 18.2 %collective-permute-start.13 = (bf16[528,256]{1,0:T(8,128)(2,1)}, bf16[528,256]{1,0:T(8,128)(2,1)S(1)}, u32[]{:S(2)}, u32[]{:S(2)}) collective-permute-start(bf16[528,256]{1,0:T(8,128)(2,1)} %get-tuple-element.48.hidden_ref), channel_id=1, source_target_pairs={{0,2},{1,3},{2,0},{3,1},{4,6},{5,7},{6,4},{7,5},{8,10},{9,11},{10,... | collective-permute-start | bytes 811016 | tf_op jit(solution)/shard_map/ppermute | solution.py:428
  40.7 14.4 %collective-permute-start.15 = (bf16[528,256]{1,0:T(8,128)(2,1)S(1)}, bf16[528,256]{1,0:T(8,128)(2,1)S(1)}, u32[]{:S(2)}, u32[]{:S(2)}) collective-permute-start(bf16[528,256]{1,0:T(8,128)(2,1)S(1)} %collective-permute-done.7), channel_id=1, source_target_pairs={{0,2},{1,3},{2,0},{3,1},{4,6},{5,7},{6,4},{7,5},{8,10},{9,11},{10,... | collective-permute-start | bytes 811016 | tf_op jit(solution)/shard_map/ppermute | solution.py:428
  42.1 14.0 %collective-permute-start.8 = (bf16[528,256]{1,0:T(8,128)(2,1)S(1)}, bf16[528,256]{1,0:T(8,128)(2,1)S(1)}, u32[]{:S(2)}, u32[]{:S(2)}) collective-permute-start(bf16[528,256]{1,0:T(8,128)(2,1)S(1)} %collective-permute-done.7), channel_id=1, source_target_pairs={{0,4},{4,0},{8,12},{12,8},{16,20},{20,16},{24,28},{28,24},{1,5},{5... | collective-permute-start | bytes 811016 | tf_op jit(solution)/shard_map/ppermute | solution.py:428
  45.0 9.0 %collective-permute-start.14 = (bf16[528,256]{1,0:T(8,128)(2,1)S(1)}, bf16[528,256]{1,0:T(8,128)(2,1)S(1)}, u32[]{:S(2)}, u32[]{:S(2)}) collective-permute-start(bf16[528,256]{1,0:T(8,128)(2,1)S(1)} %collective-permute-done.6), channel_id=1, source_target_pairs={{0,2},{1,3},{2,0},{3,1},{4,6},{5,7},{6,4},{7,5},{8,10},{9,11},{10,... | collective-permute-start | bytes 811016 | tf_op jit(solution)/shard_map/ppermute | solution.py:428
  45.5 11.8 %collective-permute-start.10 = (bf16[528,256]{1,0:T(8,128)(2,1)S(1)}, bf16[528,256]{1,0:T(8,128)(2,1)S(1)}, u32[]{:S(2)}, u32[]{:S(2)}) collective-permute-start(bf16[528,256]{1,0:T(8,128)(2,1)S(1)} %collective-permute-done.9), channel_id=1, source_target_pairs={{0,4},{4,0},{8,12},{12,8},{16,20},{20,16},{24,28},{28,24},{1,5},{5... | collective-permute-start | bytes 811016 | tf_op jit(solution)/shard_map/ppermute | solution.py:428
  46.1 23.7 %collective-permute-start.12 = (bf16[528,256]{1,0:T(8,128)(2,1)S(1)}, bf16[528,256]{1,0:T(8,128)(2,1)S(1)}, u32[]{:S(2)}, u32[]{:S(2)}) collective-permute-start(bf16[528,256]{1,0:T(8,128)(2,1)S(1)} %collective-permute-done.11), channel_id=1, source_target_pairs={{0,4},{4,0},{8,12},{12,8},{16,20},{20,16},{24,28},{28,24},{1,5},{5... | collective-permute-start | bytes 811016 | tf_op jit(solution)/shard_map/ppermute | solution.py:428
  54.0 15.3 %collective-permute-start.17 = (bf16[528,256]{1,0:T(8,128)(2,1)S(1)}, bf16[528,256]{1,0:T(8,128)(2,1)S(1)}, u32[]{:S(2)}, u32[]{:S(2)}) collective-permute-start(bf16[528,256]{1,0:T(8,128)(2,1)S(1)} %collective-permute-done.9), channel_id=1, source_target_pairs={{0,2},{1,3},{2,0},{3,1},{4,6},{5,7},{6,4},{7,5},{8,10},{9,11},{10,... | collective-permute-start | bytes 811016 | tf_op jit(solution)/shard_map/ppermute | solution.py:428
  55.1 14.1 %collective-permute-start.19 = (bf16[528,256]{1,0:T(8,128)(2,1)S(1)}, bf16[528,256]{1,0:T(8,128)(2,1)S(1)}, u32[]{:S(2)}, u32[]{:S(2)}) collective-permute-start(bf16[528,256]{1,0:T(8,128)(2,1)S(1)} %collective-permute-done.11), channel_id=1, source_target_pairs={{0,2},{1,3},{2,0},{3,1},{4,6},{5,7},{6,4},{7,5},{8,10},{9,11},{10,... | collective-permute-start | bytes 811016 | tf_op jit(solution)/shard_map/ppermute | solution.py:428
  56.1 13.8 %collective-permute-start.16 = (bf16[528,256]{1,0:T(8,128)(2,1)S(1)}, bf16[528,256]{1,0:T(8,128)(2,1)S(1)}, u32[]{:S(2)}, u32[]{:S(2)}) collective-permute-start(bf16[528,256]{1,0:T(8,128)(2,1)S(1)} %collective-permute-done.15), channel_id=1, source_target_pairs={{0,4},{4,0},{8,12},{12,8},{16,20},{20,16},{24,28},{28,24},{1,5},{5... | collective-permute-start | bytes 811016 | tf_op jit(solution)/shard_map/ppermute | solution.py:428
  57.3 14.8 %collective-permute-start.18 = (bf16[528,256]{1,0:T(8,128)(2,1)S(1)}, bf16[528,256]{1,0:T(8,128)(2,1)S(1)}, u32[]{:S(2)}, u32[]{:S(2)}) collective-permute-start(bf16[528,256]{1,0:T(8,128)(2,1)S(1)} %collective-permute-done.10), channel_id=1, source_target_pairs={{0,2},{1,3},{2,0},{3,1},{4,6},{5,7},{6,4},{7,5},{8,10},{9,11},{10,... | collective-permute-start | bytes 811016 | tf_op jit(solution)/shard_map/ppermute | solution.py:428
  69.2 11.5 %collective-permute-start.21 = (bf16[2048,256]{1,0:T(8,128)(2,1)S(1)}, bf16[2048,256]{1,0:T(8,128)(2,1)}, u32[]{:S(2)}, u32[]{:S(2)}) collective-permute-start(bf16[2048,256]{1,0:T(8,128)(2,1)S(1)} %pad_maximum_fusion), channel_id=1, source_target_pairs={{0,1},{1,0},{2,3},{3,2},{4,5},{5,4},{6,7},{7,6},{8,9},{9,8},{10,11... | collective-permute-start | bytes 3145736 | tf_op jit(solution)/shard_map/ppermute | solution.py:428
  69.2 9.0 %collective-permute-start.20 = (bf16[528,256]{1,0:T(8,128)(2,1)S(1)}, bf16[528,256]{1,0:T(8,128)(2,1)S(1)}, u32[]{:S(2)}, u32[]{:S(2)}) collective-permute-start(bf16[528,256]{1,0:T(8,128)(2,1)S(1)} %collective-permute-done.19), channel_id=1, source_target_pairs={{0,4},{4,0},{8,12},{12,8},{16,20},{20,16},{24,28},{28,24},{1,5},{5... | collective-permute-start | bytes 811016 | tf_op jit(solution)/shard_map/ppermute | solution.py:428
  70.0 10.7 %collective-permute-start.22 = (bf16[2048,256]{1,0:T(8,128)(2,1)S(1)}, bf16[2048,256]{1,0:T(8,128)(2,1)}, u32[]{:S(2)}, u32[]{:S(2)}) collective-permute-start(bf16[2048,256]{1,0:T(8,128)(2,1)S(1)} %pad_maximum_fusion.1), channel_id=1, source_target_pairs={{0,1},{1,0},{2,3},{3,2},{4,5},{5,4},{6,7},{7,6},{8,9},{9,8},{10,11... | collective-permute-start | bytes 3145736 | tf_op jit(solution)/shard_map/ppermute | solution.py:428
  72.3 8.5 %collective-permute-start.23 = (bf16[2048,256]{1,0:T(8,128)(2,1)S(1)}, bf16[2048,256]{1,0:T(8,128)(2,1)}, u32[]{:S(2)}, u32[]{:S(2)}) collective-permute-start(bf16[2048,256]{1,0:T(8,128)(2,1)S(1)} %pad_maximum_fusion.2), channel_id=1, source_target_pairs={{0,1},{1,0},{2,3},{3,2},{4,5},{5,4},{6,7},{7,6},{8,9},{9,8},{10,11... | collective-permute-start | bytes 3145736 | tf_op jit(solution)/shard_map/ppermute | solution.py:428
  103.0 21.2 %collective-permute-start.25 = (f32[96,256]{1,0:T(8,128)}, f32[96,256]{1,0:T(8,128)S(1)}, u32[]{:S(2)}, u32[]{:S(2)}) collective-permute-start(f32[96,256]{1,0:T(8,128)} %get-tuple-element.61), channel_id=1, source_target_pairs={{0,1},{1,0},{2,3},{3,2},{4,5},{5,4},{6,7},{7,6},{8,9},{9,8},{10,11... | collective-permute-start | bytes 294920 | tf_op jit(solution)/shard_map/ppermute | solution.py:428
  103.2 21.0 %collective-permute-start.26 = (f32[96,256]{1,0:T(8,128)}, f32[96,256]{1,0:T(8,128)S(1)}, u32[]{:S(2)}, u32[]{:S(2)}) collective-permute-start(f32[96,256]{1,0:T(8,128)} %get-tuple-element.62), channel_id=1, source_target_pairs={{0,2},{1,3},{2,0},{3,1},{4,6},{5,7},{6,4},{7,5},{8,10},{9,11},{10,... | collective-permute-start | bytes 294920 | tf_op jit(solution)/shard_map/ppermute | solution.py:428
  104.0 20.1 %collective-permute-start.27 = (f32[96,256]{1,0:T(8,128)}, f32[96,256]{1,0:T(8,128)S(1)}, u32[]{:S(2)}, u32[]{:S(2)}) collective-permute-start(f32[96,256]{1,0:T(8,128)} %get-tuple-element.63), channel_id=1, source_target_pairs={{0,3},{1,2},{2,1},{3,0},{4,7},{5,6},{6,5},{7,4},{8,11},{9,10},{10,... | collective-permute-start | bytes 294920 | tf_op jit(solution)/shard_map/ppermute | solution.py:428
  124.7 6.8 %collective-permute-start.38 = (bf16[16,128,256]{2,1,0:T(8,128)(2,1)}, bf16[16,128,256]{2,1,0:T(8,128)(2,1)S(1)}, u32[]{:S(2)}, u32[]{:S(2)}) collective-permute-start(bf16[16,128,256]{2,1,0:T(8,128)(2,1)} %get-tuple-element.69), channel_id=1, source_target_pairs={{0,1},{1,0},{2,3},{3,2},{4,5},{5,4},{6,7},{7,6},{8,9},{9,8},{10,11... | collective-permute-start | bytes 3145736 | tf_op jit(solution)/shard_map/ppermute | solution.py:428
  124.7 7.6 %collective-permute-start.33 = (bf16[16,128,256]{2,1,0:T(8,128)(2,1)}, bf16[16,128,256]{2,1,0:T(8,128)(2,1)S(1)}, u32[]{:S(2)}, u32[]{:S(2)}) collective-permute-start(bf16[16,128,256]{2,1,0:T(8,128)(2,1)} %get-tuple-element.67), channel_id=1, source_target_pairs={{0,1},{1,0},{2,3},{3,2},{4,5},{5,4},{6,7},{7,6},{8,9},{9,8},{10,11... | collective-permute-start | bytes 3145736 | tf_op jit(solution)/shard_map/ppermute | solution.py:428
  125.2 9.0 %collective-permute-start.28 = (bf16[16,128,256]{2,1,0:T(8,128)(2,1)}, bf16[16,128,256]{2,1,0:T(8,128)(2,1)S(1)}, u32[]{:S(2)}, u32[]{:S(2)}) collective-permute-start(bf16[16,128,256]{2,1,0:T(8,128)(2,1)} %get-tuple-element.65), channel_id=1, source_target_pairs={{0,1},{1,0},{2,3},{3,2},{4,5},{5,4},{6,7},{7,6},{8,9},{9,8},{10,11... | collective-permute-start | bytes 3145736 | tf_op jit(solution)/shard_map/ppermute | solution.py:428
  129.4 9.1 %collective-permute-start.44 = (bf16[512,256]{1,0:T(8,128)(2,1)S(1)}, bf16[512,256]{1,0:T(8,128)(2,1)S(1)}, u32[]{:S(2)}, u32[]{:S(2)}) collective-permute-start(bf16[512,256]{1,0:T(8,128)(2,1)S(1)} %bitcast.103), channel_id=1, source_target_pairs={{0,2},{1,3},{2,0},{3,1},{4,6},{5,7},{6,4},{7,5},{8,10},{9,11},{10,... | collective-permute-start | bytes 786440 | tf_op jit(solution)/shard_map/ppermute | solution.py:428
  130.2 38.8 %collective-permute-start.46 = (bf16[512,256]{1,0:T(8,128)(2,1)S(1)}, bf16[512,256]{1,0:T(8,128)(2,1)S(1)}, u32[]{:S(2)}, u32[]{:S(2)}) collective-permute-start(bf16[512,256]{1,0:T(8,128)(2,1)S(1)} %bitcast.99), channel_id=1, source_target_pairs={{0,2},{1,3},{2,0},{3,1},{4,6},{5,7},{6,4},{7,5},{8,10},{9,11},{10,... | collective-permute-start | bytes 786440 | tf_op jit(solution)/shard_map/ppermute | solution.py:428
  131.8 9.3 %collective-permute-start.40 = (bf16[512,256]{1,0:T(8,128)(2,1)S(1)}, bf16[512,256]{1,0:T(8,128)(2,1)S(1)}, u32[]{:S(2)}, u32[]{:S(2)}) collective-permute-start(bf16[512,256]{1,0:T(8,128)(2,1)S(1)} %bitcast.104), channel_id=1, source_target_pairs={{0,4},{4,0},{8,12},{12,8},{16,20},{20,16},{24,28},{28,24},{1,5},{5... | collective-permute-start | bytes 786440 | tf_op jit(solution)/shard_map/ppermute | solution.py:428
  132.4 19.3 %collective-permute-start.39 = (bf16[512,256]{1,0:T(8,128)(2,1)S(1)}, bf16[512,256]{1,0:T(8,128)(2,1)S(1)}, u32[]{:S(2)}, u32[]{:S(2)}) collective-permute-start(bf16[512,256]{1,0:T(8,128)(2,1)S(1)} %bitcast.102), channel_id=1, source_target_pairs={{0,4},{4,0},{8,12},{12,8},{16,20},{20,16},{24,28},{28,24},{1,5},{5... | collective-permute-start | bytes 786440 | tf_op jit(solution)/shard_map/ppermute | solution.py:428
  134.2 15.6 %collective-permute-start.34 = (bf16[512,256]{1,0:T(8,128)(2,1)S(1)}, bf16[512,256]{1,0:T(8,128)(2,1)S(1)}, u32[]{:S(2)}, u32[]{:S(2)}) collective-permute-start(bf16[512,256]{1,0:T(8,128)(2,1)S(1)} %bitcast.105), channel_id=1, source_target_pairs={{0,2},{1,3},{2,0},{3,1},{4,6},{5,7},{6,4},{7,5},{8,10},{9,11},{10,... | collective-permute-start | bytes 786440 | tf_op jit(solution)/shard_map/ppermute | solution.py:428
  138.5 22.9 %collective-permute-start.36 = (bf16[512,256]{1,0:T(8,128)(2,1)S(1)}, bf16[512,256]{1,0:T(8,128)(2,1)S(1)}, u32[]{:S(2)}, u32[]{:S(2)}) collective-permute-start(bf16[512,256]{1,0:T(8,128)(2,1)S(1)} %bitcast.101), channel_id=1, source_target_pairs={{0,2},{1,3},{2,0},{3,1},{4,6},{5,7},{6,4},{7,5},{8,10},{9,11},{10,... | collective-permute-start | bytes 786440 | tf_op jit(solution)/shard_map/ppermute | solution.py:428
  141.0 10.0 %collective-permute-start.30 = (bf16[512,256]{1,0:T(8,128)(2,1)S(1)}, bf16[512,256]{1,0:T(8,128)(2,1)S(1)}, u32[]{:S(2)}, u32[]{:S(2)}) collective-permute-start(bf16[512,256]{1,0:T(8,128)(2,1)S(1)} %bitcast.106), channel_id=1, source_target_pairs={{0,4},{4,0},{8,12},{12,8},{16,20},{20,16},{24,28},{28,24},{1,5},{5... | collective-permute-start | bytes 786440 | tf_op jit(solution)/shard_map/ppermute | solution.py:428
  149.7 10.7 %collective-permute-start.41 = (bf16[512,256]{1,0:T(8,128)(2,1)S(1)}, bf16[512,256]{1,0:T(8,128)(2,1)S(1)}, u32[]{:S(2)}, u32[]{:S(2)}) collective-permute-start(bf16[512,256]{1,0:T(8,128)(2,1)S(1)} %fusion.1), channel_id=1, source_target_pairs={{0,2},{1,3},{2,0},{3,1},{4,6},{5,7},{6,4},{7,5},{8,10},{9,11},{10,... | collective-permute-start | bytes 786440 | tf_op jit(solution)/shard_map/ppermute | solution.py:428
  151.1 10.9 %collective-permute-start.35 = (bf16[512,256]{1,0:T(8,128)(2,1)S(1)}, bf16[512,256]{1,0:T(8,128)(2,1)S(1)}, u32[]{:S(2)}, u32[]{:S(2)}) collective-permute-start(bf16[512,256]{1,0:T(8,128)(2,1)S(1)} %fusion.4), channel_id=1, source_target_pairs={{0,4},{4,0},{8,12},{12,8},{16,20},{20,16},{24,28},{28,24},{1,5},{5... | collective-permute-start | bytes 786440 | tf_op jit(solution)/shard_map/ppermute | solution.py:428
  151.7 13.9 %collective-permute-start.29 = (bf16[512,256]{1,0:T(8,128)(2,1)S(1)}, bf16[512,256]{1,0:T(8,128)(2,1)S(1)}, u32[]{:S(2)}, u32[]{:S(2)}) collective-permute-start(bf16[512,256]{1,0:T(8,128)(2,1)S(1)} %bitcast.100), channel_id=1, source_target_pairs={{0,4},{4,0},{8,12},{12,8},{16,20},{20,16},{24,28},{28,24},{1,5},{5... | collective-permute-start | bytes 786440 | tf_op jit(solution)/shard_map/ppermute | solution.py:428
  160.4 7.8 %collective-permute-start.31 = (bf16[512,256]{1,0:T(8,128)(2,1)S(1)}, bf16[512,256]{1,0:T(8,128)(2,1)S(1)}, u32[]{:S(2)}, u32[]{:S(2)}) collective-permute-start(bf16[512,256]{1,0:T(8,128)(2,1)S(1)} %fusion.7), channel_id=1, source_target_pairs={{0,2},{1,3},{2,0},{3,1},{4,6},{5,7},{6,4},{7,5},{8,10},{9,11},{10,... | collective-permute-start | bytes 786440 | tf_op jit(solution)/shard_map/ppermute | solution.py:428
  161.4 8.3 %collective-permute-start.45 = (bf16[512,256]{1,0:T(8,128)(2,1)S(1)}, bf16[512,256]{1,0:T(8,128)(2,1)S(1)}, u32[]{:S(2)}, u32[]{:S(2)}) collective-permute-start(bf16[512,256]{1,0:T(8,128)(2,1)S(1)} %fusion), channel_id=1, source_target_pairs={{0,4},{4,0},{8,12},{12,8},{16,20},{20,16},{24,28},{28,24},{1,5},{5... | collective-permute-start | bytes 786440 | tf_op jit(solution)/shard_map/ppermute | solution.py:428
  162.0 11.1 %collective-permute-start.42 = (bf16[512,256]{1,0:T(8,128)(2,1)S(1)}, bf16[512,256]{1,0:T(8,128)(2,1)S(1)}, u32[]{:S(2)}, u32[]{:S(2)}) collective-permute-start(bf16[512,256]{1,0:T(8,128)(2,1)S(1)} %fusion.3), channel_id=1, source_target_pairs={{0,24},{4,28},{8,16},{12,20},{16,8},{20,12},{24,0},{28,4},{1,25},{... | collective-permute-start | bytes 786440 | tf_op jit(solution)/shard_map/ppermute | solution.py:428
  165.6 20.4 %collective-permute-start.37 = (bf16[512,256]{1,0:T(8,128)(2,1)S(1)}, bf16[512,256]{1,0:T(8,128)(2,1)S(1)}, u32[]{:S(2)}, u32[]{:S(2)}) collective-permute-start(bf16[512,256]{1,0:T(8,128)(2,1)S(1)} %fusion.6), channel_id=1, source_target_pairs={{0,16},{4,20},{8,24},{12,28},{16,0},{20,4},{24,8},{28,12},{1,17},{... | collective-permute-start | bytes 786440 | tf_op jit(solution)/shard_map/ppermute | solution.py:428
  168.3 17.7 %collective-permute-start.32 = (bf16[512,256]{1,0:T(8,128)(2,1)S(1)}, bf16[512,256]{1,0:T(8,128)(2,1)S(1)}, u32[]{:S(2)}, u32[]{:S(2)}) collective-permute-start(bf16[512,256]{1,0:T(8,128)(2,1)S(1)} %fusion.9), channel_id=1, source_target_pairs={{0,8},{4,12},{8,0},{12,4},{16,24},{20,28},{24,16},{28,20},{1,9},{5... | collective-permute-start | bytes 786440 | tf_op jit(solution)/shard_map/ppermute | solution.py:428
  169.0 21.0 %collective-permute-start.52 = (f32[96,256]{1,0:T(8,128)S(1)}, f32[96,256]{1,0:T(8,128)S(1)}, u32[]{:S(2)}, u32[]{:S(2)}) collective-permute-start(f32[96,256]{1,0:T(8,128)S(1)} %add_add_fusion), channel_id=1, source_target_pairs={{0,4},{4,0},{8,12},{12,8},{16,20},{20,16},{24,28},{28,24},{1,5},{5... | collective-permute-start | bytes 294920 | tf_op jit(solution)/shard_map/ppermute | solution.py:428
  189.8 6.8 %collective-permute-start.47 = (f32[2,72,256]{2,1,0:T(8,128)}, f32[2,72,256]{2,1,0:T(8,128)S(1)}, u32[]{:S(2)}, u32[]{:S(2)}) collective-permute-start(f32[2,72,256]{2,1,0:T(8,128)} %get-tuple-element.75), channel_id=1, source_target_pairs={{0,1},{1,0},{2,3},{3,2},{4,5},{5,4},{6,7},{7,6},{8,9},{9,8},{10,11... | collective-permute-start | bytes 442376 | tf_op jit(solution)/shard_map/ppermute | solution.py:428
  195.3 7.4 %collective-permute-start.54 = (f32[96,256]{1,0:T(8,128)S(1)}, f32[96,256]{1,0:T(8,128)S(1)}, u32[]{:S(2)}, u32[]{:S(2)}) collective-permute-start(f32[96,256]{1,0:T(8,128)S(1)} %add.320), channel_id=1, source_target_pairs={{0,16},{4,20},{8,24},{12,28},{16,0},{20,4},{24,8},{28,12},{1,17},{... | collective-permute-start | bytes 294920 | tf_op jit(solution)/shard_map/ppermute | solution.py:428
  197.6 7.1 %collective-permute-start.48 = (f32[1,72,256]{2,1,0:T(8,128)S(1)}, f32[1,72,256]{2,1,0:T(8,128)S(1)}, u32[]{:S(2)}, u32[]{:S(2)}) collective-permute-start(f32[1,72,256]{2,1,0:T(8,128)S(1)} %slice.304), channel_id=1, source_target_pairs={{0,2},{1,3},{2,0},{3,1},{4,6},{5,7},{6,4},{7,5},{8,10},{9,11},{10,... | collective-permute-start | bytes 221192 | tf_op jit(solution)/shard_map/ppermute | solution.py:428
  202.8 5.7 %collective-permute-start.56 = (f32[96,256]{1,0:T(8,128)S(1)}, f32[96,256]{1,0:T(8,128)S(1)}, u32[]{:S(2)}, u32[]{:S(2)}) collective-permute-start(f32[96,256]{1,0:T(8,128)S(1)} %add.321), channel_id=1, source_target_pairs={{0,2},{1,3},{2,0},{3,1},{4,6},{5,7},{6,4},{7,5},{8,10},{9,11},{10,... | collective-permute-start | bytes 294920 | tf_op jit(solution)/shard_map/ppermute | solution.py:428
  214.8 6.2 %collective-permute-start.51 = (f32[72,256]{1,0:T(8,128)S(1)}, f32[72,256]{1,0:T(8,128)S(1)}, u32[]{:S(2)}, u32[]{:S(2)}) collective-permute-start(f32[72,256]{1,0:T(8,128)S(1)} %add.313), channel_id=1, source_target_pairs={{0,16},{4,20},{8,24},{12,28},{16,0},{20,4},{24,8},{28,12},{1,17},{... | collective-permute-start | bytes 221192 | tf_op jit(solution)/shard_map/ppermute | solution.py:428
  (31 other events, 239.3 us)

commit v5 on v4

--- a/solution.py
+++ b/solution.py
@@ -185,8 +185,8 @@
     classes = w_self.shape[0]
     second = -(-classes // 8) * 8
     share = -(-(2 * second + 8) // (8 * n_feat)) * 8
-    step = group_of(total, 32)
-    unroll = group_of(step, 32)
+    step = group_of(total, 64)
+    unroll = group_of(step, 64)
     steps = total // step
     lead = (((0,), (0,)), ((), ()))
     last = (((1,), (1,)), ((), ()))
@@ -314,8 +314,8 @@
     devices = owners.shape[0]
     each = slots // devices
     plane = devices // arrays
-    step = group_of(total, 32)
-    unroll = group_of(step, 32)
+    step = group_of(total, 64)
+    unroll = group_of(step, 64)
     steps = total // step
 
     def kernel(dst_s, src_s, owner_s, mine_s, tile_ref, gnum_ref, *refs):
@@ -399,7 +399,7 @@
     def kernel(*refs):
         own_ref, pre_ref = refs[terms : terms + 2]
         part_refs = refs[terms + 2 : terms + 2 + count]
-        even_ref, odd_ref = refs[terms + 2 + count :]
+        outs = refs[terms + 2 + count :]
         grad = refs[0][...].astype(F32)
         for term in range(1, terms):
             grad = grad + refs[term][...].astype(F32)
@@ -407,18 +407,15 @@
         grad_pre = jnp.where(pre_ref[...] > 0.0, grad, 0.0).astype(BF16)
         gb = jnp.sum(grad_pre.astype(F32), axis=0, keepdims=True)
         for r in range(count):
-            target = odd_ref if r % 2 else even_ref
-            target[r // 2, :features] = jnp.dot(
-                part_refs[r][...], grad_pre, preferred_element_type=F32
-            )
-            target[r // 2, features:] = jnp.broadcast_to(gb, (8, width))
-
-    shape = (count // 2, features + 8, width)
+            outs[r][:features] = jnp.dot(part_refs[r][...], grad_pre, preferred_element_type=F32)
+            outs[r][features:] = jnp.broadcast_to(gb, (8, width))
+
+    shape = (features + 8, width)
     return pl.pallas_call(
         kernel,
         in_specs=[VMEM] * (terms + 2 + count),
-        out_specs=[VMEM] * 2,
-        out_shape=[jax.ShapeDtypeStruct(shape, F32)] * 2,
+        out_specs=[VMEM] * count,
+        out_shape=[jax.ShapeDtypeStruct(shape, F32)] * count,
         compiler_params=BIG,
         name="first_gradients",
     )(*returned, own, pre, *parts)
@@ -428,13 +425,11 @@
     return lax.ppermute(value, axis, [(k, k ^ mask) for k in range(lax.axis_size(axis))])
 
 
-def feat_sum(even, odd):
-    value = even + swap(odd, "feat", 1)
-    mask = 2
-    while value.shape[0] > 1:
-        value = value[0::2] + swap(value[1::2], "feat", mask)
-        mask *= 2
-    return value[0]
+def feat_sum(pieces):
+    total = pieces[0]
+    for r in range(1, len(pieces)):
+        total = total + swap(pieces[r], "feat", r)
+    return total
 
 
 def gather_blocks(value, planes, across, rows, beside):
@@ -565,8 +560,8 @@
     third = jnp.take(third, jnp.arange(n_feat) ^ me_feat, axis=0).reshape(-1, width)
     second = -(-classes // 8) * 8
     terms = return_blocks(arrays, planes, across)
-    even, odd = first_gradients(terms, own, pre, parts)
-    last = doubling_sum(feat_sum(even, odd), "dom")
+    pieces = first_gradients(terms, own, pre, parts)
+    last = doubling_sum(feat_sum(pieces), "dom")
     edge = 2 * features
     return (
         last[features:edge],

time: 223 us -> 215 us (0.964)
  Pallas kernels: 60.9 us -> 55.2 us
  waiting for transfers between devices: 95.1 us -> 90.2 us
    ppermute x58 -> x59, waiting for transfers between devices: 95.1 us -> 90.2 us  [swap(): lax.ppermute(value, axis, [(k, k ^ mask) for k in range(lax.axis_size(axi...]
    pallas_call x1, Pallas kernels: 20.6 us -> 17.8 us  [output_layer(): pl.pallas_call(kernel, grid_spec=pltpu.PrefetchScalarGridSpec(num_scalar_...]
    pallas_call x1, Pallas kernels: 19.2 us -> 16.4 us  [slot_gradients(): pl.pallas_call(kernel, grid_spec=pltpu.PrefetchScalarGridSpec(num_scalar_...]
    ppermute x58 -> x59, starting transfers between devices: 47.2 us -> 49.3 us  [swap(): lax.ppermute(value, axis, [(k, k ^ mask) for k in range(lax.axis_size(axi...]
  transfers between devices with their start and end apart: 58 -> 59, of which waited for: 24 -> 26; matrix products, arithmetic and copies ran while one was open for 6% -> 6% of each run, Pallas kernels for 17% -> 16%
where the time goes in v5:
time: 215 us; the launch traced here: 214 us
  waiting for transfers between devices  90.2 us (42%)
  Pallas kernels  55.2 us (26%)
  starting transfers between devices  49.3 us (23%)
  other arithmetic  8.99 us (4%)
  local copies, waits for them, and re-layouts  8.76 us (4%)
    ppermute x59, waiting for transfers between devices, swap(): lax.ppermute(value, axis, [(k, k ^ mask) for k in range(lax.axis_size(axi...  90.2 us
    ppermute x59, starting transfers between devices, swap(): lax.ppermute(value, axis, [(k, k ^ mask) for k in range(lax.axis_size(axi...  49.3 us
    pallas_call x1, Pallas kernels, output_layer(): pl.pallas_call(kernel, grid_spec=pltpu.PrefetchScalarGridSpec(num_scalar_...  17.8 us
    pallas_call x1, Pallas kernels, slot_gradients(): pl.pallas_call(kernel, grid_spec=pltpu.PrefetchScalarGridSpec(num_scalar_...  16.4 us
    pallas_call x1, Pallas kernels, row_weights(): pl.pallas_call(kernel, grid_spec=pltpu.PrefetchScalarGridSpec(num_scalar_...  11.1 us
    pallas_call x1, Pallas kernels, first_layer(): pl.pallas_call(kernel, grid_spec=pltpu.PrefetchScalarGridSpec(num_scalar_...  4.65 us
  transfers between devices with their start and end apart: 59, of which 26 were waited for; matrix products, arithmetic and copies ran while one was open for 6% of the time, Pallas kernels for 16%

profile of v5, /device:TPU:0, one launch (start us, length us, event | category | flops | bytes accessed | tf_op | source)
XLA Modules:
  0.0 213.7 jit_solution(14700535844034666504)
XLA Ops:
  2.8 2.6 %collective-permute-start.4 = (bf16[80,256]{1,0:T(8,128)(2,1)S(1)}, bf16[80,256]{1,0:T(8,128)(2,1)S(1)}, u32[]{:S(2)}, u32[]{:S(2)}) collective-permute-start(bf16[80,256]{1,0:T(8,128)(2,1)S(1)} %fusion.11.refs_4_), channel_id=1, source_target_pairs={{0,2},{1,3},{2,0},{3,1},{4,6},{5,7},{6,4},{7,5},{8,10},{9,11},{10,... | collective-permute-start | bytes 122888 | tf_op jit(solution)/shard_map/ppermute | solution.py:425
  5.5 4.7 %first_layer.1 = (bf16[64,512]{1,0:T(8,128)(2,1)}, bf16[64,512]{1,0:T(8,128)(2,1)}, bf16[64,512]{1,0:T(8,128)(2,1)}, bf16[64,512]{1,0:T(8,128)(2,1)}) custom-call(s32[64]{0:T(128)} %dst_s.3, s32[64]{0:T(128)} %src_s.3, s32[1]{0:T(128)} %bitcast.me_s, bf16[64,128,128]{2,1,0:T(8,128)(2,1)} %tile_ref.4, bf16[32,4096]{1,0:T(8,128)(2,1)} %feat_ref.1), custom_call_target="tpu_custom_call" | custom-call | tf_op jit(solution)/shard_map/first_layer/pallas_call | solution.py:76
  10.3 1.9 collective-permute-start.1
  12.4 2.5 %collective-permute-done.1.refs_2_.refs_10_ = bf16[64,512]{1,0:T(8,128)(2,1)S(1)} collective-permute-done((bf16[64,512]{1,0:T(8,128)(2,1)}, bf16[64,512]{1,0:T(8,128)(2,1)S(1)}, u32[]{:S(2)}, u32[]{:S(2)}) %collective-permute-start.1) | collective-permute-done | bytes 65568 | tf_op jit(solution)/shard_map/ppermute | solution.py:425
  14.9 1.9 collective-permute-done.2.refs_3_.refs_11_
  17.5 2.3 %hidden_layer.1 = (f32[512,256]{1,0:T(8,128)}, bf16[528,256]{1,0:T(8,128)(2,1)}) custom-call(bf16[64,512]{1,0:T(8,128)(2,1)} %get-tuple-element.45.refs_0_.refs_8_, bf16[64,512]{1,0:T(8,128)(2,1)} %copy-done.6, bf16[64,512]{1,0:T(8,128)(2,1)} %copy-done.7, bf16[64,512]{1,0:T(8,128)(2,1)} %copy-done.8, bf16[80,256]{1,0:T(8,128)(2,1)} %copy-done.14, ...), custom_call_target="tpu_custom_call" | custom-call | tf_op jit(solution)/shard_map/hidden_layer/pallas_call | solution.py:117
  19.8 1.6 collective-permute-start.7
  21.4 1.5 collective-permute-start.6
  22.9 2.6 %collective-permute-start.9 = (bf16[528,256]{1,0:T(8,128)(2,1)}, bf16[528,256]{1,0:T(8,128)(2,1)S(1)}, u32[]{:S(2)}, u32[]{:S(2)}) collective-permute-start(bf16[528,256]{1,0:T(8,128)(2,1)} %get-tuple-element.50.hidden_ref), channel_id=1, source_target_pairs={{0,16},{4,20},{8,24},{12,28},{16,0},{20,4},{24,8},{28,12},{1,17},{... | collective-permute-start | bytes 811016 | tf_op jit(solution)/shard_map/ppermute | solution.py:425
  29.6 11.1 %row_weights.1.weight_ref = f32[4,128,128]{2,1,0:T(8,128)} custom-call(s32[384]{0:T(512)} %dst_s.6, bf16[384,128,128]{2,1,0:T(8,128)(2,1)} %tile_ref.7), custom_call_target="tpu_custom_call" | custom-call | flops 12582912 | bytes 12582912 | tf_op jit(solution)/shard_map/row_weights/pallas_call | solution.py:158
  40.7 1.4 collective-permute-start.15
  42.7 2.3 %collective-permute-done.9 = bf16[528,256]{1,0:T(8,128)(2,1)S(1)} collective-permute-done((bf16[528,256]{1,0:T(8,128)(2,1)}, bf16[528,256]{1,0:T(8,128)(2,1)S(1)}, u32[]{:S(2)}, u32[]{:S(2)}) %collective-permute-start.9) | collective-permute-done | bytes 270368 | tf_op jit(solution)/shard_map/ppermute | solution.py:425
  46.1 1.6 collective-permute-start.12
  47.7 6.3 %collective-permute-done.14 = bf16[528,256]{1,0:T(8,128)(2,1)S(1)} collective-permute-done((bf16[528,256]{1,0:T(8,128)(2,1)S(1)}, bf16[528,256]{1,0:T(8,128)(2,1)S(1)}, u32[]{:S(2)}, u32[]{:S(2)}) %collective-permute-start.14) | collective-permute-done | bytes 270368 | tf_op jit(solution)/shard_map/ppermute | solution.py:425
  54.0 1.1 collective-permute-start.17
  58.0 11.2 %collective-permute-done.19 = bf16[528,256]{1,0:T(8,128)(2,1)S(1)} collective-permute-done((bf16[528,256]{1,0:T(8,128)(2,1)S(1)}, bf16[528,256]{1,0:T(8,128)(2,1)S(1)}, u32[]{:S(2)}, u32[]{:S(2)}) %collective-permute-start.19) | collective-permute-done | bytes 270368 | tf_op jit(solution)/shard_map/ppermute | solution.py:425
  70.3 1.9 collective-permute-done.18
  72.4 5.8 %collective-permute-done.20 = bf16[528,256]{1,0:T(8,128)(2,1)S(1)} collective-permute-done((bf16[528,256]{1,0:T(8,128)(2,1)S(1)}, bf16[528,256]{1,0:T(8,128)(2,1)S(1)}, u32[]{:S(2)}, u32[]{:S(2)}) %collective-permute-start.20) | collective-permute-done | bytes 270368 | tf_op jit(solution)/shard_map/ppermute | solution.py:425
  78.2 1.1 pad_maximum_fusion.3
  80.7 1.6 collective-permute-done.24
  82.3 17.8 %output_layer.1 = (f32[96,256]{1,0:T(8,128)}, f32[96,256]{1,0:T(8,128)}, f32[96,256]{1,0:T(8,128)}, f32[96,256]{1,0:T(8,128)}, bf16[4,128,256]{2,1,0:T(8,128)(2,1)}, /*index=5*/f32[512,256]{1,0:T(8,128)}) custom-call(s32[384]{0:T(512)} %dst_s.6, s32[384]{0:T(512)} %src_s.5, s32[64]{0:T(128)} %add.286.place_s, s32[1]{0:T(128)} %bitcast.me_s, ...), custom_call_target="tpu_custom_call" | custom-call | flops 12884901888 | bytes 12582912 | tf_op jit(solution)/shard_map/output_layer/pallas_call | solution.py:277
  102.1 16.4 %slot_gradients.1 = (bf16[16,128,256]{2,1,0:T(8,128)(2,1)}, bf16[16,128,256]{2,1,0:T(8,128)(2,1)}, bf16[16,128,256]{2,1,0:T(8,128)(2,1)}, bf16[16,128,256]{2,1,0...) custom-call(s32[384]{0:T(512)} %dst_s.6, ...), custom_call_target="tpu_custom_call" | custom-call | flops 12884901888 | bytes 12582912 | tf_op jit(solution)/shard_map/slot_gradients/pallas_call | solution.py:370
  120.2 4.6 %collective-permute-done.53 = f32[96,256]{1,0:T(8,128)S(1)} collective-permute-done((f32[96,256]{1,0:T(8,128)S(1)}, f32[96,256]{1,0:T(8,128)S(1)}, u32[]{:S(2)}, u32[]{:S(2)}) %collective-permute-start.53) | collective-permute-done | bytes 98336 | tf_op jit(solution)/shard_map/ppermute | solution.py:425
  125.5 2.2 %add_convert_fusion = (bf16[4,128,256]{2,1,0:T(8,128)(2,1)S(1)}, bf16[4,128,256]{2,1,0:T(8,128)(2,1)S(1)}, bf16[4,128,256]{2,1,0:T(8,128)(2,1)S(1)}, bf16[4,128,256]{2,1,0:T(8,128)(2,1)}) fusion(bf16[16,128,256]{2,1,0:T(8,128)(2,1)S(1)} %collective-permute-done.43, bf16[16,128,256]{2,1,0:T(8,128)(2,1)} %get-tuple-element.72), kind=kLoop, calls=%fused_computation.23 | loop fusion | flops 2097152 | bytes 3145728 | tf_op jit(solution)/shard_map/convert_element_type | solution.py:462
  129.4 1.5 collective-permute-start.39
  131.2 1.4 collective-permute-start.34
  132.9 4.0 %collective-permute-done.44 = bf16[512,256]{1,0:T(8,128)(2,1)S(1)} collective-permute-done((bf16[512,256]{1,0:T(8,128)(2,1)S(1)}, bf16[512,256]{1,0:T(8,128)(2,1)S(1)}, u32[]{:S(2)}, u32[]{:S(2)}) %collective-permute-start.44) | collective-permute-done | bytes 262176 | tf_op jit(solution)/shard_map/ppermute | solution.py:425
  138.8 3.8 %collective-permute-done.34 = bf16[512,256]{1,0:T(8,128)(2,1)S(1)} collective-permute-done((bf16[512,256]{1,0:T(8,128)(2,1)S(1)}, bf16[512,256]{1,0:T(8,128)(2,1)S(1)}, u32[]{:S(2)}, u32[]{:S(2)}) %collective-permute-start.34) | collective-permute-done | bytes 262176 | tf_op jit(solution)/shard_map/ppermute | solution.py:425
  143.4 4.0 %collective-permute-done.30 = bf16[512,256]{1,0:T(8,128)(2,1)S(1)} collective-permute-done((bf16[512,256]{1,0:T(8,128)(2,1)S(1)}, bf16[512,256]{1,0:T(8,128)(2,1)S(1)}, u32[]{:S(2)}, u32[]{:S(2)}) %collective-permute-start.30) | collective-permute-done | bytes 262176 | tf_op jit(solution)/shard_map/ppermute | solution.py:425
  148.1 1.5 collective-permute-start.29
  149.6 2.5 %collective-permute-done.41 = bf16[512,256]{1,0:T(8,128)(2,1)S(1)} collective-permute-done((bf16[512,256]{1,0:T(8,128)(2,1)S(1)}, bf16[512,256]{1,0:T(8,128)(2,1)S(1)}, u32[]{:S(2)}, u32[]{:S(2)}) %collective-permute-start.41) | collective-permute-done | bytes 262176 | tf_op jit(solution)/shard_map/ppermute | solution.py:425
  153.0 1.4 collective-permute-start.46
  154.4 2.3 %collective-permute-done.35 = bf16[512,256]{1,0:T(8,128)(2,1)S(1)} collective-permute-done((bf16[512,256]{1,0:T(8,128)(2,1)S(1)}, bf16[512,256]{1,0:T(8,128)(2,1)S(1)}, u32[]{:S(2)}, u32[]{:S(2)}) %collective-permute-start.35) | collective-permute-done | bytes 262176 | tf_op jit(solution)/shard_map/ppermute | solution.py:425
  157.3 4.9 %collective-permute-done.29 = bf16[512,256]{1,0:T(8,128)(2,1)S(1)} collective-permute-done((bf16[512,256]{1,0:T(8,128)(2,1)S(1)}, bf16[512,256]{1,0:T(8,128)(2,1)S(1)}, u32[]{:S(2)}, u32[]{:S(2)}) %collective-permute-start.29) | collective-permute-done | bytes 262176 | tf_op jit(solution)/shard_map/ppermute | solution.py:425
  162.2 3.3 %collective-permute-start.42 = (bf16[512,256]{1,0:T(8,128)(2,1)S(1)}, bf16[512,256]{1,0:T(8,128)(2,1)S(1)}, u32[]{:S(2)}, u32[]{:S(2)}) collective-permute-start(bf16[512,256]{1,0:T(8,128)(2,1)S(1)} %fusion.3), channel_id=1, source_target_pairs={{0,24},{4,28},{8,16},{12,20},{16,8},{20,12},{24,0},{28,4},{1,25},{... | collective-permute-start | bytes 786440 | tf_op jit(solution)/shard_map/ppermute | solution.py:425
  167.0 2.7 %collective-permute-start.55 = (f32[96,256]{1,0:T(8,128)S(1)}, f32[96,256]{1,0:T(8,128)S(1)}, u32[]{:S(2)}, u32[]{:S(2)}) collective-permute-start(f32[96,256]{1,0:T(8,128)S(1)} %add.324), channel_id=1, source_target_pairs={{0,16},{4,20},{8,24},{12,28},{16,0},{20,4},{24,8},{28,12},{1,17},{... | collective-permute-start | bytes 294920 | tf_op jit(solution)/shard_map/ppermute | solution.py:425
  169.7 3.6 %collective-permute-done.42.refs_2_ = bf16[512,256]{1,0:T(8,128)(2,1)S(1)} collective-permute-done((bf16[512,256]{1,0:T(8,128)(2,1)S(1)}, bf16[512,256]{1,0:T(8,128)(2,1)S(1)}, u32[]{:S(2)}, u32[]{:S(2)}) %collective-permute-start.42) | collective-permute-done | bytes 262176 | tf_op jit(solution)/shard_map/ppermute | solution.py:425
  173.4 12.9 %collective-permute-done.37.refs_1_ = bf16[512,256]{1,0:T(8,128)(2,1)S(1)} collective-permute-done((bf16[512,256]{1,0:T(8,128)(2,1)S(1)}, bf16[512,256]{1,0:T(8,128)(2,1)S(1)}, u32[]{:S(2)}, u32[]{:S(2)}) %collective-permute-start.37) | collective-permute-done | bytes 262176 | tf_op jit(solution)/shard_map/ppermute | solution.py:425
  187.2 2.9 %first_gradients.1 = (f32[72,256]{1,0:T(8,128)}, f32[72,256]{1,0:T(8,128)}, f32[72,256]{1,0:T(8,128)}, f32[72,256]{1,0:T(8,128)}) custom-call(bf16[512,256]{1,0:T(8,128)(2,1)} %copy-done.13, bf16[512,256]{1,0:T(8,128)(2,1)} %copy-done.12, bf16[512,256]{1,0:T(8,128)(2,1)} %copy-done.11, bf16[512,256]{1,0:T(8,128)(2,1)} %bitcast.95, ...), custom_call_target="tpu_custom_call" | custom-call | tf_op jit(solution)/shard_map/first_gradients/pallas_call | solution.py:414
  190.1 1.3 collective-permute-start.48
  192.4 1.2 collective-permute-start.57
  193.9 1.5 collective-permute-done.48
  197.6 1.5 collective-permute-done.57
  199.1 1.2 collective-permute-done.58
  200.9 1.1 collective-permute-done.50
  202.4 4.0 %collective-permute-done.51 = f32[72,256]{1,0:T(8,128)S(1)} collective-permute-done((f32[72,256]{1,0:T(8,128)S(1)}, f32[72,256]{1,0:T(8,128)S(1)}, u32[]{:S(2)}, u32[]{:S(2)}) %collective-permute-start.51) | collective-permute-done | bytes 73760 | tf_op jit(solution)/shard_map/ppermute | solution.py:425
  206.4 1.6 collective-permute-start.52
  209.3 3.2 %collective-permute-done.52 = f32[72,256]{1,0:T(8,128)S(1)} collective-permute-done((f32[72,256]{1,0:T(8,128)S(1)}, f32[72,256]{1,0:T(8,128)S(1)}, u32[]{:S(2)}, u32[]{:S(2)}) %collective-permute-start.52) | collective-permute-done | bytes 73760 | tf_op jit(solution)/shard_map/ppermute | solution.py:425
  (196 shorter events, 35.3 us)
Async XLA Ops:
  2.3 9.9 %collective-permute-start.3 = (bf16[80,256]{1,0:T(8,128)(2,1)S(1)}, bf16[80,256]{1,0:T(8,128)(2,1)S(1)}, u32[]{:S(2)}, u32[]{:S(2)}) collective-permute-start(bf16[80,256]{1,0:T(8,128)(2,1)S(1)} %fusion.11.refs_4_), channel_id=1, source_target_pairs={{0,1},{1,0},{2,3},{3,2},{4,5},{5,4},{6,7},{7,6},{8,9},{9,8},{10,11... | collective-permute-start | bytes 122888 | tf_op jit(solution)/shard_map/ppermute | solution.py:425
  2.8 9.5 %collective-permute-start.4 = (bf16[80,256]{1,0:T(8,128)(2,1)S(1)}, bf16[80,256]{1,0:T(8,128)(2,1)S(1)}, u32[]{:S(2)}, u32[]{:S(2)}) collective-permute-start(bf16[80,256]{1,0:T(8,128)(2,1)S(1)} %fusion.11.refs_4_), channel_id=1, source_target_pairs={{0,2},{1,3},{2,0},{3,1},{4,6},{5,7},{6,4},{7,5},{8,10},{9,11},{10,... | collective-permute-start | bytes 122888 | tf_op jit(solution)/shard_map/ppermute | solution.py:425
  5.4 7.0 %collective-permute-start.5 = (bf16[80,256]{1,0:T(8,128)(2,1)S(1)}, bf16[80,256]{1,0:T(8,128)(2,1)S(1)}, u32[]{:S(2)}, u32[]{:S(2)}) collective-permute-start(bf16[80,256]{1,0:T(8,128)(2,1)S(1)} %fusion.11.refs_4_), channel_id=1, source_target_pairs={{0,3},{1,2},{2,1},{3,0},{4,7},{5,6},{6,5},{7,4},{8,11},{9,10},{10,... | collective-permute-start | bytes 122888 | tf_op jit(solution)/shard_map/ppermute | solution.py:425
  19.8 20.8 %collective-permute-start.7 = (bf16[528,256]{1,0:T(8,128)(2,1)}, bf16[528,256]{1,0:T(8,128)(2,1)S(1)}, u32[]{:S(2)}, u32[]{:S(2)}) collective-permute-start(bf16[528,256]{1,0:T(8,128)(2,1)} %get-tuple-element.50.hidden_ref), channel_id=1, source_target_pairs={{0,8},{4,12},{8,0},{12,4},{16,24},{20,28},{24,16},{28,20},{1,9},{5... | collective-permute-start | bytes 811016 | tf_op jit(solution)/shard_map/ppermute | solution.py:425
  21.4 20.7 %collective-permute-start.6 = (bf16[528,256]{1,0:T(8,128)(2,1)}, bf16[528,256]{1,0:T(8,128)(2,1)S(1)}, u32[]{:S(2)}, u32[]{:S(2)}) collective-permute-start(bf16[528,256]{1,0:T(8,128)(2,1)} %get-tuple-element.50.hidden_ref), channel_id=1, source_target_pairs={{0,4},{4,0},{8,12},{12,8},{16,20},{20,16},{24,28},{28,24},{1,5},{5... | collective-permute-start | bytes 811016 | tf_op jit(solution)/shard_map/ppermute | solution.py:425
  22.9 22.1 %collective-permute-start.9 = (bf16[528,256]{1,0:T(8,128)(2,1)}, bf16[528,256]{1,0:T(8,128)(2,1)S(1)}, u32[]{:S(2)}, u32[]{:S(2)}) collective-permute-start(bf16[528,256]{1,0:T(8,128)(2,1)} %get-tuple-element.50.hidden_ref), channel_id=1, source_target_pairs={{0,16},{4,20},{8,24},{12,28},{16,0},{20,4},{24,8},{28,12},{1,17},{... | collective-permute-start | bytes 811016 | tf_op jit(solution)/shard_map/ppermute | solution.py:425
  27.0 18.5 %collective-permute-start.11 = (bf16[528,256]{1,0:T(8,128)(2,1)}, bf16[528,256]{1,0:T(8,128)(2,1)S(1)}, u32[]{:S(2)}, u32[]{:S(2)}) collective-permute-start(bf16[528,256]{1,0:T(8,128)(2,1)} %get-tuple-element.50.hidden_ref), channel_id=1, source_target_pairs={{0,24},{4,28},{8,16},{12,20},{16,8},{20,12},{24,0},{28,4},{1,25},{... | collective-permute-start | bytes 811016 | tf_op jit(solution)/shard_map/ppermute | solution.py:425
  28.0 18.2 %collective-permute-start.13 = (bf16[528,256]{1,0:T(8,128)(2,1)}, bf16[528,256]{1,0:T(8,128)(2,1)S(1)}, u32[]{:S(2)}, u32[]{:S(2)}) collective-permute-start(bf16[528,256]{1,0:T(8,128)(2,1)} %get-tuple-element.50.hidden_ref), channel_id=1, source_target_pairs={{0,2},{1,3},{2,0},{3,1},{4,6},{5,7},{6,4},{7,5},{8,10},{9,11},{10,... | collective-permute-start | bytes 811016 | tf_op jit(solution)/shard_map/ppermute | solution.py:425
  40.7 14.4 %collective-permute-start.15 = (bf16[528,256]{1,0:T(8,128)(2,1)S(1)}, bf16[528,256]{1,0:T(8,128)(2,1)S(1)}, u32[]{:S(2)}, u32[]{:S(2)}) collective-permute-start(bf16[528,256]{1,0:T(8,128)(2,1)S(1)} %collective-permute-done.7), channel_id=1, source_target_pairs={{0,2},{1,3},{2,0},{3,1},{4,6},{5,7},{6,4},{7,5},{8,10},{9,11},{10,... | collective-permute-start | bytes 811016 | tf_op jit(solution)/shard_map/ppermute | solution.py:425
  42.1 14.0 %collective-permute-start.8 = (bf16[528,256]{1,0:T(8,128)(2,1)S(1)}, bf16[528,256]{1,0:T(8,128)(2,1)S(1)}, u32[]{:S(2)}, u32[]{:S(2)}) collective-permute-start(bf16[528,256]{1,0:T(8,128)(2,1)S(1)} %collective-permute-done.7), channel_id=1, source_target_pairs={{0,4},{4,0},{8,12},{12,8},{16,20},{20,16},{24,28},{28,24},{1,5},{5... | collective-permute-start | bytes 811016 | tf_op jit(solution)/shard_map/ppermute | solution.py:425
  45.0 9.0 %collective-permute-start.14 = (bf16[528,256]{1,0:T(8,128)(2,1)S(1)}, bf16[528,256]{1,0:T(8,128)(2,1)S(1)}, u32[]{:S(2)}, u32[]{:S(2)}) collective-permute-start(bf16[528,256]{1,0:T(8,128)(2,1)S(1)} %collective-permute-done.6), channel_id=1, source_target_pairs={{0,2},{1,3},{2,0},{3,1},{4,6},{5,7},{6,4},{7,5},{8,10},{9,11},{10,... | collective-permute-start | bytes 811016 | tf_op jit(solution)/shard_map/ppermute | solution.py:425
  45.5 11.8 %collective-permute-start.10 = (bf16[528,256]{1,0:T(8,128)(2,1)S(1)}, bf16[528,256]{1,0:T(8,128)(2,1)S(1)}, u32[]{:S(2)}, u32[]{:S(2)}) collective-permute-start(bf16[528,256]{1,0:T(8,128)(2,1)S(1)} %collective-permute-done.9), channel_id=1, source_target_pairs={{0,4},{4,0},{8,12},{12,8},{16,20},{20,16},{24,28},{28,24},{1,5},{5... | collective-permute-start | bytes 811016 | tf_op jit(solution)/shard_map/ppermute | solution.py:425
  46.1 23.7 %collective-permute-start.12 = (bf16[528,256]{1,0:T(8,128)(2,1)S(1)}, bf16[528,256]{1,0:T(8,128)(2,1)S(1)}, u32[]{:S(2)}, u32[]{:S(2)}) collective-permute-start(bf16[528,256]{1,0:T(8,128)(2,1)S(1)} %collective-permute-done.11), channel_id=1, source_target_pairs={{0,4},{4,0},{8,12},{12,8},{16,20},{20,16},{24,28},{28,24},{1,5},{5... | collective-permute-start | bytes 811016 | tf_op jit(solution)/shard_map/ppermute | solution.py:425
  54.0 15.2 %collective-permute-start.17 = (bf16[528,256]{1,0:T(8,128)(2,1)S(1)}, bf16[528,256]{1,0:T(8,128)(2,1)S(1)}, u32[]{:S(2)}, u32[]{:S(2)}) collective-permute-start(bf16[528,256]{1,0:T(8,128)(2,1)S(1)} %collective-permute-done.9), channel_id=1, source_target_pairs={{0,2},{1,3},{2,0},{3,1},{4,6},{5,7},{6,4},{7,5},{8,10},{9,11},{10,... | collective-permute-start | bytes 811016 | tf_op jit(solution)/shard_map/ppermute | solution.py:425
  55.1 14.1 %collective-permute-start.19 = (bf16[528,256]{1,0:T(8,128)(2,1)S(1)}, bf16[528,256]{1,0:T(8,128)(2,1)S(1)}, u32[]{:S(2)}, u32[]{:S(2)}) collective-permute-start(bf16[528,256]{1,0:T(8,128)(2,1)S(1)} %collective-permute-done.11), channel_id=1, source_target_pairs={{0,2},{1,3},{2,0},{3,1},{4,6},{5,7},{6,4},{7,5},{8,10},{9,11},{10,... | collective-permute-start | bytes 811016 | tf_op jit(solution)/shard_map/ppermute | solution.py:425
  56.1 13.8 %collective-permute-start.16 = (bf16[528,256]{1,0:T(8,128)(2,1)S(1)}, bf16[528,256]{1,0:T(8,128)(2,1)S(1)}, u32[]{:S(2)}, u32[]{:S(2)}) collective-permute-start(bf16[528,256]{1,0:T(8,128)(2,1)S(1)} %collective-permute-done.15), channel_id=1, source_target_pairs={{0,4},{4,0},{8,12},{12,8},{16,20},{20,16},{24,28},{28,24},{1,5},{5... | collective-permute-start | bytes 811016 | tf_op jit(solution)/shard_map/ppermute | solution.py:425
  57.3 14.9 %collective-permute-start.18 = (bf16[528,256]{1,0:T(8,128)(2,1)S(1)}, bf16[528,256]{1,0:T(8,128)(2,1)S(1)}, u32[]{:S(2)}, u32[]{:S(2)}) collective-permute-start(bf16[528,256]{1,0:T(8,128)(2,1)S(1)} %collective-permute-done.10), channel_id=1, source_target_pairs={{0,2},{1,3},{2,0},{3,1},{4,6},{5,7},{6,4},{7,5},{8,10},{9,11},{10,... | collective-permute-start | bytes 811016 | tf_op jit(solution)/shard_map/ppermute | solution.py:425
  69.2 11.5 %collective-permute-start.21 = (bf16[2048,256]{1,0:T(8,128)(2,1)S(1)}, bf16[2048,256]{1,0:T(8,128)(2,1)}, u32[]{:S(2)}, u32[]{:S(2)}) collective-permute-start(bf16[2048,256]{1,0:T(8,128)(2,1)S(1)} %pad_maximum_fusion), channel_id=1, source_target_pairs={{0,1},{1,0},{2,3},{3,2},{4,5},{5,4},{6,7},{7,6},{8,9},{9,8},{10,11... | collective-permute-start | bytes 3145736 | tf_op jit(solution)/shard_map/ppermute | solution.py:425
  69.2 9.0 %collective-permute-start.20 = (bf16[528,256]{1,0:T(8,128)(2,1)S(1)}, bf16[528,256]{1,0:T(8,128)(2,1)S(1)}, u32[]{:S(2)}, u32[]{:S(2)}) collective-permute-start(bf16[528,256]{1,0:T(8,128)(2,1)S(1)} %collective-permute-done.19), channel_id=1, source_target_pairs={{0,4},{4,0},{8,12},{12,8},{16,20},{20,16},{24,28},{28,24},{1,5},{5... | collective-permute-start | bytes 811016 | tf_op jit(solution)/shard_map/ppermute | solution.py:425
  70.0 10.7 %collective-permute-start.22 = (bf16[2048,256]{1,0:T(8,128)(2,1)S(1)}, bf16[2048,256]{1,0:T(8,128)(2,1)}, u32[]{:S(2)}, u32[]{:S(2)}) collective-permute-start(bf16[2048,256]{1,0:T(8,128)(2,1)S(1)} %pad_maximum_fusion.1), channel_id=1, source_target_pairs={{0,1},{1,0},{2,3},{3,2},{4,5},{5,4},{6,7},{7,6},{8,9},{9,8},{10,11... | collective-permute-start | bytes 3145736 | tf_op jit(solution)/shard_map/ppermute | solution.py:425
  72.3 8.4 %collective-permute-start.23 = (bf16[2048,256]{1,0:T(8,128)(2,1)S(1)}, bf16[2048,256]{1,0:T(8,128)(2,1)}, u32[]{:S(2)}, u32[]{:S(2)}) collective-permute-start(bf16[2048,256]{1,0:T(8,128)(2,1)S(1)} %pad_maximum_fusion.2), channel_id=1, source_target_pairs={{0,1},{1,0},{2,3},{3,2},{4,5},{5,4},{6,7},{7,6},{8,9},{9,8},{10,11... | collective-permute-start | bytes 3145736 | tf_op jit(solution)/shard_map/ppermute | solution.py:425
  100.1 18.3 %collective-permute-start.25 = (f32[96,256]{1,0:T(8,128)}, f32[96,256]{1,0:T(8,128)S(1)}, u32[]{:S(2)}, u32[]{:S(2)}) collective-permute-start(f32[96,256]{1,0:T(8,128)} %get-tuple-element.63), channel_id=1, source_target_pairs={{0,1},{1,0},{2,3},{3,2},{4,5},{5,4},{6,7},{7,6},{8,9},{9,8},{10,11... | collective-permute-start | bytes 294920 | tf_op jit(solution)/shard_map/ppermute | solution.py:425
  100.3 18.1 %collective-permute-start.26 = (f32[96,256]{1,0:T(8,128)}, f32[96,256]{1,0:T(8,128)S(1)}, u32[]{:S(2)}, u32[]{:S(2)}) collective-permute-start(f32[96,256]{1,0:T(8,128)} %get-tuple-element.64), channel_id=1, source_target_pairs={{0,2},{1,3},{2,0},{3,1},{4,6},{5,7},{6,4},{7,5},{8,10},{9,11},{10,... | collective-permute-start | bytes 294920 | tf_op jit(solution)/shard_map/ppermute | solution.py:425
  101.1 17.3 %collective-permute-start.27 = (f32[96,256]{1,0:T(8,128)}, f32[96,256]{1,0:T(8,128)S(1)}, u32[]{:S(2)}, u32[]{:S(2)}) collective-permute-start(f32[96,256]{1,0:T(8,128)} %get-tuple-element.65), channel_id=1, source_target_pairs={{0,3},{1,2},{2,1},{3,0},{4,7},{5,6},{6,5},{7,4},{8,11},{9,10},{10,... | collective-permute-start | bytes 294920 | tf_op jit(solution)/shard_map/ppermute | solution.py:425
  118.5 7.0 %collective-permute-start.43 = (bf16[16,128,256]{2,1,0:T(8,128)(2,1)}, bf16[16,128,256]{2,1,0:T(8,128)(2,1)S(1)}, u32[]{:S(2)}, u32[]{:S(2)}) collective-permute-start(bf16[16,128,256]{2,1,0:T(8,128)(2,1)} %get-tuple-element.73), channel_id=1, source_target_pairs={{0,1},{1,0},{2,3},{3,2},{4,5},{5,4},{6,7},{7,6},{8,9},{9,8},{10,11... | collective-permute-start | bytes 3145736 | tf_op jit(solution)/shard_map/ppermute | solution.py:425
  119.0 9.5 %collective-permute-start.38 = (bf16[16,128,256]{2,1,0:T(8,128)(2,1)}, bf16[16,128,256]{2,1,0:T(8,128)(2,1)S(1)}, u32[]{:S(2)}, u32[]{:S(2)}) collective-permute-start(bf16[16,128,256]{2,1,0:T(8,128)(2,1)} %get-tuple-element.71), channel_id=1, source_target_pairs={{0,1},{1,0},{2,3},{3,2},{4,5},{5,4},{6,7},{7,6},{8,9},{9,8},{10,11... | collective-permute-start | bytes 3145736 | tf_op jit(solution)/shard_map/ppermute | solution.py:425
  119.1 10.4 %collective-permute-start.33 = (bf16[16,128,256]{2,1,0:T(8,128)(2,1)}, bf16[16,128,256]{2,1,0:T(8,128)(2,1)S(1)}, u32[]{:S(2)}, u32[]{:S(2)}) collective-permute-start(bf16[16,128,256]{2,1,0:T(8,128)(2,1)} %get-tuple-element.69), channel_id=1, source_target_pairs={{0,1},{1,0},{2,3},{3,2},{4,5},{5,4},{6,7},{7,6},{8,9},{9,8},{10,11... | collective-permute-start | bytes 3145736 | tf_op jit(solution)/shard_map/ppermute | solution.py:425
  119.5 11.7 %collective-permute-start.28 = (bf16[16,128,256]{2,1,0:T(8,128)(2,1)}, bf16[16,128,256]{2,1,0:T(8,128)(2,1)S(1)}, u32[]{:S(2)}, u32[]{:S(2)}) collective-permute-start(bf16[16,128,256]{2,1,0:T(8,128)(2,1)} %get-tuple-element.67), channel_id=1, source_target_pairs={{0,1},{1,0},{2,3},{3,2},{4,5},{5,4},{6,7},{7,6},{8,9},{9,8},{10,11... | collective-permute-start | bytes 3145736 | tf_op jit(solution)/shard_map/ppermute | solution.py:425
  124.8 41.1 %collective-permute-start.54 = (f32[96,256]{1,0:T(8,128)S(1)}, f32[96,256]{1,0:T(8,128)S(1)}, u32[]{:S(2)}, u32[]{:S(2)}) collective-permute-start(f32[96,256]{1,0:T(8,128)S(1)} %add.323), channel_id=1, source_target_pairs={{0,8},{4,12},{8,0},{12,4},{16,24},{20,28},{24,16},{28,20},{1,9},{5... | collective-permute-start | bytes 294920 | tf_op jit(solution)/shard_map/ppermute | solution.py:425
  127.7 9.2 %collective-permute-start.44 = (bf16[512,256]{1,0:T(8,128)(2,1)S(1)}, bf16[512,256]{1,0:T(8,128)(2,1)S(1)}, u32[]{:S(2)}, u32[]{:S(2)}) collective-permute-start(bf16[512,256]{1,0:T(8,128)(2,1)S(1)} %bitcast.101), channel_id=1, source_target_pairs={{0,2},{1,3},{2,0},{3,1},{4,6},{5,7},{6,4},{7,5},{8,10},{9,11},{10,... | collective-permute-start | bytes 786440 | tf_op jit(solution)/shard_map/ppermute | solution.py:425
  128.8 9.3 %collective-permute-start.40 = (bf16[512,256]{1,0:T(8,128)(2,1)S(1)}, bf16[512,256]{1,0:T(8,128)(2,1)S(1)}, u32[]{:S(2)}, u32[]{:S(2)}) collective-permute-start(bf16[512,256]{1,0:T(8,128)(2,1)S(1)} %bitcast.102), channel_id=1, source_target_pairs={{0,4},{4,0},{8,12},{12,8},{16,20},{20,16},{24,28},{28,24},{1,5},{5... | collective-permute-start | bytes 786440 | tf_op jit(solution)/shard_map/ppermute | solution.py:425
  129.4 18.6 %collective-permute-start.39 = (bf16[512,256]{1,0:T(8,128)(2,1)S(1)}, bf16[512,256]{1,0:T(8,128)(2,1)S(1)}, u32[]{:S(2)}, u32[]{:S(2)}) collective-permute-start(bf16[512,256]{1,0:T(8,128)(2,1)S(1)} %bitcast.100), channel_id=1, source_target_pairs={{0,4},{4,0},{8,12},{12,8},{16,20},{20,16},{24,28},{28,24},{1,5},{5... | collective-permute-start | bytes 786440 | tf_op jit(solution)/shard_map/ppermute | solution.py:425
  131.2 11.3 %collective-permute-start.34 = (bf16[512,256]{1,0:T(8,128)(2,1)S(1)}, bf16[512,256]{1,0:T(8,128)(2,1)S(1)}, u32[]{:S(2)}, u32[]{:S(2)}) collective-permute-start(bf16[512,256]{1,0:T(8,128)(2,1)S(1)} %bitcast.103), channel_id=1, source_target_pairs={{0,2},{1,3},{2,0},{3,1},{4,6},{5,7},{6,4},{7,5},{8,10},{9,11},{10,... | collective-permute-start | bytes 786440 | tf_op jit(solution)/shard_map/ppermute | solution.py:425
  137.0 16.1 %collective-permute-start.36 = (bf16[512,256]{1,0:T(8,128)(2,1)S(1)}, bf16[512,256]{1,0:T(8,128)(2,1)S(1)}, u32[]{:S(2)}, u32[]{:S(2)}) collective-permute-start(bf16[512,256]{1,0:T(8,128)(2,1)S(1)} %bitcast.99), channel_id=1, source_target_pairs={{0,2},{1,3},{2,0},{3,1},{4,6},{5,7},{6,4},{7,5},{8,10},{9,11},{10,... | collective-permute-start | bytes 786440 | tf_op jit(solution)/shard_map/ppermute | solution.py:425
  138.1 9.3 %collective-permute-start.30 = (bf16[512,256]{1,0:T(8,128)(2,1)S(1)}, bf16[512,256]{1,0:T(8,128)(2,1)S(1)}, u32[]{:S(2)}, u32[]{:S(2)}) collective-permute-start(bf16[512,256]{1,0:T(8,128)(2,1)S(1)} %bitcast.104), channel_id=1, source_target_pairs={{0,4},{4,0},{8,12},{12,8},{16,20},{20,16},{24,28},{28,24},{1,5},{5... | collective-permute-start | bytes 786440 | tf_op jit(solution)/shard_map/ppermute | solution.py:425
  142.6 9.6 %collective-permute-start.41 = (bf16[512,256]{1,0:T(8,128)(2,1)S(1)}, bf16[512,256]{1,0:T(8,128)(2,1)S(1)}, u32[]{:S(2)}, u32[]{:S(2)}) collective-permute-start(bf16[512,256]{1,0:T(8,128)(2,1)S(1)} %fusion.1), channel_id=1, source_target_pairs={{0,2},{1,3},{2,0},{3,1},{4,6},{5,7},{6,4},{7,5},{8,10},{9,11},{10,... | collective-permute-start | bytes 786440 | tf_op jit(solution)/shard_map/ppermute | solution.py:425
  147.4 9.2 %collective-permute-start.35 = (bf16[512,256]{1,0:T(8,128)(2,1)S(1)}, bf16[512,256]{1,0:T(8,128)(2,1)S(1)}, u32[]{:S(2)}, u32[]{:S(2)}) collective-permute-start(bf16[512,256]{1,0:T(8,128)(2,1)S(1)} %fusion.4), channel_id=1, source_target_pairs={{0,4},{4,0},{8,12},{12,8},{16,20},{20,16},{24,28},{28,24},{1,5},{5... | collective-permute-start | bytes 786440 | tf_op jit(solution)/shard_map/ppermute | solution.py:425
  148.1 14.1 %collective-permute-start.29 = (bf16[512,256]{1,0:T(8,128)(2,1)S(1)}, bf16[512,256]{1,0:T(8,128)(2,1)S(1)}, u32[]{:S(2)}, u32[]{:S(2)}) collective-permute-start(bf16[512,256]{1,0:T(8,128)(2,1)S(1)} %bitcast.98), channel_id=1, source_target_pairs={{0,4},{4,0},{8,12},{12,8},{16,20},{20,16},{24,28},{28,24},{1,5},{5... | collective-permute-start | bytes 786440 | tf_op jit(solution)/shard_map/ppermute | solution.py:425
  152.2 13.4 %collective-permute-start.31 = (bf16[512,256]{1,0:T(8,128)(2,1)S(1)}, bf16[512,256]{1,0:T(8,128)(2,1)S(1)}, u32[]{:S(2)}, u32[]{:S(2)}) collective-permute-start(bf16[512,256]{1,0:T(8,128)(2,1)S(1)} %fusion.7), channel_id=1, source_target_pairs={{0,2},{1,3},{2,0},{3,1},{4,6},{5,7},{6,4},{7,5},{8,10},{9,11},{10,... | collective-permute-start | bytes 786440 | tf_op jit(solution)/shard_map/ppermute | solution.py:425
  153.0 14.0 %collective-permute-start.46 = (bf16[512,256]{1,0:T(8,128)(2,1)S(1)}, bf16[512,256]{1,0:T(8,128)(2,1)S(1)}, u32[]{:S(2)}, u32[]{:S(2)}) collective-permute-start(bf16[512,256]{1,0:T(8,128)(2,1)S(1)} %bitcast.97), channel_id=1, source_target_pairs={{0,2},{1,3},{2,0},{3,1},{4,6},{5,7},{6,4},{7,5},{8,10},{9,11},{10,... | collective-permute-start | bytes 786440 | tf_op jit(solution)/shard_map/ppermute | solution.py:425
  156.6 13.1 %collective-permute-start.45 = (bf16[512,256]{1,0:T(8,128)(2,1)S(1)}, bf16[512,256]{1,0:T(8,128)(2,1)S(1)}, u32[]{:S(2)}, u32[]{:S(2)}) collective-permute-start(bf16[512,256]{1,0:T(8,128)(2,1)S(1)} %fusion), channel_id=1, source_target_pairs={{0,4},{4,0},{8,12},{12,8},{16,20},{20,16},{24,28},{28,24},{1,5},{5... | collective-permute-start | bytes 786440 | tf_op jit(solution)/shard_map/ppermute | solution.py:425
  162.2 11.1 %collective-permute-start.42 = (bf16[512,256]{1,0:T(8,128)(2,1)S(1)}, bf16[512,256]{1,0:T(8,128)(2,1)S(1)}, u32[]{:S(2)}, u32[]{:S(2)}) collective-permute-start(bf16[512,256]{1,0:T(8,128)(2,1)S(1)} %fusion.3), channel_id=1, source_target_pairs={{0,24},{4,28},{8,16},{12,20},{16,8},{20,12},{24,0},{28,4},{1,25},{... | collective-permute-start | bytes 786440 | tf_op jit(solution)/shard_map/ppermute | solution.py:425
  165.5 20.8 %collective-permute-start.37 = (bf16[512,256]{1,0:T(8,128)(2,1)S(1)}, bf16[512,256]{1,0:T(8,128)(2,1)S(1)}, u32[]{:S(2)}, u32[]{:S(2)}) collective-permute-start(bf16[512,256]{1,0:T(8,128)(2,1)S(1)} %fusion.6), channel_id=1, source_target_pairs={{0,16},{4,20},{8,24},{12,28},{16,0},{20,4},{24,8},{28,12},{1,17},{... | collective-permute-start | bytes 786440 | tf_op jit(solution)/shard_map/ppermute | solution.py:425
  165.9 20.4 %collective-permute-start.32 = (bf16[512,256]{1,0:T(8,128)(2,1)S(1)}, bf16[512,256]{1,0:T(8,128)(2,1)S(1)}, u32[]{:S(2)}, u32[]{:S(2)}) collective-permute-start(bf16[512,256]{1,0:T(8,128)(2,1)S(1)} %fusion.9), channel_id=1, source_target_pairs={{0,8},{4,12},{8,0},{12,4},{16,24},{20,28},{24,16},{28,20},{1,9},{5... | collective-permute-start | bytes 786440 | tf_op jit(solution)/shard_map/ppermute | solution.py:425
  167.0 24.9 %collective-permute-start.55 = (f32[96,256]{1,0:T(8,128)S(1)}, f32[96,256]{1,0:T(8,128)S(1)}, u32[]{:S(2)}, u32[]{:S(2)}) collective-permute-start(f32[96,256]{1,0:T(8,128)S(1)} %add.324), channel_id=1, source_target_pairs={{0,16},{4,20},{8,24},{12,28},{16,0},{20,4},{24,8},{28,12},{1,17},{... | collective-permute-start | bytes 294920 | tf_op jit(solution)/shard_map/ppermute | solution.py:425
  192.4 6.7 %collective-permute-start.57 = (f32[96,256]{1,0:T(8,128)S(1)}, f32[96,256]{1,0:T(8,128)S(1)}, u32[]{:S(2)}, u32[]{:S(2)}) collective-permute-start(f32[96,256]{1,0:T(8,128)S(1)} %add.325), channel_id=1, source_target_pairs={{0,2},{1,3},{2,0},{3,1},{4,6},{5,7},{6,4},{7,5},{8,10},{9,11},{10,... | collective-permute-start | bytes 294920 | tf_op jit(solution)/shard_map/ppermute | solution.py:425
  193.6 6.7 %collective-permute-start.58 = (f32[96,256]{1,0:T(8,128)S(1)}, f32[96,256]{1,0:T(8,128)S(1)}, u32[]{:S(2)}, u32[]{:S(2)}) collective-permute-start(f32[96,256]{1,0:T(8,128)S(1)} %add.325), channel_id=1, source_target_pairs={{0,3},{1,2},{2,1},{3,0},{4,7},{5,6},{6,5},{7,4},{8,11},{9,10},{10,... | collective-permute-start | bytes 294920 | tf_op jit(solution)/shard_map/ppermute | solution.py:425
  206.4 6.1 %collective-permute-start.52 = (f32[72,256]{1,0:T(8,128)S(1)}, f32[72,256]{1,0:T(8,128)S(1)}, u32[]{:S(2)}, u32[]{:S(2)}) collective-permute-start(f32[72,256]{1,0:T(8,128)S(1)} %add.317), channel_id=1, source_target_pairs={{0,16},{4,20},{8,24},{12,28},{16,0},{20,4},{24,8},{28,12},{1,17},{... | collective-permute-start | bytes 221192 | tf_op jit(solution)/shard_map/ppermute | solution.py:425
  (32 other events, 246.5 us)

commit v6 on v5

--- a/solution.py
+++ b/solution.py
@@ -185,8 +185,8 @@
     classes = w_self.shape[0]
     second = -(-classes // 8) * 8
     share = -(-(2 * second + 8) // (8 * n_feat)) * 8
-    step = group_of(total, 64)
-    unroll = group_of(step, 64)
+    step = group_of(total, 96)
+    unroll = group_of(step, 96)
     steps = total // step
     lead = (((0,), (0,)), ((), ()))
     last = (((1,), (1,)), ((), ()))
@@ -314,8 +314,8 @@
     devices = owners.shape[0]
     each = slots // devices
     plane = devices // arrays
-    step = group_of(total, 64)
-    unroll = group_of(step, 64)
+    step = group_of(total, 96)
+    unroll = group_of(step, 96)
     steps = total // step
 
     def kernel(dst_s, src_s, owner_s, mine_s, tile_ref, gnum_ref, *refs):

time: 215 us -> 213 us (level)
  no operation moved by 1% of the time
where the time goes in v6:
time: 213 us; the launch traced here: 212 us
  waiting for transfers between devices  90.4 us (42%)
  Pallas kernels  53.7 us (25%)
  starting transfers between devices  49.1 us (23%)
  other arithmetic  8.99 us (4%)
  local copies, waits for them, and re-layouts  8.76 us (4%)
    ppermute x59, waiting for transfers between devices, swap(): lax.ppermute(value, axis, [(k, k ^ mask) for k in range(lax.axis_size(axi...  90.4 us
    ppermute x59, starting transfers between devices, swap(): lax.ppermute(value, axis, [(k, k ^ mask) for k in range(lax.axis_size(axi...  49.1 us
    pallas_call x1, Pallas kernels, output_layer(): pl.pallas_call(kernel, grid_spec=pltpu.PrefetchScalarGridSpec(num_scalar_...  17.1 us
    pallas_call x1, Pallas kernels, slot_gradients(): pl.pallas_call(kernel, grid_spec=pltpu.PrefetchScalarGridSpec(num_scalar_...  15.6 us
    pallas_call x1, Pallas kernels, row_weights(): pl.pallas_call(kernel, grid_spec=pltpu.PrefetchScalarGridSpec(num_scalar_...  11.1 us
    pallas_call x1, Pallas kernels, first_layer(): pl.pallas_call(kernel, grid_spec=pltpu.PrefetchScalarGridSpec(num_scalar_...  4.66 us
  transfers between devices with their start and end apart: 59, of which 26 were waited for; matrix products, arithmetic and copies ran while one was open for 6% of the time, Pallas kernels for 16%

profile of v6, /device:TPU:0, one launch (start us, length us, event | category | flops | bytes accessed | tf_op | source)
XLA Modules:
  0.0 212.2 jit_solution(6609274813309641240)
XLA Ops:
  2.8 2.6 %collective-permute-start.4 = (bf16[80,256]{1,0:T(8,128)(2,1)S(1)}, bf16[80,256]{1,0:T(8,128)(2,1)S(1)}, u32[]{:S(2)}, u32[]{:S(2)}) collective-permute-start(bf16[80,256]{1,0:T(8,128)(2,1)S(1)} %fusion.11.refs_4_), channel_id=1, source_target_pairs={{0,2},{1,3},{2,0},{3,1},{4,6},{5,7},{6,4},{7,5},{8,10},{9,11},{10,... | collective-permute-start | bytes 122888 | tf_op jit(solution)/shard_map/ppermute | solution.py:425
  5.5 4.7 %first_layer.1 = (bf16[64,512]{1,0:T(8,128)(2,1)}, bf16[64,512]{1,0:T(8,128)(2,1)}, bf16[64,512]{1,0:T(8,128)(2,1)}, bf16[64,512]{1,0:T(8,128)(2,1)}) custom-call(s32[64]{0:T(128)} %dst_s.3, s32[64]{0:T(128)} %src_s.3, s32[1]{0:T(128)} %bitcast.me_s, bf16[64,128,128]{2,1,0:T(8,128)(2,1)} %tile_ref.4, bf16[32,4096]{1,0:T(8,128)(2,1)} %feat_ref.1), custom_call_target="tpu_custom_call" | custom-call | tf_op jit(solution)/shard_map/first_layer/pallas_call | solution.py:76
  10.3 1.9 collective-permute-start.1
  12.4 2.5 %collective-permute-done.1.refs_2_.refs_10_ = bf16[64,512]{1,0:T(8,128)(2,1)S(1)} collective-permute-done((bf16[64,512]{1,0:T(8,128)(2,1)}, bf16[64,512]{1,0:T(8,128)(2,1)S(1)}, u32[]{:S(2)}, u32[]{:S(2)}) %collective-permute-start.1) | collective-permute-done | bytes 65568 | tf_op jit(solution)/shard_map/ppermute | solution.py:425
  14.9 1.9 collective-permute-done.2.refs_3_.refs_11_
  17.5 2.3 %hidden_layer.1 = (f32[512,256]{1,0:T(8,128)}, bf16[528,256]{1,0:T(8,128)(2,1)}) custom-call(bf16[64,512]{1,0:T(8,128)(2,1)} %get-tuple-element.45.refs_0_.refs_8_, bf16[64,512]{1,0:T(8,128)(2,1)} %copy-done.6, bf16[64,512]{1,0:T(8,128)(2,1)} %copy-done.7, bf16[64,512]{1,0:T(8,128)(2,1)} %copy-done.8, bf16[80,256]{1,0:T(8,128)(2,1)} %copy-done.14, ...), custom_call_target="tpu_custom_call" | custom-call | tf_op jit(solution)/shard_map/hidden_layer/pallas_call | solution.py:117
  19.8 1.6 collective-permute-start.7
  21.4 1.5 collective-permute-start.6
  22.9 2.6 %collective-permute-start.9 = (bf16[528,256]{1,0:T(8,128)(2,1)}, bf16[528,256]{1,0:T(8,128)(2,1)S(1)}, u32[]{:S(2)}, u32[]{:S(2)}) collective-permute-start(bf16[528,256]{1,0:T(8,128)(2,1)} %get-tuple-element.50.hidden_ref), channel_id=1, source_target_pairs={{0,16},{4,20},{8,24},{12,28},{16,0},{20,4},{24,8},{28,12},{1,17},{... | collective-permute-start | bytes 811016 | tf_op jit(solution)/shard_map/ppermute | solution.py:425
  29.6 11.1 %row_weights.1.weight_ref = f32[4,128,128]{2,1,0:T(8,128)} custom-call(s32[384]{0:T(512)} %dst_s.6, bf16[384,128,128]{2,1,0:T(8,128)(2,1)} %tile_ref.7), custom_call_target="tpu_custom_call" | custom-call | flops 12582912 | bytes 12582912 | tf_op jit(solution)/shard_map/row_weights/pallas_call | solution.py:158
  40.7 1.4 collective-permute-start.15
  42.7 2.3 %collective-permute-done.9 = bf16[528,256]{1,0:T(8,128)(2,1)S(1)} collective-permute-done((bf16[528,256]{1,0:T(8,128)(2,1)}, bf16[528,256]{1,0:T(8,128)(2,1)S(1)}, u32[]{:S(2)}, u32[]{:S(2)}) %collective-permute-start.9) | collective-permute-done | bytes 270368 | tf_op jit(solution)/shard_map/ppermute | solution.py:425
  46.1 1.6 collective-permute-start.12
  47.7 6.3 %collective-permute-done.14 = bf16[528,256]{1,0:T(8,128)(2,1)S(1)} collective-permute-done((bf16[528,256]{1,0:T(8,128)(2,1)S(1)}, bf16[528,256]{1,0:T(8,128)(2,1)S(1)}, u32[]{:S(2)}, u32[]{:S(2)}) %collective-permute-start.14) | collective-permute-done | bytes 270368 | tf_op jit(solution)/shard_map/ppermute | solution.py:425
  54.0 1.1 collective-permute-start.17
  55.1 1.0 collective-permute-start.19
  58.0 11.2 %collective-permute-done.19 = bf16[528,256]{1,0:T(8,128)(2,1)S(1)} collective-permute-done((bf16[528,256]{1,0:T(8,128)(2,1)S(1)}, bf16[528,256]{1,0:T(8,128)(2,1)S(1)}, u32[]{:S(2)}, u32[]{:S(2)}) %collective-permute-start.19) | collective-permute-done | bytes 270368 | tf_op jit(solution)/shard_map/ppermute | solution.py:425
  70.3 1.9 collective-permute-done.18
  72.4 5.8 %collective-permute-done.20 = bf16[528,256]{1,0:T(8,128)(2,1)S(1)} collective-permute-done((bf16[528,256]{1,0:T(8,128)(2,1)S(1)}, bf16[528,256]{1,0:T(8,128)(2,1)S(1)}, u32[]{:S(2)}, u32[]{:S(2)}) %collective-permute-start.20) | collective-permute-done | bytes 270368 | tf_op jit(solution)/shard_map/ppermute | solution.py:425
  78.2 1.1 pad_maximum_fusion.3
  80.8 1.6 collective-permute-done.24
  82.3 17.1 %output_layer.1 = (f32[96,256]{1,0:T(8,128)}, f32[96,256]{1,0:T(8,128)}, f32[96,256]{1,0:T(8,128)}, f32[96,256]{1,0:T(8,128)}, bf16[4,128,256]{2,1,0:T(8,128)(2,1)}, /*index=5*/f32[512,256]{1,0:T(8,128)}) custom-call(s32[384]{0:T(512)} %dst_s.6, s32[384]{0:T(512)} %src_s.5, s32[64]{0:T(128)} %add.286.place_s, s32[1]{0:T(128)} %bitcast.me_s, ...), custom_call_target="tpu_custom_call" | custom-call | flops 12884901888 | bytes 12582912 | tf_op jit(solution)/shard_map/output_layer/pallas_call | solution.py:277
  101.4 15.6 %slot_gradients.1 = (bf16[16,128,256]{2,1,0:T(8,128)(2,1)}, bf16[16,128,256]{2,1,0:T(8,128)(2,1)}, bf16[16,128,256]{2,1,0:T(8,128)(2,1)}, bf16[16,128,256]{2,1,0...) custom-call(s32[384]{0:T(512)} %dst_s.6, ...), custom_call_target="tpu_custom_call" | custom-call | flops 12884901888 | bytes 12582912 | tf_op jit(solution)/shard_map/slot_gradients/pallas_call | solution.py:370
  118.7 4.6 %collective-permute-done.53 = f32[96,256]{1,0:T(8,128)S(1)} collective-permute-done((f32[96,256]{1,0:T(8,128)S(1)}, f32[96,256]{1,0:T(8,128)S(1)}, u32[]{:S(2)}, u32[]{:S(2)}) %collective-permute-start.53) | collective-permute-done | bytes 98336 | tf_op jit(solution)/shard_map/ppermute | solution.py:425
  124.0 2.2 %add_convert_fusion = (bf16[4,128,256]{2,1,0:T(8,128)(2,1)S(1)}, bf16[4,128,256]{2,1,0:T(8,128)(2,1)S(1)}, bf16[4,128,256]{2,1,0:T(8,128)(2,1)S(1)}, bf16[4,128,256]{2,1,0:T(8,128)(2,1)}) fusion(bf16[16,128,256]{2,1,0:T(8,128)(2,1)S(1)} %collective-permute-done.43, bf16[16,128,256]{2,1,0:T(8,128)(2,1)} %get-tuple-element.72), kind=kLoop, calls=%fused_computation.23 | loop fusion | flops 2097152 | bytes 3145728 | tf_op jit(solution)/shard_map/convert_element_type | solution.py:462
  127.9 1.5 collective-permute-start.39
  129.8 1.3 collective-permute-start.34
  131.4 4.0 %collective-permute-done.44 = bf16[512,256]{1,0:T(8,128)(2,1)S(1)} collective-permute-done((bf16[512,256]{1,0:T(8,128)(2,1)S(1)}, bf16[512,256]{1,0:T(8,128)(2,1)S(1)}, u32[]{:S(2)}, u32[]{:S(2)}) %collective-permute-start.44) | collective-permute-done | bytes 262176 | tf_op jit(solution)/shard_map/ppermute | solution.py:425
  137.3 3.9 %collective-permute-done.34 = bf16[512,256]{1,0:T(8,128)(2,1)S(1)} collective-permute-done((bf16[512,256]{1,0:T(8,128)(2,1)S(1)}, bf16[512,256]{1,0:T(8,128)(2,1)S(1)}, u32[]{:S(2)}, u32[]{:S(2)}) %collective-permute-start.34) | collective-permute-done | bytes 262176 | tf_op jit(solution)/shard_map/ppermute | solution.py:425
  142.0 4.0 %collective-permute-done.30 = bf16[512,256]{1,0:T(8,128)(2,1)S(1)} collective-permute-done((bf16[512,256]{1,0:T(8,128)(2,1)S(1)}, bf16[512,256]{1,0:T(8,128)(2,1)S(1)}, u32[]{:S(2)}, u32[]{:S(2)}) %collective-permute-start.30) | collective-permute-done | bytes 262176 | tf_op jit(solution)/shard_map/ppermute | solution.py:425
  146.6 1.6 collective-permute-start.29
  148.2 2.5 %collective-permute-done.41 = bf16[512,256]{1,0:T(8,128)(2,1)S(1)} collective-permute-done((bf16[512,256]{1,0:T(8,128)(2,1)S(1)}, bf16[512,256]{1,0:T(8,128)(2,1)S(1)}, u32[]{:S(2)}, u32[]{:S(2)}) %collective-permute-start.41) | collective-permute-done | bytes 262176 | tf_op jit(solution)/shard_map/ppermute | solution.py:425
  151.6 1.3 collective-permute-start.46
  152.9 2.3 %collective-permute-done.35 = bf16[512,256]{1,0:T(8,128)(2,1)S(1)} collective-permute-done((bf16[512,256]{1,0:T(8,128)(2,1)S(1)}, bf16[512,256]{1,0:T(8,128)(2,1)S(1)}, u32[]{:S(2)}, u32[]{:S(2)}) %collective-permute-start.35) | collective-permute-done | bytes 262176 | tf_op jit(solution)/shard_map/ppermute | solution.py:425
  155.8 4.9 %collective-permute-done.29 = bf16[512,256]{1,0:T(8,128)(2,1)S(1)} collective-permute-done((bf16[512,256]{1,0:T(8,128)(2,1)S(1)}, bf16[512,256]{1,0:T(8,128)(2,1)S(1)}, u32[]{:S(2)}, u32[]{:S(2)}) %collective-permute-start.29) | collective-permute-done | bytes 262176 | tf_op jit(solution)/shard_map/ppermute | solution.py:425
  160.8 3.3 %collective-permute-start.42 = (bf16[512,256]{1,0:T(8,128)(2,1)S(1)}, bf16[512,256]{1,0:T(8,128)(2,1)S(1)}, u32[]{:S(2)}, u32[]{:S(2)}) collective-permute-start(bf16[512,256]{1,0:T(8,128)(2,1)S(1)} %fusion.3), channel_id=1, source_target_pairs={{0,24},{4,28},{8,16},{12,20},{16,8},{20,12},{24,0},{28,4},{1,25},{... | collective-permute-start | bytes 786440 | tf_op jit(solution)/shard_map/ppermute | solution.py:425
  165.6 2.7 %collective-permute-start.55 = (f32[96,256]{1,0:T(8,128)S(1)}, f32[96,256]{1,0:T(8,128)S(1)}, u32[]{:S(2)}, u32[]{:S(2)}) collective-permute-start(f32[96,256]{1,0:T(8,128)S(1)} %add.324), channel_id=1, source_target_pairs={{0,16},{4,20},{8,24},{12,28},{16,0},{20,4},{24,8},{28,12},{1,17},{... | collective-permute-start | bytes 294920 | tf_op jit(solution)/shard_map/ppermute | solution.py:425
  168.3 3.7 %collective-permute-done.42.refs_2_ = bf16[512,256]{1,0:T(8,128)(2,1)S(1)} collective-permute-done((bf16[512,256]{1,0:T(8,128)(2,1)S(1)}, bf16[512,256]{1,0:T(8,128)(2,1)S(1)}, u32[]{:S(2)}, u32[]{:S(2)}) %collective-permute-start.42) | collective-permute-done | bytes 262176 | tf_op jit(solution)/shard_map/ppermute | solution.py:425
  171.9 12.9 %collective-permute-done.37.refs_1_ = bf16[512,256]{1,0:T(8,128)(2,1)S(1)} collective-permute-done((bf16[512,256]{1,0:T(8,128)(2,1)S(1)}, bf16[512,256]{1,0:T(8,128)(2,1)S(1)}, u32[]{:S(2)}, u32[]{:S(2)}) %collective-permute-start.37) | collective-permute-done | bytes 262176 | tf_op jit(solution)/shard_map/ppermute | solution.py:425
  185.7 2.9 %first_gradients.1 = (f32[72,256]{1,0:T(8,128)}, f32[72,256]{1,0:T(8,128)}, f32[72,256]{1,0:T(8,128)}, f32[72,256]{1,0:T(8,128)}) custom-call(bf16[512,256]{1,0:T(8,128)(2,1)} %copy-done.13, bf16[512,256]{1,0:T(8,128)(2,1)} %copy-done.12, bf16[512,256]{1,0:T(8,128)(2,1)} %copy-done.11, bf16[512,256]{1,0:T(8,128)(2,1)} %bitcast.95, ...), custom_call_target="tpu_custom_call" | custom-call | tf_op jit(solution)/shard_map/first_gradients/pallas_call | solution.py:414
  188.6 1.3 collective-permute-start.48
  190.9 1.3 collective-permute-start.57
  192.4 1.5 collective-permute-done.48
  196.1 1.4 collective-permute-done.57
  197.6 1.3 collective-permute-done.58
  200.8 4.0 %collective-permute-done.51 = f32[72,256]{1,0:T(8,128)S(1)} collective-permute-done((f32[72,256]{1,0:T(8,128)S(1)}, f32[72,256]{1,0:T(8,128)S(1)}, u32[]{:S(2)}, u32[]{:S(2)}) %collective-permute-start.51) | collective-permute-done | bytes 73760 | tf_op jit(solution)/shard_map/ppermute | solution.py:425
  204.9 1.6 collective-permute-start.52
  207.8 3.2 %collective-permute-done.52 = f32[72,256]{1,0:T(8,128)S(1)} collective-permute-done((f32[72,256]{1,0:T(8,128)S(1)}, f32[72,256]{1,0:T(8,128)S(1)}, u32[]{:S(2)}, u32[]{:S(2)}) %collective-permute-start.52) | collective-permute-done | bytes 73760 | tf_op jit(solution)/shard_map/ppermute | solution.py:425
  (196 shorter events, 35.1 us)
Async XLA Ops:
  2.3 9.9 %collective-permute-start.3 = (bf16[80,256]{1,0:T(8,128)(2,1)S(1)}, bf16[80,256]{1,0:T(8,128)(2,1)S(1)}, u32[]{:S(2)}, u32[]{:S(2)}) collective-permute-start(bf16[80,256]{1,0:T(8,128)(2,1)S(1)} %fusion.11.refs_4_), channel_id=1, source_target_pairs={{0,1},{1,0},{2,3},{3,2},{4,5},{5,4},{6,7},{7,6},{8,9},{9,8},{10,11... | collective-permute-start | bytes 122888 | tf_op jit(solution)/shard_map/ppermute | solution.py:425
  2.8 9.5 %collective-permute-start.4 = (bf16[80,256]{1,0:T(8,128)(2,1)S(1)}, bf16[80,256]{1,0:T(8,128)(2,1)S(1)}, u32[]{:S(2)}, u32[]{:S(2)}) collective-permute-start(bf16[80,256]{1,0:T(8,128)(2,1)S(1)} %fusion.11.refs_4_), channel_id=1, source_target_pairs={{0,2},{1,3},{2,0},{3,1},{4,6},{5,7},{6,4},{7,5},{8,10},{9,11},{10,... | collective-permute-start | bytes 122888 | tf_op jit(solution)/shard_map/ppermute | solution.py:425
  5.4 7.0 %collective-permute-start.5 = (bf16[80,256]{1,0:T(8,128)(2,1)S(1)}, bf16[80,256]{1,0:T(8,128)(2,1)S(1)}, u32[]{:S(2)}, u32[]{:S(2)}) collective-permute-start(bf16[80,256]{1,0:T(8,128)(2,1)S(1)} %fusion.11.refs_4_), channel_id=1, source_target_pairs={{0,3},{1,2},{2,1},{3,0},{4,7},{5,6},{6,5},{7,4},{8,11},{9,10},{10,... | collective-permute-start | bytes 122888 | tf_op jit(solution)/shard_map/ppermute | solution.py:425
  19.8 20.9 %collective-permute-start.7 = (bf16[528,256]{1,0:T(8,128)(2,1)}, bf16[528,256]{1,0:T(8,128)(2,1)S(1)}, u32[]{:S(2)}, u32[]{:S(2)}) collective-permute-start(bf16[528,256]{1,0:T(8,128)(2,1)} %get-tuple-element.50.hidden_ref), channel_id=1, source_target_pairs={{0,8},{4,12},{8,0},{12,4},{16,24},{20,28},{24,16},{28,20},{1,9},{5... | collective-permute-start | bytes 811016 | tf_op jit(solution)/shard_map/ppermute | solution.py:425
  21.4 20.7 %collective-permute-start.6 = (bf16[528,256]{1,0:T(8,128)(2,1)}, bf16[528,256]{1,0:T(8,128)(2,1)S(1)}, u32[]{:S(2)}, u32[]{:S(2)}) collective-permute-start(bf16[528,256]{1,0:T(8,128)(2,1)} %get-tuple-element.50.hidden_ref), channel_id=1, source_target_pairs={{0,4},{4,0},{8,12},{12,8},{16,20},{20,16},{24,28},{28,24},{1,5},{5... | collective-permute-start | bytes 811016 | tf_op jit(solution)/shard_map/ppermute | solution.py:425
  22.9 22.1 %collective-permute-start.9 = (bf16[528,256]{1,0:T(8,128)(2,1)}, bf16[528,256]{1,0:T(8,128)(2,1)S(1)}, u32[]{:S(2)}, u32[]{:S(2)}) collective-permute-start(bf16[528,256]{1,0:T(8,128)(2,1)} %get-tuple-element.50.hidden_ref), channel_id=1, source_target_pairs={{0,16},{4,20},{8,24},{12,28},{16,0},{20,4},{24,8},{28,12},{1,17},{... | collective-permute-start | bytes 811016 | tf_op jit(solution)/shard_map/ppermute | solution.py:425
  27.0 18.4 %collective-permute-start.11 = (bf16[528,256]{1,0:T(8,128)(2,1)}, bf16[528,256]{1,0:T(8,128)(2,1)S(1)}, u32[]{:S(2)}, u32[]{:S(2)}) collective-permute-start(bf16[528,256]{1,0:T(8,128)(2,1)} %get-tuple-element.50.hidden_ref), channel_id=1, source_target_pairs={{0,24},{4,28},{8,16},{12,20},{16,8},{20,12},{24,0},{28,4},{1,25},{... | collective-permute-start | bytes 811016 | tf_op jit(solution)/shard_map/ppermute | solution.py:425
  28.0 18.2 %collective-permute-start.13 = (bf16[528,256]{1,0:T(8,128)(2,1)}, bf16[528,256]{1,0:T(8,128)(2,1)S(1)}, u32[]{:S(2)}, u32[]{:S(2)}) collective-permute-start(bf16[528,256]{1,0:T(8,128)(2,1)} %get-tuple-element.50.hidden_ref), channel_id=1, source_target_pairs={{0,2},{1,3},{2,0},{3,1},{4,6},{5,7},{6,4},{7,5},{8,10},{9,11},{10,... | collective-permute-start | bytes 811016 | tf_op jit(solution)/shard_map/ppermute | solution.py:425
  40.7 14.4 %collective-permute-start.15 = (bf16[528,256]{1,0:T(8,128)(2,1)S(1)}, bf16[528,256]{1,0:T(8,128)(2,1)S(1)}, u32[]{:S(2)}, u32[]{:S(2)}) collective-permute-start(bf16[528,256]{1,0:T(8,128)(2,1)S(1)} %collective-permute-done.7), channel_id=1, source_target_pairs={{0,2},{1,3},{2,0},{3,1},{4,6},{5,7},{6,4},{7,5},{8,10},{9,11},{10,... | collective-permute-start | bytes 811016 | tf_op jit(solution)/shard_map/ppermute | solution.py:425
  42.1 14.0 %collective-permute-start.8 = (bf16[528,256]{1,0:T(8,128)(2,1)S(1)}, bf16[528,256]{1,0:T(8,128)(2,1)S(1)}, u32[]{:S(2)}, u32[]{:S(2)}) collective-permute-start(bf16[528,256]{1,0:T(8,128)(2,1)S(1)} %collective-permute-done.7), channel_id=1, source_target_pairs={{0,4},{4,0},{8,12},{12,8},{16,20},{20,16},{24,28},{28,24},{1,5},{5... | collective-permute-start | bytes 811016 | tf_op jit(solution)/shard_map/ppermute | solution.py:425
  45.0 9.0 %collective-permute-start.14 = (bf16[528,256]{1,0:T(8,128)(2,1)S(1)}, bf16[528,256]{1,0:T(8,128)(2,1)S(1)}, u32[]{:S(2)}, u32[]{:S(2)}) collective-permute-start(bf16[528,256]{1,0:T(8,128)(2,1)S(1)} %collective-permute-done.6), channel_id=1, source_target_pairs={{0,2},{1,3},{2,0},{3,1},{4,6},{5,7},{6,4},{7,5},{8,10},{9,11},{10,... | collective-permute-start | bytes 811016 | tf_op jit(solution)/shard_map/ppermute | solution.py:425
  45.5 11.8 %collective-permute-start.10 = (bf16[528,256]{1,0:T(8,128)(2,1)S(1)}, bf16[528,256]{1,0:T(8,128)(2,1)S(1)}, u32[]{:S(2)}, u32[]{:S(2)}) collective-permute-start(bf16[528,256]{1,0:T(8,128)(2,1)S(1)} %collective-permute-done.9), channel_id=1, source_target_pairs={{0,4},{4,0},{8,12},{12,8},{16,20},{20,16},{24,28},{28,24},{1,5},{5... | collective-permute-start | bytes 811016 | tf_op jit(solution)/shard_map/ppermute | solution.py:425
  46.1 23.7 %collective-permute-start.12 = (bf16[528,256]{1,0:T(8,128)(2,1)S(1)}, bf16[528,256]{1,0:T(8,128)(2,1)S(1)}, u32[]{:S(2)}, u32[]{:S(2)}) collective-permute-start(bf16[528,256]{1,0:T(8,128)(2,1)S(1)} %collective-permute-done.11), channel_id=1, source_target_pairs={{0,4},{4,0},{8,12},{12,8},{16,20},{20,16},{24,28},{28,24},{1,5},{5... | collective-permute-start | bytes 811016 | tf_op jit(solution)/shard_map/ppermute | solution.py:425
  54.0 15.2 %collective-permute-start.17 = (bf16[528,256]{1,0:T(8,128)(2,1)S(1)}, bf16[528,256]{1,0:T(8,128)(2,1)S(1)}, u32[]{:S(2)}, u32[]{:S(2)}) collective-permute-start(bf16[528,256]{1,0:T(8,128)(2,1)S(1)} %collective-permute-done.9), channel_id=1, source_target_pairs={{0,2},{1,3},{2,0},{3,1},{4,6},{5,7},{6,4},{7,5},{8,10},{9,11},{10,... | collective-permute-start | bytes 811016 | tf_op jit(solution)/shard_map/ppermute | solution.py:425
  55.1 14.1 %collective-permute-start.19 = (bf16[528,256]{1,0:T(8,128)(2,1)S(1)}, bf16[528,256]{1,0:T(8,128)(2,1)S(1)}, u32[]{:S(2)}, u32[]{:S(2)}) collective-permute-start(bf16[528,256]{1,0:T(8,128)(2,1)S(1)} %collective-permute-done.11), channel_id=1, source_target_pairs={{0,2},{1,3},{2,0},{3,1},{4,6},{5,7},{6,4},{7,5},{8,10},{9,11},{10,... | collective-permute-start | bytes 811016 | tf_op jit(solution)/shard_map/ppermute | solution.py:425
  56.1 13.8 %collective-permute-start.16 = (bf16[528,256]{1,0:T(8,128)(2,1)S(1)}, bf16[528,256]{1,0:T(8,128)(2,1)S(1)}, u32[]{:S(2)}, u32[]{:S(2)}) collective-permute-start(bf16[528,256]{1,0:T(8,128)(2,1)S(1)} %collective-permute-done.15), channel_id=1, source_target_pairs={{0,4},{4,0},{8,12},{12,8},{16,20},{20,16},{24,28},{28,24},{1,5},{5... | collective-permute-start | bytes 811016 | tf_op jit(solution)/shard_map/ppermute | solution.py:425
  57.3 14.9 %collective-permute-start.18 = (bf16[528,256]{1,0:T(8,128)(2,1)S(1)}, bf16[528,256]{1,0:T(8,128)(2,1)S(1)}, u32[]{:S(2)}, u32[]{:S(2)}) collective-permute-start(bf16[528,256]{1,0:T(8,128)(2,1)S(1)} %collective-permute-done.10), channel_id=1, source_target_pairs={{0,2},{1,3},{2,0},{3,1},{4,6},{5,7},{6,4},{7,5},{8,10},{9,11},{10,... | collective-permute-start | bytes 811016 | tf_op jit(solution)/shard_map/ppermute | solution.py:425
  69.2 11.5 %collective-permute-start.21 = (bf16[2048,256]{1,0:T(8,128)(2,1)S(1)}, bf16[2048,256]{1,0:T(8,128)(2,1)}, u32[]{:S(2)}, u32[]{:S(2)}) collective-permute-start(bf16[2048,256]{1,0:T(8,128)(2,1)S(1)} %pad_maximum_fusion), channel_id=1, source_target_pairs={{0,1},{1,0},{2,3},{3,2},{4,5},{5,4},{6,7},{7,6},{8,9},{9,8},{10,11... | collective-permute-start | bytes 3145736 | tf_op jit(solution)/shard_map/ppermute | solution.py:425
  69.3 9.0 %collective-permute-start.20 = (bf16[528,256]{1,0:T(8,128)(2,1)S(1)}, bf16[528,256]{1,0:T(8,128)(2,1)S(1)}, u32[]{:S(2)}, u32[]{:S(2)}) collective-permute-start(bf16[528,256]{1,0:T(8,128)(2,1)S(1)} %collective-permute-done.19), channel_id=1, source_target_pairs={{0,4},{4,0},{8,12},{12,8},{16,20},{20,16},{24,28},{28,24},{1,5},{5... | collective-permute-start | bytes 811016 | tf_op jit(solution)/shard_map/ppermute | solution.py:425
  70.0 10.7 %collective-permute-start.22 = (bf16[2048,256]{1,0:T(8,128)(2,1)S(1)}, bf16[2048,256]{1,0:T(8,128)(2,1)}, u32[]{:S(2)}, u32[]{:S(2)}) collective-permute-start(bf16[2048,256]{1,0:T(8,128)(2,1)S(1)} %pad_maximum_fusion.1), channel_id=1, source_target_pairs={{0,1},{1,0},{2,3},{3,2},{4,5},{5,4},{6,7},{7,6},{8,9},{9,8},{10,11... | collective-permute-start | bytes 3145736 | tf_op jit(solution)/shard_map/ppermute | solution.py:425
  72.3 8.4 %collective-permute-start.23 = (bf16[2048,256]{1,0:T(8,128)(2,1)S(1)}, bf16[2048,256]{1,0:T(8,128)(2,1)}, u32[]{:S(2)}, u32[]{:S(2)}) collective-permute-start(bf16[2048,256]{1,0:T(8,128)(2,1)S(1)} %pad_maximum_fusion.2), channel_id=1, source_target_pairs={{0,1},{1,0},{2,3},{3,2},{4,5},{5,4},{6,7},{7,6},{8,9},{9,8},{10,11... | collective-permute-start | bytes 3145736 | tf_op jit(solution)/shard_map/ppermute | solution.py:425
  99.4 17.6 %collective-permute-start.25 = (f32[96,256]{1,0:T(8,128)}, f32[96,256]{1,0:T(8,128)S(1)}, u32[]{:S(2)}, u32[]{:S(2)}) collective-permute-start(f32[96,256]{1,0:T(8,128)} %get-tuple-element.63), channel_id=1, source_target_pairs={{0,1},{1,0},{2,3},{3,2},{4,5},{5,4},{6,7},{7,6},{8,9},{9,8},{10,11... | collective-permute-start | bytes 294920 | tf_op jit(solution)/shard_map/ppermute | solution.py:425
  99.6 17.4 %collective-permute-start.26 = (f32[96,256]{1,0:T(8,128)}, f32[96,256]{1,0:T(8,128)S(1)}, u32[]{:S(2)}, u32[]{:S(2)}) collective-permute-start(f32[96,256]{1,0:T(8,128)} %get-tuple-element.64), channel_id=1, source_target_pairs={{0,2},{1,3},{2,0},{3,1},{4,6},{5,7},{6,4},{7,5},{8,10},{9,11},{10,... | collective-permute-start | bytes 294920 | tf_op jit(solution)/shard_map/ppermute | solution.py:425
  100.5 16.5 %collective-permute-start.27 = (f32[96,256]{1,0:T(8,128)}, f32[96,256]{1,0:T(8,128)S(1)}, u32[]{:S(2)}, u32[]{:S(2)}) collective-permute-start(f32[96,256]{1,0:T(8,128)} %get-tuple-element.65), channel_id=1, source_target_pairs={{0,3},{1,2},{2,1},{3,0},{4,7},{5,6},{6,5},{7,4},{8,11},{9,10},{10,... | collective-permute-start | bytes 294920 | tf_op jit(solution)/shard_map/ppermute | solution.py:425
  117.0 7.0 %collective-permute-start.43 = (bf16[16,128,256]{2,1,0:T(8,128)(2,1)}, bf16[16,128,256]{2,1,0:T(8,128)(2,1)S(1)}, u32[]{:S(2)}, u32[]{:S(2)}) collective-permute-start(bf16[16,128,256]{2,1,0:T(8,128)(2,1)} %get-tuple-element.73), channel_id=1, source_target_pairs={{0,1},{1,0},{2,3},{3,2},{4,5},{5,4},{6,7},{7,6},{8,9},{9,8},{10,11... | collective-permute-start | bytes 3145736 | tf_op jit(solution)/shard_map/ppermute | solution.py:425
  117.5 9.5 %collective-permute-start.38 = (bf16[16,128,256]{2,1,0:T(8,128)(2,1)}, bf16[16,128,256]{2,1,0:T(8,128)(2,1)S(1)}, u32[]{:S(2)}, u32[]{:S(2)}) collective-permute-start(bf16[16,128,256]{2,1,0:T(8,128)(2,1)} %get-tuple-element.71), channel_id=1, source_target_pairs={{0,1},{1,0},{2,3},{3,2},{4,5},{5,4},{6,7},{7,6},{8,9},{9,8},{10,11... | collective-permute-start | bytes 3145736 | tf_op jit(solution)/shard_map/ppermute | solution.py:425
  117.6 10.3 %collective-permute-start.33 = (bf16[16,128,256]{2,1,0:T(8,128)(2,1)}, bf16[16,128,256]{2,1,0:T(8,128)(2,1)S(1)}, u32[]{:S(2)}, u32[]{:S(2)}) collective-permute-start(bf16[16,128,256]{2,1,0:T(8,128)(2,1)} %get-tuple-element.69), channel_id=1, source_target_pairs={{0,1},{1,0},{2,3},{3,2},{4,5},{5,4},{6,7},{7,6},{8,9},{9,8},{10,11... | collective-permute-start | bytes 3145736 | tf_op jit(solution)/shard_map/ppermute | solution.py:425
  118.0 11.7 %collective-permute-start.28 = (bf16[16,128,256]{2,1,0:T(8,128)(2,1)}, bf16[16,128,256]{2,1,0:T(8,128)(2,1)S(1)}, u32[]{:S(2)}, u32[]{:S(2)}) collective-permute-start(bf16[16,128,256]{2,1,0:T(8,128)(2,1)} %get-tuple-element.67), channel_id=1, source_target_pairs={{0,1},{1,0},{2,3},{3,2},{4,5},{5,4},{6,7},{7,6},{8,9},{9,8},{10,11... | collective-permute-start | bytes 3145736 | tf_op jit(solution)/shard_map/ppermute | solution.py:425
  123.4 41.0 %collective-permute-start.54 = (f32[96,256]{1,0:T(8,128)S(1)}, f32[96,256]{1,0:T(8,128)S(1)}, u32[]{:S(2)}, u32[]{:S(2)}) collective-permute-start(f32[96,256]{1,0:T(8,128)S(1)} %add.323), channel_id=1, source_target_pairs={{0,8},{4,12},{8,0},{12,4},{16,24},{20,28},{24,16},{28,20},{1,9},{5... | collective-permute-start | bytes 294920 | tf_op jit(solution)/shard_map/ppermute | solution.py:425
  126.2 9.2 %collective-permute-start.44 = (bf16[512,256]{1,0:T(8,128)(2,1)S(1)}, bf16[512,256]{1,0:T(8,128)(2,1)S(1)}, u32[]{:S(2)}, u32[]{:S(2)}) collective-permute-start(bf16[512,256]{1,0:T(8,128)(2,1)S(1)} %bitcast.101), channel_id=1, source_target_pairs={{0,2},{1,3},{2,0},{3,1},{4,6},{5,7},{6,4},{7,5},{8,10},{9,11},{10,... | collective-permute-start | bytes 786440 | tf_op jit(solution)/shard_map/ppermute | solution.py:425
  127.3 9.3 %collective-permute-start.40 = (bf16[512,256]{1,0:T(8,128)(2,1)S(1)}, bf16[512,256]{1,0:T(8,128)(2,1)S(1)}, u32[]{:S(2)}, u32[]{:S(2)}) collective-permute-start(bf16[512,256]{1,0:T(8,128)(2,1)S(1)} %bitcast.102), channel_id=1, source_target_pairs={{0,4},{4,0},{8,12},{12,8},{16,20},{20,16},{24,28},{28,24},{1,5},{5... | collective-permute-start | bytes 786440 | tf_op jit(solution)/shard_map/ppermute | solution.py:425
  127.9 18.6 %collective-permute-start.39 = (bf16[512,256]{1,0:T(8,128)(2,1)S(1)}, bf16[512,256]{1,0:T(8,128)(2,1)S(1)}, u32[]{:S(2)}, u32[]{:S(2)}) collective-permute-start(bf16[512,256]{1,0:T(8,128)(2,1)S(1)} %bitcast.100), channel_id=1, source_target_pairs={{0,4},{4,0},{8,12},{12,8},{16,20},{20,16},{24,28},{28,24},{1,5},{5... | collective-permute-start | bytes 786440 | tf_op jit(solution)/shard_map/ppermute | solution.py:425
  129.8 11.3 %collective-permute-start.34 = (bf16[512,256]{1,0:T(8,128)(2,1)S(1)}, bf16[512,256]{1,0:T(8,128)(2,1)S(1)}, u32[]{:S(2)}, u32[]{:S(2)}) collective-permute-start(bf16[512,256]{1,0:T(8,128)(2,1)S(1)} %bitcast.103), channel_id=1, source_target_pairs={{0,2},{1,3},{2,0},{3,1},{4,6},{5,7},{6,4},{7,5},{8,10},{9,11},{10,... | collective-permute-start | bytes 786440 | tf_op jit(solution)/shard_map/ppermute | solution.py:425
  135.5 16.1 %collective-permute-start.36 = (bf16[512,256]{1,0:T(8,128)(2,1)S(1)}, bf16[512,256]{1,0:T(8,128)(2,1)S(1)}, u32[]{:S(2)}, u32[]{:S(2)}) collective-permute-start(bf16[512,256]{1,0:T(8,128)(2,1)S(1)} %bitcast.99), channel_id=1, source_target_pairs={{0,2},{1,3},{2,0},{3,1},{4,6},{5,7},{6,4},{7,5},{8,10},{9,11},{10,... | collective-permute-start | bytes 786440 | tf_op jit(solution)/shard_map/ppermute | solution.py:425
  136.7 9.3 %collective-permute-start.30 = (bf16[512,256]{1,0:T(8,128)(2,1)S(1)}, bf16[512,256]{1,0:T(8,128)(2,1)S(1)}, u32[]{:S(2)}, u32[]{:S(2)}) collective-permute-start(bf16[512,256]{1,0:T(8,128)(2,1)S(1)} %bitcast.104), channel_id=1, source_target_pairs={{0,4},{4,0},{8,12},{12,8},{16,20},{20,16},{24,28},{28,24},{1,5},{5... | collective-permute-start | bytes 786440 | tf_op jit(solution)/shard_map/ppermute | solution.py:425
  141.1 9.6 %collective-permute-start.41 = (bf16[512,256]{1,0:T(8,128)(2,1)S(1)}, bf16[512,256]{1,0:T(8,128)(2,1)S(1)}, u32[]{:S(2)}, u32[]{:S(2)}) collective-permute-start(bf16[512,256]{1,0:T(8,128)(2,1)S(1)} %fusion.1), channel_id=1, source_target_pairs={{0,2},{1,3},{2,0},{3,1},{4,6},{5,7},{6,4},{7,5},{8,10},{9,11},{10,... | collective-permute-start | bytes 786440 | tf_op jit(solution)/shard_map/ppermute | solution.py:425
  146.0 9.2 %collective-permute-start.35 = (bf16[512,256]{1,0:T(8,128)(2,1)S(1)}, bf16[512,256]{1,0:T(8,128)(2,1)S(1)}, u32[]{:S(2)}, u32[]{:S(2)}) collective-permute-start(bf16[512,256]{1,0:T(8,128)(2,1)S(1)} %fusion.4), channel_id=1, source_target_pairs={{0,4},{4,0},{8,12},{12,8},{16,20},{20,16},{24,28},{28,24},{1,5},{5... | collective-permute-start | bytes 786440 | tf_op jit(solution)/shard_map/ppermute | solution.py:425
  146.6 14.2 %collective-permute-start.29 = (bf16[512,256]{1,0:T(8,128)(2,1)S(1)}, bf16[512,256]{1,0:T(8,128)(2,1)S(1)}, u32[]{:S(2)}, u32[]{:S(2)}) collective-permute-start(bf16[512,256]{1,0:T(8,128)(2,1)S(1)} %bitcast.98), channel_id=1, source_target_pairs={{0,4},{4,0},{8,12},{12,8},{16,20},{20,16},{24,28},{28,24},{1,5},{5... | collective-permute-start | bytes 786440 | tf_op jit(solution)/shard_map/ppermute | solution.py:425
  150.7 13.4 %collective-permute-start.31 = (bf16[512,256]{1,0:T(8,128)(2,1)S(1)}, bf16[512,256]{1,0:T(8,128)(2,1)S(1)}, u32[]{:S(2)}, u32[]{:S(2)}) collective-permute-start(bf16[512,256]{1,0:T(8,128)(2,1)S(1)} %fusion.7), channel_id=1, source_target_pairs={{0,2},{1,3},{2,0},{3,1},{4,6},{5,7},{6,4},{7,5},{8,10},{9,11},{10,... | collective-permute-start | bytes 786440 | tf_op jit(solution)/shard_map/ppermute | solution.py:425
  151.6 14.0 %collective-permute-start.46 = (bf16[512,256]{1,0:T(8,128)(2,1)S(1)}, bf16[512,256]{1,0:T(8,128)(2,1)S(1)}, u32[]{:S(2)}, u32[]{:S(2)}) collective-permute-start(bf16[512,256]{1,0:T(8,128)(2,1)S(1)} %bitcast.97), channel_id=1, source_target_pairs={{0,2},{1,3},{2,0},{3,1},{4,6},{5,7},{6,4},{7,5},{8,10},{9,11},{10,... | collective-permute-start | bytes 786440 | tf_op jit(solution)/shard_map/ppermute | solution.py:425
  155.2 13.1 %collective-permute-start.45 = (bf16[512,256]{1,0:T(8,128)(2,1)S(1)}, bf16[512,256]{1,0:T(8,128)(2,1)S(1)}, u32[]{:S(2)}, u32[]{:S(2)}) collective-permute-start(bf16[512,256]{1,0:T(8,128)(2,1)S(1)} %fusion), channel_id=1, source_target_pairs={{0,4},{4,0},{8,12},{12,8},{16,20},{20,16},{24,28},{28,24},{1,5},{5... | collective-permute-start | bytes 786440 | tf_op jit(solution)/shard_map/ppermute | solution.py:425
  160.8 11.1 %collective-permute-start.42 = (bf16[512,256]{1,0:T(8,128)(2,1)S(1)}, bf16[512,256]{1,0:T(8,128)(2,1)S(1)}, u32[]{:S(2)}, u32[]{:S(2)}) collective-permute-start(bf16[512,256]{1,0:T(8,128)(2,1)S(1)} %fusion.3), channel_id=1, source_target_pairs={{0,24},{4,28},{8,16},{12,20},{16,8},{20,12},{24,0},{28,4},{1,25},{... | collective-permute-start | bytes 786440 | tf_op jit(solution)/shard_map/ppermute | solution.py:425
  164.1 20.8 %collective-permute-start.37 = (bf16[512,256]{1,0:T(8,128)(2,1)S(1)}, bf16[512,256]{1,0:T(8,128)(2,1)S(1)}, u32[]{:S(2)}, u32[]{:S(2)}) collective-permute-start(bf16[512,256]{1,0:T(8,128)(2,1)S(1)} %fusion.6), channel_id=1, source_target_pairs={{0,16},{4,20},{8,24},{12,28},{16,0},{20,4},{24,8},{28,12},{1,17},{... | collective-permute-start | bytes 786440 | tf_op jit(solution)/shard_map/ppermute | solution.py:425
  164.4 20.4 %collective-permute-start.32 = (bf16[512,256]{1,0:T(8,128)(2,1)S(1)}, bf16[512,256]{1,0:T(8,128)(2,1)S(1)}, u32[]{:S(2)}, u32[]{:S(2)}) collective-permute-start(bf16[512,256]{1,0:T(8,128)(2,1)S(1)} %fusion.9), channel_id=1, source_target_pairs={{0,8},{4,12},{8,0},{12,4},{16,24},{20,28},{24,16},{28,20},{1,9},{5... | collective-permute-start | bytes 786440 | tf_op jit(solution)/shard_map/ppermute | solution.py:425
  165.6 24.9 %collective-permute-start.55 = (f32[96,256]{1,0:T(8,128)S(1)}, f32[96,256]{1,0:T(8,128)S(1)}, u32[]{:S(2)}, u32[]{:S(2)}) collective-permute-start(f32[96,256]{1,0:T(8,128)S(1)} %add.324), channel_id=1, source_target_pairs={{0,16},{4,20},{8,24},{12,28},{16,0},{20,4},{24,8},{28,12},{1,17},{... | collective-permute-start | bytes 294920 | tf_op jit(solution)/shard_map/ppermute | solution.py:425
  190.9 6.7 %collective-permute-start.57 = (f32[96,256]{1,0:T(8,128)S(1)}, f32[96,256]{1,0:T(8,128)S(1)}, u32[]{:S(2)}, u32[]{:S(2)}) collective-permute-start(f32[96,256]{1,0:T(8,128)S(1)} %add.325), channel_id=1, source_target_pairs={{0,2},{1,3},{2,0},{3,1},{4,6},{5,7},{6,4},{7,5},{8,10},{9,11},{10,... | collective-permute-start | bytes 294920 | tf_op jit(solution)/shard_map/ppermute | solution.py:425
  192.2 6.7 %collective-permute-start.58 = (f32[96,256]{1,0:T(8,128)S(1)}, f32[96,256]{1,0:T(8,128)S(1)}, u32[]{:S(2)}, u32[]{:S(2)}) collective-permute-start(f32[96,256]{1,0:T(8,128)S(1)} %add.325), channel_id=1, source_target_pairs={{0,3},{1,2},{2,1},{3,0},{4,7},{5,6},{6,5},{7,4},{8,11},{9,10},{10,... | collective-permute-start | bytes 294920 | tf_op jit(solution)/shard_map/ppermute | solution.py:425
  204.9 6.1 %collective-permute-start.52 = (f32[72,256]{1,0:T(8,128)S(1)}, f32[72,256]{1,0:T(8,128)S(1)}, u32[]{:S(2)}, u32[]{:S(2)}) collective-permute-start(f32[72,256]{1,0:T(8,128)S(1)} %add.317), channel_id=1, source_target_pairs={{0,16},{4,20},{8,24},{12,28},{16,0},{20,4},{24,8},{28,12},{1,17},{... | collective-permute-start | bytes 221192 | tf_op jit(solution)/shard_map/ppermute | solution.py:425
  (32 other events, 244.9 us)
